TPU v7x, 32 devices: a whole 2x2x4 slice. The times are simulated.
32 devices in a mesh: dp: 8 (over z, y), seq: 4 (over x, core).
Axes of the slice: x: 2, y: 2, z: 4, core: 2. Of those that a mesh axis runs over, the one named last changes fastest.
Arguments:
- tokens: bfloat16 [6144, 1024], P(('dp', 'seq')), may hold values from -6 to 6
- doc_start: int32 [8, 768], P('dp'), may hold values from 0 to 767, as said below
- lexical_ids: int32 [6144], P(('dp', 'seq')), may hold values from 0 to 250001, as said below
- queries: bfloat16 [8, 32, 1024], P('dp'), may hold values from -0.5 to 0.5
- match_index: int32 [8, 32], P('dp'), may hold values from 0 to 767
- query_weight: bfloat16 [2, 1024, 1024], P(None, ('dp', 'seq')), may hold values from -0.25 to 0.25
- query_bias: bfloat16 [2, 1024], P(None, ('dp', 'seq')), may hold values from -3 to 3
- key_weight: bfloat16 [2, 1024, 1024], P(None, ('dp', 'seq')), may hold values from -0.25 to 0.25
- value_weight: bfloat16 [2, 1024, 1024], P(None, ('dp', 'seq')), may hold values from -0.1875 to 0.1875
- value_bias: bfloat16 [2, 1024], P(None, ('dp', 'seq')), may hold values from -3 to 3
- out_weight: bfloat16 [2, 1024, 1024], P(None, ('dp', 'seq')), may hold values from -0.75 to 0.75
- out_bias: bfloat16 [2, 1024], P(None, ('dp', 'seq')), may hold values from -3 to 3
- norm_gain: bfloat16 [2, 1024], P(None, ('dp', 'seq')), may hold values from 0.25 to 1.75
- norm_bias: bfloat16 [2, 1024], P(None, ('dp', 'seq')), may hold values from -3 to 3
- expand_weight: bfloat16 [2, 1024, 4096], P(None, ('dp', 'seq')), may hold values from -0.1875 to 0.1875
- expand_bias: bfloat16 [2, 4096], P(None, ('dp', 'seq')), may hold values from -3 to 3
- shrink_weight: bfloat16 [2, 4096, 1024], P(None, ('dp', 'seq')), may hold values from -0.09375 to 0.09375
- shrink_bias: bfloat16 [2, 1024], P(None, ('dp', 'seq')), may hold values from -3 to 3
- final_gain: bfloat16 [2, 1024], P(None, ('dp', 'seq')), may hold values from 0.25 to 1.75
- final_bias: bfloat16 [2, 1024], P(None, ('dp', 'seq')), may hold values from -3 to 3
- lexical_weight: bfloat16 [1024], replicated, may hold values from -0.1875 to 0.1875
- lexical_bias: bfloat16 [1], replicated, may hold values from -3 to 3
- score_cot: float32 [8, 32], P('dp'), may hold values from -96 to 96
- encoded_cot: bfloat16 [6144, 1024], P(('dp', 'seq')), may hold values from -6 to 6
Outputs:
- encoded: bfloat16 [6144, 1024], P(('dp', 'seq'))
- scores: float32 [8, 32], P('dp')
- lexical_stats: float32 [2], replicated
- tokens_grad: bfloat16 [6144, 1024], P(('dp', 'seq'))
- query_weight_grad: float32 [2, 1024, 1024], P(None, ('dp', 'seq'))
- query_bias_grad: float32 [2, 1024], P(None, ('dp', 'seq'))
- key_weight_grad: float32 [2, 1024, 1024], P(None, ('dp', 'seq'))
- value_weight_grad: float32 [2, 1024, 1024], P(None, ('dp', 'seq'))
- value_bias_grad: float32 [2, 1024], P(None, ('dp', 'seq'))
- out_weight_grad: float32 [2, 1024, 1024], P(None, ('dp', 'seq'))
- out_bias_grad: float32 [2, 1024], P(None, ('dp', 'seq'))
- norm_gain_grad: float32 [2, 1024], P(None, ('dp', 'seq'))
- norm_bias_grad: float32 [2, 1024], P(None, ('dp', 'seq'))
- expand_weight_grad: float32 [2, 1024, 4096], P(None, ('dp', 'seq'))
- expand_bias_grad: float32 [2, 4096], P(None, ('dp', 'seq'))
- shrink_weight_grad: float32 [2, 4096, 1024], P(None, ('dp', 'seq'))
- shrink_bias_grad: float32 [2, 1024], P(None, ('dp', 'seq'))
- final_gain_grad: float32 [2, 1024], P(None, ('dp', 'seq'))
- final_bias_grad: float32 [2, 1024], P(None, ('dp', 'seq'))
Inputs may be any that keep to these rules, and one draw needn't show every extreme that they name: `doc_start`: documents are contiguous runs of a group; in every group one document begins before position 48 and ends within the last 49 positions, and the group's last position is a document of one token. `lexical_ids`: ids of a vocabulary of 250002; ids 0 to 3 are special tokens.
All inputs are finite; a program needn't handle non-finite values.
Results may differ from a plain program's by a relative error of at most 0.035.
The roundings to bfloat16 on the way count: a program that leaves them out, or rounds other values in their place, can miss the bound.
Values may be sent and summed in bfloat16 or wider, within the bound.
No kernel may reach another device: no remote copies, remote signals or barrier semaphores. Data moves between devices by JAX's collectives and lax.ppermute only.
A program may use at most 256 MiB of HBM per device.

v0:
```python
import math

import jax
import jax.numpy as jnp
from jax import lax
from jax.sharding import PartitionSpec as P

HEAD = 64


EPSILON = 1e-05
NEGATIVE = -1e30
HIGHEST = lax.Precision.HIGHEST


def layer_norm(resid, gain_vec, bias_vec):
    center = resid - jnp.mean(resid, axis=-1, keepdims=True)
    spread = jnp.mean(center * center, axis=-1, keepdims=True)
    return center * lax.rsqrt(spread + EPSILON) * gain_vec + bias_vec


def gelu_exact(values):
    return jax.nn.gelu(values, approximate=False)


def matmul_f32(left, right):
    return jnp.dot(left, right, preferred_element_type=jnp.float32)


def column_sums(matrix):
    return jnp.sum(matrix.astype(jnp.float32), axis=0)


def head_blocks(matrix):
    row_count = matrix.shape[0]
    pairs = matrix.shape[1] // (2 * HEAD)
    return matrix.reshape(row_count, pairs, 2, HEAD).transpose(1, 2, 0, 3)


def join_heads(blocks):
    return blocks.transpose(2, 0, 1, 3).reshape(blocks.shape[2], -1)


def pair_scores(query_couple, key_couple, same_doc):
    score_scale = 1.0 / math.sqrt(HEAD)
    head_scores = (
        jnp.einsum("yfk,yzk->yfz", query_couple, key_couple, preferred_element_type=jnp.float32)
        * score_scale
    )
    return jnp.where(same_doc[None], head_scores, NEGATIVE)


def attend(query_rows, key_all, value_all, same_doc):

    def one_pair(pieces):
        query_couple, key_couple, value_couple = pieces
        head_scores = pair_scores(query_couple, key_couple, same_doc)
        row_max = jnp.max(head_scores, axis=-1, keepdims=True)
        raised = jnp.exp(head_scores - row_max)
        row_sum = jnp.sum(raised, axis=-1, keepdims=True)
        weight_tensors = (raised / row_sum).astype(jnp.bfloat16)
        output_tensor = jnp.einsum(
            "rez,rzf->ref", weight_tensors, value_couple, preferred_element_type=jnp.float32
        )
        return (output_tensor, row_max, row_sum)

    output_tensor, row_max, row_sum = lax.map(
        one_pair, (head_blocks(query_rows), head_blocks(key_all), head_blocks(value_all))
    )
    return (join_heads(output_tensor), row_max, row_sum)


def attend_back(query_rows, key_all, value_all, same_doc, row_max, row_sum, low_attn):
    score_scale = 1.0 / math.sqrt(HEAD)

    def one_pair(pieces):
        query_couple, key_couple, value_couple, pair_max, pair_sum, gradient_couple = pieces
        head_scores = pair_scores(query_couple, key_couple, same_doc)
        probs = jnp.exp(head_scores - pair_max) / pair_sum
        grad_probs = jnp.einsum(
            "yfk,yzk->yfz", gradient_couple, value_couple, preferred_element_type=jnp.float32
        )
        grad_value = jnp.einsum(
            "jqb,jql->jbl",
            probs.astype(jnp.bfloat16),
            gradient_couple,
            preferred_element_type=jnp.float32,
        )
        grad_scores = probs * (grad_probs - jnp.sum(probs * grad_probs, axis=-1, keepdims=True))
        reduced_scores = grad_scores.astype(jnp.bfloat16)
        grad_query = (
            jnp.einsum(
                "rez,rzf->ref", reduced_scores, key_couple, preferred_element_type=jnp.float32
            )
            * score_scale
        )
        grad_key = (
            jnp.einsum(
                "jqb,jql->jbl", reduced_scores, query_couple, preferred_element_type=jnp.float32
            )
            * score_scale
        )
        return (grad_query, grad_key, grad_value)

    grad_query, grad_key, grad_value = lax.map(
        one_pair,
        (
            head_blocks(query_rows),
            head_blocks(key_all),
            head_blocks(value_all),
            row_max,
            row_sum,
            head_blocks(low_attn),
        ),
    )
    return (join_heads(grad_query), join_heads(grad_key), join_heads(grad_value))


def fetch_layer(layer_index, shards):
    (
        query_weight,
        query_bias,
        key_weight,
        value_weight,
        value_bias,
        out_weight,
        out_bias,
        norm_gain,
        norm_bias,
        expand_weight,
        expand_bias,
        shrink_weight,
        shrink_bias,
        final_gain,
        final_bias,
    ) = shards
    return (
        lax.all_gather(query_weight[layer_index], ("dp", "seq"), axis=0, tiled=True),
        lax.all_gather(query_bias[layer_index], ("dp", "seq"), axis=0, tiled=True),
        lax.all_gather(key_weight[layer_index], ("dp", "seq"), axis=0, tiled=True),
        lax.all_gather(value_weight[layer_index], ("dp", "seq"), axis=0, tiled=True),
        lax.all_gather(value_bias[layer_index], ("dp", "seq"), axis=0, tiled=True),
        lax.all_gather(out_weight[layer_index], ("dp", "seq"), axis=0, tiled=True),
        lax.all_gather(out_bias[layer_index], ("dp", "seq"), axis=0, tiled=True),
        lax.all_gather(norm_gain[layer_index], ("dp", "seq"), axis=0, tiled=True),
        lax.all_gather(norm_bias[layer_index], ("dp", "seq"), axis=0, tiled=True),
        lax.all_gather(expand_weight[layer_index], ("dp", "seq"), axis=0, tiled=True),
        lax.all_gather(expand_bias[layer_index], ("dp", "seq"), axis=0, tiled=True),
        lax.all_gather(shrink_weight[layer_index], ("dp", "seq"), axis=0, tiled=True),
        lax.all_gather(shrink_bias[layer_index], ("dp", "seq"), axis=0, tiled=True),
        lax.all_gather(final_gain[layer_index], ("dp", "seq"), axis=0, tiled=True),
        lax.all_gather(final_bias[layer_index], ("dp", "seq"), axis=0, tiled=True),
    )


def fetch_again(layer_index, shards):
    (
        query_weight,
        query_bias,
        key_weight,
        value_weight,
        value_bias,
        out_weight,
        out_bias,
        norm_gain,
        norm_bias,
        expand_weight,
        expand_bias,
        shrink_weight,
        shrink_bias,
        final_gain,
        final_bias,
    ) = shards
    return (
        lax.all_gather(query_weight[layer_index], ("dp", "seq"), axis=0, tiled=True),
        lax.all_gather(query_bias[layer_index], ("dp", "seq"), axis=0, tiled=True),
        lax.all_gather(key_weight[layer_index], ("dp", "seq"), axis=0, tiled=True),
        lax.all_gather(value_weight[layer_index], ("dp", "seq"), axis=0, tiled=True),
        lax.all_gather(value_bias[layer_index], ("dp", "seq"), axis=0, tiled=True),
        lax.all_gather(out_weight[layer_index], ("dp", "seq"), axis=0, tiled=True),
        lax.all_gather(out_bias[layer_index], ("dp", "seq"), axis=0, tiled=True),
        lax.all_gather(norm_gain[layer_index], ("dp", "seq"), axis=0, tiled=True),
        lax.all_gather(norm_bias[layer_index], ("dp", "seq"), axis=0, tiled=True),
        lax.all_gather(expand_weight[layer_index], ("dp", "seq"), axis=0, tiled=True),
        lax.all_gather(expand_bias[layer_index], ("dp", "seq"), axis=0, tiled=True),
        lax.all_gather(shrink_weight[layer_index], ("dp", "seq"), axis=0, tiled=True),
        lax.all_gather(shrink_bias[layer_index], ("dp", "seq"), axis=0, tiled=True),
        lax.all_gather(final_gain[layer_index], ("dp", "seq"), axis=0, tiled=True),
        lax.all_gather(final_bias[layer_index], ("dp", "seq"), axis=0, tiled=True),
    )


def reduce_layer(
    grad_query,
    grad_qbias,
    grad_key,
    grad_value,
    grad_vbias,
    grad_output,
    grad_obias,
    grad_ngain,
    grad_nbias,
    grad_expand,
    grad_ebias,
    grad_shrink,
    grad_sbias,
    grad_fgain,
    grad_fbias,
):
    return (
        lax.psum_scatter(grad_query, ("dp", "seq"), scatter_dimension=0, tiled=True),
        lax.psum_scatter(grad_qbias, ("dp", "seq"), scatter_dimension=0, tiled=True),
        lax.psum_scatter(grad_key, ("dp", "seq"), scatter_dimension=0, tiled=True),
        lax.psum_scatter(grad_value, ("dp", "seq"), scatter_dimension=0, tiled=True),
        lax.psum_scatter(grad_vbias, ("dp", "seq"), scatter_dimension=0, tiled=True),
        lax.psum_scatter(grad_output, ("dp", "seq"), scatter_dimension=0, tiled=True),
        lax.psum_scatter(grad_obias, ("dp", "seq"), scatter_dimension=0, tiled=True),
        lax.psum_scatter(grad_ngain, ("dp", "seq"), scatter_dimension=0, tiled=True),
        lax.psum_scatter(grad_nbias, ("dp", "seq"), scatter_dimension=0, tiled=True),
        lax.psum_scatter(grad_expand, ("dp", "seq"), scatter_dimension=0, tiled=True),
        lax.psum_scatter(grad_ebias, ("dp", "seq"), scatter_dimension=0, tiled=True),
        lax.psum_scatter(grad_shrink, ("dp", "seq"), scatter_dimension=0, tiled=True),
        lax.psum_scatter(grad_sbias, ("dp", "seq"), scatter_dimension=0, tiled=True),
        lax.psum_scatter(grad_fgain, ("dp", "seq"), scatter_dimension=0, tiled=True),
        lax.psum_scatter(grad_fbias, ("dp", "seq"), scatter_dimension=0, tiled=True),
    )


def forward_layer(hidden, params, same_doc):
    (
        query_weight,
        query_bias,
        key_weight,
        value_weight,
        value_bias,
        out_weight,
        out_bias,
        norm_gain,
        norm_bias,
        expand_weight,
        expand_bias,
        shrink_weight,
        shrink_bias,
        final_gain,
        final_bias,
    ) = params
    low_in = hidden.astype(jnp.bfloat16)
    query_rows = (matmul_f32(low_in, query_weight) + query_bias.astype(jnp.float32)).astype(
        jnp.bfloat16
    )
    key_rows = matmul_f32(low_in, key_weight).astype(jnp.bfloat16)
    value_rows = (matmul_f32(low_in, value_weight) + value_bias.astype(jnp.float32)).astype(
        jnp.bfloat16
    )
    key_all, value_all = (
        lax.all_gather(key_rows, "seq", axis=0, tiled=True),
        lax.all_gather(value_rows, "seq", axis=0, tiled=True),
    )
    attended, row_max, row_sum = attend(query_rows, key_all, value_all, same_doc)
    low_attended = attended.astype(jnp.bfloat16)
    first_resid = hidden + (matmul_f32(low_attended, out_weight) + out_bias.astype(jnp.float32))
    normed = layer_norm(first_resid, norm_gain.astype(jnp.float32), norm_bias.astype(jnp.float32))
    low_normed = normed.astype(jnp.bfloat16)
    inner = matmul_f32(low_normed, expand_weight) + expand_bias.astype(jnp.float32)
    active = gelu_exact(inner).astype(jnp.bfloat16)
    second_resid = normed + (matmul_f32(active, shrink_weight) + shrink_bias.astype(jnp.float32))
    output_tensor = layer_norm(
        second_resid, final_gain.astype(jnp.float32), final_bias.astype(jnp.float32)
    )
    kept_values = (
        low_in,
        query_rows,
        key_all,
        value_all,
        row_max,
        row_sum,
        low_attended,
        first_resid,
        low_normed,
        inner,
        active,
        second_resid,
    )
    return (output_tensor, kept_values)


def backward_layer(grad_output, params, kept_values, same_doc):
    (
        query_weight,
        query_bias,
        key_weight,
        value_weight,
        value_bias,
        out_weight,
        out_bias,
        norm_gain,
        norm_bias,
        expand_weight,
        expand_bias,
        shrink_weight,
        shrink_bias,
        final_gain,
        final_bias,
    ) = params
    (
        low_in,
        query_rows,
        key_all,
        value_all,
        row_max,
        row_sum,
        low_attended,
        first_resid,
        low_normed,
        inner,
        active,
        second_resid,
    ) = kept_values
    unused_final, pull_final = jax.vjp(
        layer_norm, second_resid, final_gain.astype(jnp.float32), final_bias.astype(jnp.float32)
    )
    grad_second, grad_fgain, grad_fbias = pull_final(grad_output)
    low_second = grad_second.astype(jnp.bfloat16)
    grad_shrink = matmul_f32(active.T, low_second)
    grad_sbias = column_sums(low_second)
    unused_gelu, pull_gelu = jax.vjp(gelu_exact, inner)
    low_inner = pull_gelu(matmul_f32(low_second, shrink_weight.T))[0].astype(jnp.bfloat16)
    grad_expand = matmul_f32(low_normed.T, low_inner)
    grad_ebias = column_sums(low_inner)
    grad_normed = grad_second + matmul_f32(low_inner, expand_weight.T)
    unused_norm, pull_norm = jax.vjp(
        layer_norm, first_resid, norm_gain.astype(jnp.float32), norm_bias.astype(jnp.float32)
    )
    grad_first, grad_ngain, grad_nbias = pull_norm(grad_normed)
    low_first = grad_first.astype(jnp.bfloat16)
    grad_out = matmul_f32(low_attended.T, low_first)
    grad_obias = column_sums(low_first)
    low_attn = matmul_f32(low_first, out_weight.T).astype(jnp.bfloat16)
    grad_qrows, grad_kall, grad_vall = attend_back(
        query_rows, key_all, value_all, same_doc, row_max, row_sum, low_attn
    )
    grad_krows, grad_vrows = (
        lax.psum_scatter(
            grad_kall.astype(jnp.bfloat16), "seq", scatter_dimension=0, tiled=True
        ).astype(jnp.float32),
        lax.psum_scatter(
            grad_vall.astype(jnp.bfloat16), "seq", scatter_dimension=0, tiled=True
        ).astype(jnp.float32),
    )
    low_query = grad_qrows.astype(jnp.bfloat16)
    low_key = grad_krows.astype(jnp.bfloat16)
    low_value = grad_vrows.astype(jnp.bfloat16)
    grad_query = matmul_f32(low_in.T, low_query)
    grad_qbias = column_sums(low_query)
    grad_key = matmul_f32(low_in.T, low_key)
    grad_value = matmul_f32(low_in.T, low_value)
    grad_vbias = column_sums(low_value)
    grad_input = (
        grad_first
        + matmul_f32(low_query, query_weight.T)
        + matmul_f32(low_key, key_weight.T)
        + matmul_f32(low_value, value_weight.T)
    )
    grads = (
        grad_query,
        grad_qbias,
        grad_key,
        grad_value,
        grad_vbias,
        grad_out,
        grad_obias,
        grad_ngain,
        grad_nbias,
        grad_expand,
        grad_ebias,
        grad_shrink,
        grad_sbias,
        grad_fgain,
        grad_fbias,
    )
    return (grad_input, grads)


def local(
    tokens,
    doc_start,
    lexical_ids,
    queries,
    match_index,
    query_weight,
    query_bias,
    key_weight,
    value_weight,
    value_bias,
    out_weight,
    out_bias,
    norm_gain,
    norm_bias,
    expand_weight,
    expand_bias,
    shrink_weight,
    shrink_bias,
    final_gain,
    final_bias,
    lexical_weight,
    lexical_bias,
    score_cot,
    encoded_cot,
):
    shards = (
        query_weight,
        query_bias,
        key_weight,
        value_weight,
        value_bias,
        out_weight,
        out_bias,
        norm_gain,
        norm_bias,
        expand_weight,
        expand_bias,
        shrink_weight,
        shrink_bias,
        final_gain,
        final_bias,
    )
    layers = query_weight.shape[0]
    rows_here = tokens.shape[0]
    first_row = lax.axis_index("seq") * rows_here
    group_starts = doc_start[0]
    own_starts = lax.dynamic_slice_in_dim(group_starts, first_row, rows_here)
    same_doc = own_starts[:, None] == group_starts[None, :]
    hidden = tokens.astype(jnp.float32)
    saved = []
    fetched = []
    for layer_index in range(layers):
        params = fetch_layer(layer_index, shards)
        fetched.append(params)
        hidden, kept_values = forward_layer(hidden, params, same_doc)
        saved.append(kept_values)
    encoded = hidden.astype(jnp.bfloat16)
    local_index = match_index[0] - first_row
    picker = (local_index[:, None] == jnp.arange(rows_here, dtype=jnp.int32)[None, :]).astype(
        jnp.bfloat16
    )
    chosen = matmul_f32(picker, encoded)
    query_vecs = queries[0].astype(jnp.float32)
    partial_scores = jnp.sum(query_vecs * chosen, axis=-1)
    lexical = matmul_f32(encoded, lexical_weight) + lexical_bias.astype(jnp.float32)[0]
    keep_mask = (lexical_ids >= 4).astype(jnp.float32)
    local_sums = jnp.stack(
        [
            jnp.sum(keep_mask * jax.nn.softplus(lexical)),
            jnp.sum(keep_mask * jax.nn.sigmoid(lexical)),
        ]
    )
    total_tokens = rows_here * lax.axis_size("dp") * lax.axis_size("seq")
    scores = lax.psum(partial_scores, "seq")[None, :]
    lexical_stats = lax.psum(local_sums, ("dp", "seq")) / total_tokens
    weighted = score_cot[0][:, None] * query_vecs
    grad_hidden = encoded_cot.astype(jnp.float32) + jnp.dot(
        picker.astype(jnp.float32).T, weighted, precision=HIGHEST
    )
    per_layer = [None] * layers
    for layer_index in reversed(range(layers)):
        params = fetch_again(layer_index, shards)
        grad_hidden, grads = backward_layer(grad_hidden, params, saved[layer_index], same_doc)
        per_layer[layer_index] = reduce_layer(*grads)
    stacked = tuple(
        (
            jnp.stack([per_layer[layer_index][member] for layer_index in range(layers)])
            for member in range(15)
        )
    )
    return (encoded, scores, lexical_stats, grad_hidden.astype(jnp.bfloat16)) + tuple(stacked)


def solution(mesh):
    placed = (
        P(("dp", "seq"), None),
        P("dp", None),
        P(("dp", "seq")),
        P("dp", None, None),
        P("dp", None),
        P(None, ("dp", "seq"), None),
        P(None, ("dp", "seq")),
        P(None, ("dp", "seq"), None),
        P(None, ("dp", "seq"), None),
        P(None, ("dp", "seq")),
        P(None, ("dp", "seq"), None),
        P(None, ("dp", "seq")),
        P(None, ("dp", "seq")),
        P(None, ("dp", "seq")),
        P(None, ("dp", "seq"), None),
        P(None, ("dp", "seq")),
        P(None, ("dp", "seq"), None),
        P(None, ("dp", "seq")),
        P(None, ("dp", "seq")),
        P(None, ("dp", "seq")),
        P(),
        P(),
        P("dp", None),
        P(("dp", "seq"), None),
    )
    return jax.shard_map(
        local,
        mesh=mesh,
        in_specs=placed,
        out_specs=(
            P(("dp", "seq"), None),
            P("dp", None),
            P(),
            P(("dp", "seq"), None),
            P(None, ("dp", "seq"), None),
            P(None, ("dp", "seq")),
            P(None, ("dp", "seq"), None),
            P(None, ("dp", "seq"), None),
            P(None, ("dp", "seq")),
            P(None, ("dp", "seq"), None),
            P(None, ("dp", "seq")),
            P(None, ("dp", "seq")),
            P(None, ("dp", "seq")),
            P(None, ("dp", "seq"), None),
            P(None, ("dp", "seq")),
            P(None, ("dp", "seq"), None),
            P(None, ("dp", "seq")),
            P(None, ("dp", "seq")),
            P(None, ("dp", "seq")),
        ),
        check_vma=False,
    )
```

profile of v0, /device:TPU:0, one launch (start us, length us, event | category | flops | bytes accessed | tf_op | source)
XLA Modules:
  0.0 3215.3 jit_solution(150537278262279798)
XLA Ops:
  34.4 43.1 %all-reduce.35 = (bf16[1024]{0:T(1024)(128)(2,1)S(1)}, bf16[1024]{0:T(1024)(128)(2,1)S(1)}, bf16[1024]{0:T(1024)(128)(2,1)S(1)}, bf16[1024]{0:T(1024)(128)(2,1)S...) all-reduce(bf16[1024]{0:T(1024)(128)(2,1)} %dynamic-update-slice, ...), channel_id=3, replica_groups=mesh['dp'=8,'seq'=4] {'dp','seq'}, use_global_device_ids=true, to_apply=%add | all-reduce | flops 16384 | bytes 65536
  80.8 48.8 %all-gather.57.cloned.1.call-done = bf16[1,1024,1024]{2,1,0:T(8,128)(2,1)} async-done(((bf16[1,32,1024]{2,1,0:T(8,128)(2,1)}), bf16[1,1024,1024]{2,1,0:T(8,128)(2,1)}) %all-gather.57.cloned.1.call-update) | async-done | bytes 2097168 | tf_op jit(solution)/shard_map/all_gather | solution.py:140
  137.4 39.4 %all-gather.10 = bf16[1,4096]{1,0:T(2,128)(2,1)S(1)} all-gather(bf16[1,128]{1,0:T(2,128)(2,1)S(1)} %get-tuple-element.573), channel_id=12, replica_groups=mesh['dp'=8,'seq'=4] {'dp','seq'}, dimensions={1}, use_global_device_ids=true | all-gather | bytes 8448 | tf_op jit(solution)/shard_map/all_gather | solution.py:148
  176.9 11.5 all-gather.55.cloned.1.call-done
  190.8 18.1 all-gather.49.cloned.1.call-done
  211.5 19.1 all-gather.47.cloned.1.call-done
  232.4 20.1 while.60
  252.6 37.2 %all-gather.61.cloned.1.call-done = bf16[1,1024,1024]{2,1,0:T(8,128)(2,1)} async-done(((bf16[1,32,1024]{2,1,0:T(8,128)(2,1)}), bf16[1,1024,1024]{2,1,0:T(8,128)(2,1)}) %all-gather.61.cloned.1.call-update) | async-done | bytes 2097168 | tf_op jit(solution)/shard_map/all_gather | solution.py:143
  292.3 77.2 %all-gather.63.cloned.1.call-done = bf16[1,1024,4096]{2,1,0:T(8,128)(2,1)} async-done(((bf16[1,32,4096]{2,1,0:T(8,128)(2,1)}), bf16[1,1024,4096]{2,1,0:T(8,128)(2,1)}) %all-gather.63.cloned.1.call-update) | async-done | bytes 8388624 | tf_op jit(solution)/shard_map/all_gather | solution.py:147
  369.6 12.9 multiply_convert_fusion.3
  382.5 66.4 %all-gather.65.cloned.1.call-done = bf16[1,4096,1024]{2,1,0:T(8,128)(2,1)} async-done(((bf16[1,128,1024]{2,1,0:T(8,128)(2,1)}), bf16[1,4096,1024]{2,1,0:T(8,128)(2,1)}) %all-gather.65.cloned.1.call-update) | async-done | bytes 8388624 | tf_op jit(solution)/shard_map/all_gather | solution.py:149
  455.2 51.6 %all-gather.71.cloned.1.call-done = bf16[1,1024,1024]{2,1,0:T(8,128)(2,1)} async-done(((bf16[1,32,1024]{2,1,0:T(8,128)(2,1)}), bf16[1,1024,1024]{2,1,0:T(8,128)(2,1)}) %all-gather.71.cloned.1.call-update) | async-done | bytes 2097168 | tf_op jit(solution)/shard_map/all_gather | solution.py:141
  509.7 55.0 %all-gather.69.cloned.1.call-done = bf16[1,1024,1024]{2,1,0:T(8,128)(2,1)} async-done(((bf16[1,32,1024]{2,1,0:T(8,128)(2,1)}), bf16[1,1024,1024]{2,1,0:T(8,128)(2,1)}) %all-gather.69.cloned.1.call-update) | async-done | bytes 2097168 | tf_op jit(solution)/shard_map/all_gather | solution.py:140
  569.5 39.4 %all-gather.25 = bf16[1,4096]{1,0:T(2,128)(2,1)S(1)} all-gather(bf16[1,128]{1,0:T(2,128)(2,1)S(1)} %get-tuple-element.574), channel_id=27, replica_groups=mesh['dp'=8,'seq'=4] {'dp','seq'}, dimensions={1}, use_global_device_ids=true | all-gather | bytes 8448 | tf_op jit(solution)/shard_map/all_gather | solution.py:148
  609.0 14.4 all-gather.67.cloned.1.call-done
  625.9 18.1 all-gather.53.cloned.1.call-done
  646.6 19.2 all-gather.51.cloned.1.call-done
  668.5 27.6 while.61
  696.1 28.9 all-gather.73.cloned.1.call-done
  727.6 77.0 %all-gather.75.cloned.1.call-done = bf16[1,1024,4096]{2,1,0:T(8,128)(2,1)} async-done(((bf16[1,32,4096]{2,1,0:T(8,128)(2,1)}), bf16[1,1024,4096]{2,1,0:T(8,128)(2,1)}) %all-gather.75.cloned.1.call-update) | async-done | bytes 8388624 | tf_op jit(solution)/shard_map/all_gather | solution.py:147
  804.6 13.4 multiply_convert_fusion.2
  818.0 66.0 %all-gather.77.cloned.1.call-done = bf16[1,4096,1024]{2,1,0:T(8,128)(2,1)} async-done(((bf16[1,128,1024]{2,1,0:T(8,128)(2,1)}), bf16[1,4096,1024]{2,1,0:T(8,128)(2,1)}) %all-gather.77.cloned.1.call-update) | async-done | bytes 8388624 | tf_op jit(solution)/shard_map/all_gather | solution.py:149
  884.0 5.9 fusion.294
  893.5 8.9 convert_reduce_fusion
  913.4 65.3 %while.62 = (s32[]{:T(128)}, bf16[8,2,192,64]{2,3,1,0:T(8,128)(2,1)S(1)}, bf16[8,2,768,64]{2,3,1,0:T(8,128)(2,1)}, bf16[8,2,768,64]{2,3,1,0:T(8,128)(2,1)}, bf16...) while((s32[]{:T(128)}, ...), condition=%wide.region_27.28_spmd.clone, body=%wide.region_25.27_spmd.clone.sunk | while | flops 191962752 | bytes 10933121 | solution.py:105
  984.4 24.0 reduce-scatter.51.cloned.1.call-done
  1011.9 27.3 reduce-scatter.49.cloned.1.call-done
  1047.4 8.9 convert_reduce_fusion.1
  1066.4 58.3 %while.63 = (s32[]{:T(128)}, bf16[8,2,192,64]{2,3,1,0:T(8,128)(2,1)S(1)}, bf16[8,2,768,64]{2,3,1,0:T(8,128)(2,1)}, bf16[8,2,768,64]{2,3,1,0:T(8,128)(2,1)}, bf16...) while((s32[]{:T(128)}, ...), condition=%wide.region_36.37_spmd.clone, body=%wide.region_34.36_spmd.clone.sunk | while | flops 191962752 | bytes 10933121 | solution.py:105
  1139.4 16.3 reduce-scatter.55.cloned.1.call-done
  1205.1 9.5 fusion.299
  1215.6 9.5 fusion.298
  1225.2 9.6 fusion.270
  1235.6 9.6 fusion.273
  1246.5 6.3 psum.14
  1259.5 86.3 %all-reduce.38.cloned.1.call-done = (f32[2]{0:T(128)}, f32[1024]{0:T(1024)}, f32[1024]{0:T(1024)}, f32[1024]{0:T(1024)}, f32[1024]{0:T(1024)}, /*index=5*/f32[10...) async-done(((f32[2]{0:T(128)}, f32[1024]{0:T(1024)}, ...) | async-done | bytes 98328 | tf_op jit(solution)/shard_map/psum | solution.py:459
  1358.8 131.7 %reduce-scatter.59.cloned.1.call-done = f32[32,1024]{1,0:T(8,128)} async-done(((f32[1024,1024]{1,0:T(8,128)}), f32[32,1024]{1,0:T(8,128)}) %reduce-scatter.59.cloned.1.call-update) | async-done | bytes 131088
  1491.8 137.9 %reduce-scatter.67.cloned.1.call-done = f32[32,1024]{1,0:T(8,128)} async-done(((f32[1024,1024]{1,0:T(8,128)}), f32[32,1024]{1,0:T(8,128)}) %reduce-scatter.67.cloned.1.call-update) | async-done | bytes 131088
  1631.0 137.7 %reduce-scatter.63.cloned.1.call-done = f32[32,1024]{1,0:T(8,128)} async-done(((f32[1024,1024]{1,0:T(8,128)}), f32[32,1024]{1,0:T(8,128)}) %reduce-scatter.63.cloned.1.call-update) | async-done | bytes 131088
  1769.9 137.9 %reduce-scatter.57.cloned.1.call-done = f32[32,1024]{1,0:T(8,128)} async-done(((f32[1024,1024]{1,0:T(8,128)}), f32[32,1024]{1,0:T(8,128)}) %reduce-scatter.57.cloned.1.call-update) | async-done | bytes 131088
  1909.1 137.7 %reduce-scatter.39.cloned.1.call-done = f32[32,1024]{1,0:T(8,128)} async-done(((f32[1024,1024]{1,0:T(8,128)}), f32[32,1024]{1,0:T(8,128)}) %reduce-scatter.39.cloned.1.call-update) | async-done | bytes 131088 | tf_op jit(solution)/shard_map/reduce_scatter | solution.py:216
  2046.8 139.3 %reduce-scatter.37.cloned.1.call-done = f32[32,1024]{1,0:T(8,128)} async-done(((f32[1024,1024]{1,0:T(8,128)}), f32[32,1024]{1,0:T(8,128)}) %reduce-scatter.37.cloned.1.call-update) | async-done | bytes 131088 | tf_op jit(solution)/shard_map/reduce_scatter | solution.py:216
  2188.5 136.9 %reduce-scatter.65.cloned.1.call-done = f32[32,1024]{1,0:T(8,128)} async-done(((f32[1024,1024]{1,0:T(8,128)}), f32[32,1024]{1,0:T(8,128)}) %reduce-scatter.65.cloned.1.call-update) | async-done | bytes 131088
  2326.7 138.0 %reduce-scatter.61.cloned.1.call-done = f32[32,1024]{1,0:T(8,128)} async-done(((f32[1024,1024]{1,0:T(8,128)}), f32[32,1024]{1,0:T(8,128)}) %reduce-scatter.61.cloned.1.call-update) | async-done | bytes 131088
  2467.4 178.1 %reduce-scatter.47.cloned.1.call-done = f32[128,1024]{1,0:T(8,128)} async-done(((f32[4096,1024]{1,0:T(8,128)}), f32[128,1024]{1,0:T(8,128)}) %reduce-scatter.47.cloned.1.call-update) | async-done | bytes 524304 | tf_op jit(solution)/shard_map/reduce_scatter | solution.py:222
  2645.5 186.8 %reduce-scatter.45.cloned.1.call-done = f32[128,1024]{1,0:T(8,128)} async-done(((f32[4096,1024]{1,0:T(8,128)}), f32[128,1024]{1,0:T(8,128)}) %reduce-scatter.45.cloned.1.call-update) | async-done | bytes 524304 | tf_op jit(solution)/shard_map/reduce_scatter | solution.py:222
  2834.6 185.3 %reduce-scatter.43.cloned.1.call-done = f32[32,4096]{1,0:T(8,128)} async-done(((f32[1024,4096]{1,0:T(8,128)}), f32[32,4096]{1,0:T(8,128)}) %reduce-scatter.43.cloned.1.call-update) | async-done | bytes 524304 | tf_op jit(solution)/shard_map/reduce_scatter | solution.py:220
  3019.8 186.0 %reduce-scatter.41.cloned.1.call-done = f32[32,4096]{1,0:T(8,128)} async-done(((f32[1024,4096]{1,0:T(8,128)}), f32[32,4096]{1,0:T(8,128)}) %reduce-scatter.41.cloned.1.call-update) | async-done | bytes 524304 | tf_op jit(solution)/shard_map/reduce_scatter | solution.py:220
  (592 shorter events, 385.5 us)
Async XLA Ops:
  7.2 122.5 %copy-start = (bf16[192,1024]{1,0:T(8,128)(2,1)S(1)}, bf16[192,1024]{1,0:T(8,128)(2,1)}, u32[]{:S(2)}) copy-start(bf16[192,1024]{1,0:T(8,128)(2,1)} %param.32) | copy-start | bytes 1179652
  7.2 70.4 %all-gather.59.cloned.1.call-start = ((), (), s32[]{:S(2)}) async-start(), calls=%async_computation.28 | async-start | bytes 2162688 | tf_op jit(solution)/shard_map/all_gather | solution.py:141
  8.8 120.8 %all-gather.57.cloned.1.call-start = ((), (), s32[]{:S(2)}) async-start(), calls=%async_computation.27 | async-start | bytes 2162688 | tf_op jit(solution)/shard_map/all_gather | solution.py:140
  10.4 177.9 %all-gather.55.cloned.1.call-start = ((), (), s32[]{:S(2)}) async-start(), calls=%async_computation.26 | async-start | bytes 2162688 | tf_op jit(solution)/shard_map/all_gather | solution.py:138
  12.0 196.9 %all-gather.49.cloned.1.call-start = ((), (), s32[]{:S(2)}) async-start(), calls=%async_computation.17 | async-start | bytes 1966080 | tf_op jit(solution)/shard_map/all_gather | solution.py:257
  77.5 55.1 %copy-start.39 = (bf16[2,32,1024]{2,1,0:T(8,128)(2,1)S(1)}, bf16[2,32,1024]{2,1,0:T(8,128)(2,1)}, u32[]{:S(2)}) copy-start(bf16[2,32,1024]{2,1,0:T(8,128)(2,1)} %param.42) | copy-start | bytes 393220
  77.6 55.8 %copy-start.34 = (bf16[2,32,4096]{2,1,0:T(8,128)(2,1)S(1)}, bf16[2,32,4096]{2,1,0:T(8,128)(2,1)}, u32[]{:S(2)}) copy-start(bf16[2,32,4096]{2,1,0:T(8,128)(2,1)} %param.46) | copy-start | bytes 1572868
  80.7 53.6 %copy-start.35 = (bf16[2,128,1024]{2,1,0:T(8,128)(2,1)S(1)}, bf16[2,128,1024]{2,1,0:T(8,128)(2,1)}, u32[]{:S(2)}) copy-start(bf16[2,128,1024]{2,1,0:T(8,128)(2,1)} %param.48) | copy-start | bytes 1572868
  80.7 56.6 %copy-start.42 = (s32[1,768]{1,0:T(1,128)S(1)}, s32[1,768]{1,0:T(1,128)}, u32[]{:S(2)}) copy-start(s32[1,768]{1,0:T(1,128)} %param.33) | copy-start | bytes 9220
  80.7 56.7 %copy-start.44 = (bf16[2,128]{1,0:T(2,128)(2,1)S(1)}, bf16[2,128]{1,0:T(2,128)(2,1)}, u32[]{:S(2)}) copy-start(bf16[2,128]{1,0:T(2,128)(2,1)} %param.47) | copy-start | bytes 1540
  80.8 149.8 %all-gather.47.cloned.1.call-start = ((), (), s32[]{:S(2)}) async-start(), calls=%async_computation.16 | async-start | bytes 1966080 | tf_op jit(solution)/shard_map/all_gather | solution.py:256
  132.6 157.2 %all-gather.61.cloned.1.call-start = ((), (), s32[]{:S(2)}) async-start(), calls=%async_computation.29 | async-start | bytes 2162688 | tf_op jit(solution)/shard_map/all_gather | solution.py:143
  133.3 236.2 %all-gather.63.cloned.1.call-start = ((), (), s32[]{:S(2)}) async-start(), calls=%async_computation.30 | async-start | bytes 8650752 | tf_op jit(solution)/shard_map/all_gather | solution.py:147
  134.3 314.6 %all-gather.65.cloned.1.call-start = ((), (), s32[]{:S(2)}) async-start(), calls=%async_computation.31 | async-start | bytes 8650752 | tf_op jit(solution)/shard_map/all_gather | solution.py:149
  135.2 371.6 %all-gather.71.cloned.1.call-start = ((), (), s32[]{:S(2)}) async-start(), calls=%async_computation.34 | async-start | bytes 2162688 | tf_op jit(solution)/shard_map/all_gather | solution.py:141
  135.9 428.8 %all-gather.69.cloned.1.call-start = ((), (), s32[]{:S(2)}) async-start(), calls=%async_computation.33 | async-start | bytes 2162688 | tf_op jit(solution)/shard_map/all_gather | solution.py:140
  136.5 487.0 %all-gather.67.cloned.1.call-start = ((), (), s32[]{:S(2)}) async-start(), calls=%async_computation.32 | async-start | bytes 2162688 | tf_op jit(solution)/shard_map/all_gather | solution.py:138
  137.2 506.8 %all-gather.53.cloned.1.call-start = ((), (), s32[]{:S(2)}) async-start(), calls=%async_computation.19 | async-start | bytes 1966080 | tf_op jit(solution)/shard_map/all_gather | solution.py:257
  137.4 311.5 %copy-start.37 = (f32[1024]{0:T(1024)}, f32[1024]{0:T(1024)S(1)}, u32[]{:S(2)}) copy-start(f32[1024]{0:T(1024)S(1)} %convert_element_type.374) | copy-start | bytes 12292
  252.5 37.2 %copy-start.23 = (bf16[8,2,192,64]{2,3,1,0:T(8,128)(2,1)}, bf16[8,2,192,64]{2,3,1,0:T(8,128)(2,1)S(1)}, u32[]{:S(2)}) copy-start(bf16[8,2,192,64]{2,3,1,0:T(8,128)(2,1)S(1)} %get-tuple-element.1150) | copy-start | bytes 1179652
  252.6 129.9 %copy-start.6 = (bf16[8,2,768,64]{2,3,1,0:T(8,128)(2,1)}, bf16[8,2,768,64]{2,3,1,0:T(8,128)(2,1)S(1)}, u32[]{:S(2)}) copy-start(bf16[8,2,768,64]{2,3,1,0:T(8,128)(2,1)S(1)} %get-tuple-element.1135) | copy-start | bytes 4718596
  252.6 129.9 %copy-start.12 = (bf16[8,2,192,64]{2,3,1,0:T(8,128)(2,1)}, bf16[8,2,192,64]{2,3,1,0:T(8,128)(2,1)S(1)}, u32[]{:S(2)}) copy-start(bf16[8,2,192,64]{2,3,1,0:T(8,128)(2,1)S(1)} %get-tuple-element.225) | copy-start | bytes 1179652
  455.2 153.8 %copy-start.49 = (s32[1,32]{1,0:T(1,128)S(1)}, s32[1,32]{1,0:T(1,128)}, u32[]{:S(2)}) copy-start(s32[1,32]{1,0:T(1,128)} %param.36) | copy-start | bytes 388
  509.7 156.1 %all-gather.51.cloned.1.call-start = ((), (), s32[]{:S(2)}) async-start(), calls=%async_computation.18 | async-start | bytes 1966080 | tf_op jit(solution)/shard_map/all_gather | solution.py:256
  567.7 157.3 %all-gather.73.cloned.1.call-start = ((), (), s32[]{:S(2)}) async-start(), calls=%async_computation.35 | async-start | bytes 2162688 | tf_op jit(solution)/shard_map/all_gather | solution.py:143
  568.2 236.4 %all-gather.75.cloned.1.call-start = ((), (), s32[]{:S(2)}) async-start(), calls=%async_computation.36 | async-start | bytes 8650752 | tf_op jit(solution)/shard_map/all_gather | solution.py:147
  568.8 315.2 %all-gather.77.cloned.1.call-start = ((), (), s32[]{:S(2)}) async-start(), calls=%async_computation.37 | async-start | bytes 8650752 | tf_op jit(solution)/shard_map/all_gather | solution.py:149
  569.4 439.0 %reduce-scatter.51.cloned.1.call-start = ((), (), s32[]{:S(2)}) async-start(), calls=%async_computation.39 | async-start | bytes 1966080
  609.0 281.1 %copy-start.47 = (s32[32]{0:T(128)}, s32[32]{0:T(128)S(1)}, u32[]{:S(2)}) copy-start(s32[32]{0:T(128)S(1)} %subtract_bitcast_fusion) | copy-start | bytes 388
  696.1 28.9 copy-start.24
  696.1 121.9 %copy-start.14 = (bf16[8,2,192,64]{2,3,1,0:T(8,128)(2,1)}, bf16[8,2,192,64]{2,3,1,0:T(8,128)(2,1)S(1)}, u32[]{:S(2)}) copy-start(bf16[8,2,192,64]{2,3,1,0:T(8,128)(2,1)S(1)} %get-tuple-element.226) | copy-start | bytes 1179652
  978.7 63.1 %copy-start.2 = (bf16[8,2,192,64]{2,3,1,0:T(8,128)(2,1)}, bf16[8,2,192,64]{2,3,1,0:T(8,128)(2,1)S(1)}, u32[]{:S(2)}) copy-start(bf16[8,2,192,64]{2,3,1,0:T(8,128)(2,1)S(1)} %get-tuple-element.229) | copy-start | bytes 1179652
  981.5 57.6 %reduce-scatter.49.cloned.1.call-start = ((), (), s32[]{:S(2)}) async-start(), calls=%async_computation.38 | async-start | bytes 1966080
  984.3 171.4 %reduce-scatter.55.cloned.1.call-start = ((), (), s32[]{:S(2)}) async-start(), calls=%async_computation.41 | async-start | bytes 1966080
  1127.4 67.6 %reduce-scatter.53.cloned.1.call-start = ((), (), s32[]{:S(2)}) async-start(), calls=%async_computation.40 | async-start | bytes 1966080
  1130.3 215.5 %all-reduce.38.cloned.1.call-start = ((), (), s32[]{:S(2)}) async-start(), calls=%async_computation.48 | async-start | bytes 197632 | tf_op jit(solution)/shard_map/psum | solution.py:459
  1159.6 330.9 %reduce-scatter.59.cloned.1.call-start = ((), (), s32[]{:S(2)}) async-start(), calls=%async_computation.43 | async-start | bytes 4325376
  1162.4 467.3 %reduce-scatter.67.cloned.1.call-start = ((), (), s32[]{:S(2)}) async-start(), calls=%async_computation.47 | async-start | bytes 4325376
  1165.3 603.4 %reduce-scatter.63.cloned.1.call-start = ((), (), s32[]{:S(2)}) async-start(), calls=%async_computation.45 | async-start | bytes 4325376
  1169.0 738.8 %reduce-scatter.57.cloned.1.call-start = ((), (), s32[]{:S(2)}) async-start(), calls=%async_computation.42 | async-start | bytes 4325376
  1178.1 868.7 %reduce-scatter.39.cloned.1.call-start = ((), (), s32[]{:S(2)}) async-start(), calls=%async_computation.21 | async-start | bytes 4325376 | tf_op jit(solution)/shard_map/reduce_scatter | solution.py:216
  1182.0 1004.1 %reduce-scatter.37.cloned.1.call-start = ((), (), s32[]{:S(2)}) async-start(), calls=%async_computation.20 | async-start | bytes 4325376 | tf_op jit(solution)/shard_map/reduce_scatter | solution.py:216
  1185.8 1139.6 %reduce-scatter.65.cloned.1.call-start = ((), (), s32[]{:S(2)}) async-start(), calls=%async_computation.46 | async-start | bytes 4325376
  1194.9 1269.8 %reduce-scatter.61.cloned.1.call-start = ((), (), s32[]{:S(2)}) async-start(), calls=%async_computation.44 | async-start | bytes 4325376
  1204.1 1441.4 %reduce-scatter.47.cloned.1.call-start = ((), (), s32[]{:S(2)}) async-start(), calls=%async_computation.25 | async-start | bytes 17301504 | tf_op jit(solution)/shard_map/reduce_scatter | solution.py:222
  1214.7 1617.6 %reduce-scatter.45.cloned.1.call-start = ((), (), s32[]{:S(2)}) async-start(), calls=%async_computation.24 | async-start | bytes 17301504 | tf_op jit(solution)/shard_map/reduce_scatter | solution.py:222
  1225.2 1794.7 %reduce-scatter.43.cloned.1.call-start = ((), (), s32[]{:S(2)}) async-start(), calls=%async_computation.23 | async-start | bytes 17301504 | tf_op jit(solution)/shard_map/reduce_scatter | solution.py:220
  1234.9 1970.9 %reduce-scatter.41.cloned.1.call-start = ((), (), s32[]{:S(2)}) async-start(), calls=%async_computation.22 | async-start | bytes 17301504 | tf_op jit(solution)/shard_map/reduce_scatter | solution.py:220
  (41 other events, 162.0 us)
Sparse Core Ops, SparseCore 0:
  11.5 59.4 all-gather.58
  74.3 55.2 all-gather.56
  133.1 55.2 all-gather.54
  190.4 18.4 all-gather.48
  210.9 19.6 all-gather.46
  233.3 56.4 all-gather.60
  293.2 76.2 all-gather.62
  373.0 75.8 all-gather.64
  451.8 54.9 all-gather.70
  509.5 55.2 all-gather.68
  568.2 55.2 all-gather.66
  625.5 18.4 all-gather.52
  646.1 19.6 all-gather.50
  668.5 56.4 all-gather.72
  728.3 76.2 all-gather.74
  807.9 76.0 all-gather.76
  981.6 26.7 reduce-scatter.50
  1011.0 28.1 reduce-scatter.48
  1127.5 28.2 reduce-scatter.54
  1158.3 28.1 reduce-scatter.52
  1194.6 151.0 all-reduce.37
  1348.0 142.4 reduce-scatter.58
  1492.8 136.8 reduce-scatter.66
  1631.8 136.7 reduce-scatter.62
  1770.9 136.8 reduce-scatter.56
  1909.9 136.8 reduce-scatter.38
  2049.0 137.0 reduce-scatter.36
  2188.4 136.9 reduce-scatter.64
  2327.7 136.9 reduce-scatter.60
  2466.8 178.6 reduce-scatter.46
  2647.8 184.4 reduce-scatter.44
  2834.6 185.2 reduce-scatter.42
  3022.0 183.7 reduce-scatter.40
where the time goes:
time: 3230 us; the launch traced here: 3220 us
  waiting for transfers between devices  2600 us (80%)
  matrix products  323 us (10%)
  blocking collectives  128 us (4%)
  local copies, waits for them, and re-layouts  105 us (3%)
  other arithmetic  40.9 us (1%)
    unnamed x43, waiting for transfers between devices  892 us
    reduce_scatter x2, waiting for transfers between devices, reduce_layer(): lax.psum_scatter(grad_expand, ('dp', 'seq'), scatter_dimension=0, tiled=T...  371 us
    reduce_scatter x2, waiting for transfers between devices, reduce_layer(): lax.psum_scatter(grad_shrink, ('dp', 'seq'), scatter_dimension=0, tiled=T...  365 us
    reduce_scatter x2, waiting for transfers between devices, reduce_layer(): lax.psum_scatter(grad_output, ('dp', 'seq'), scatter_dimension=0, tiled=T...  277 us
    dot_general x35, matrix products, matmul_f32(): return jnp.dot(left, right, preferred_element_type=jnp.float32)  156 us
    all_gather x2, waiting for transfers between devices, fetch_layer(): lax.all_gather(expand_weight[layer_index], ('dp', 'seq'), axis=0, tiled=T...  154 us
    all_gather x2, waiting for transfers between devices, fetch_layer(): lax.all_gather(shrink_weight[layer_index], ('dp', 'seq'), axis=0, tiled=T...  132 us
    all_gather x2, waiting for transfers between devices, fetch_layer(): lax.all_gather(key_weight[layer_index], ('dp', 'seq'), axis=0, tiled=True)  104 us
  transfers between devices with their start and end apart: 33, of which 31 were waited for; matrix products, arithmetic and copies ran while one was open for 8% of the time, Pallas kernels for 0%

commit v1 on v0

v1 whole, which is shorter than its diff:
```python
import functools
import math

import jax
import jax.numpy as jnp
from jax import lax
from jax.experimental import pallas as pl
from jax.experimental.pallas import tpu as pltpu
from jax.sharding import PartitionSpec as P

HEAD = 64
EPSILON = 1e-05
NEGATIVE = -1e30
HIGHEST = lax.Precision.HIGHEST
AXES = ("dp", "seq")
BF = jnp.bfloat16
F32 = jnp.float32
VMEM_LIMIT = 56 * 1024 * 1024


def dot(left, right, left_dim=1, right_dim=0):
    return lax.dot_general(
        left, right, (((left_dim,), (right_dim,)), ((), ())), preferred_element_type=F32
    )


def head_lanes(shape, half):
    lane = lax.broadcasted_iota(jnp.int32, shape, 1)
    return (lane < HEAD) if half == 0 else (lane >= HEAD)


def attend_kernel(block, qkv_ref, col_ref, row_ref, out_ref, max_ref, sum_ref):
    tokens, width = out_ref.shape
    pairs = width // (2 * HEAD)
    scale = 1.0 / math.sqrt(HEAD)
    for pair in range(pairs):
        lo = pair * 2 * HEAD
        keys = qkv_ref[:, width + lo : width + lo + 2 * HEAD]
        values = qkv_ref[:, 2 * width + lo : 2 * width + lo + 2 * HEAD]
        values_t = values.astype(F32).T.astype(BF)
        for start in range(0, tokens, block):
            queries = qkv_ref[start : start + block, lo : lo + 2 * HEAD] * scale
            queries = queries.astype(BF)
            same = col_ref[...] == row_ref[:, start : start + block]
            halves = []
            for half in range(2):
                lanes = head_lanes(queries.shape, half)
                scores = dot(keys, jnp.where(lanes, queries, jnp.zeros_like(queries)), 1, 1)
                scores = jnp.where(same, scores, NEGATIVE)
                top = jnp.max(scores, axis=0, keepdims=True)
                raised = jnp.exp(scores - top)
                total = jnp.sum(raised, axis=0, keepdims=True)
                probs = (raised * (1.0 / total)).astype(BF)
                mixed = dot(values_t, probs)
                halves.append(mixed[half * HEAD : (half + 1) * HEAD])
                head = 2 * pair + half
                max_ref[head : head + 1, start : start + block] = top
                sum_ref[head : head + 1, start : start + block] = total
            joined = jnp.concatenate(halves, axis=0)
            out_ref[start : start + block, lo : lo + 2 * HEAD] = joined.T.astype(BF)


def attend_back_kernel(
    block, qkv_ref, col_ref, row_ref, max_ref, sum_ref, grad_ref, out_ref, key_acc, value_acc
):
    tokens, width = grad_ref.shape
    pairs = width // (2 * HEAD)
    scale = 1.0 / math.sqrt(HEAD)
    for pair in range(pairs):
        lo = pair * 2 * HEAD
        keys = qkv_ref[:, width + lo : width + lo + 2 * HEAD]
        values = qkv_ref[:, 2 * width + lo : 2 * width + lo + 2 * HEAD]
        keys_t = keys.astype(F32).T.astype(BF)
        key_acc[...] = jnp.zeros_like(key_acc)
        value_acc[...] = jnp.zeros_like(value_acc)
        for start in range(0, tokens, block):
            queries = (qkv_ref[start : start + block, lo : lo + 2 * HEAD] * scale).astype(BF)
            grads = grad_ref[start : start + block, lo : lo + 2 * HEAD]
            same = col_ref[...] == row_ref[:, start : start + block]
            halves = []
            for half in range(2):
                lanes = head_lanes(queries.shape, half)
                own_queries = jnp.where(lanes, queries, jnp.zeros_like(queries))
                own_grads = jnp.where(lanes, grads, jnp.zeros_like(grads))
                head = 2 * pair + half
                top = max_ref[head : head + 1, start : start + block]
                total = sum_ref[head : head + 1, start : start + block]
                scores = dot(keys, own_queries, 1, 1)
                scores = jnp.where(same, scores, NEGATIVE)
                probs = jnp.exp(scores - top) * (1.0 / total)
                grad_probs = dot(values, own_grads, 1, 1)
                shared = jnp.sum(probs * grad_probs, axis=0, keepdims=True)
                grad_scores = (probs * (grad_probs - shared)).astype(BF)
                value_acc[...] += dot(probs.astype(BF), own_grads)
                key_acc[...] += dot(grad_scores, own_queries)
                mixed = dot(keys_t, grad_scores)
                halves.append(mixed[half * HEAD : (half + 1) * HEAD])
            joined = jnp.concatenate(halves, axis=0) * scale
            out_ref[start : start + block, lo : lo + 2 * HEAD] = joined.T.astype(BF)
        out_ref[:, width + lo : width + lo + 2 * HEAD] = key_acc[...].astype(BF)
        out_ref[:, 2 * width + lo : 2 * width + lo + 2 * HEAD] = value_acc[...].astype(BF)


def attend(qkv, starts):
    tokens, width = qkv.shape[0], qkv.shape[1] // 3
    heads = width // HEAD
    whole = pl.BlockSpec(memory_space=pltpu.VMEM)
    return pl.pallas_call(
        functools.partial(attend_kernel, 256),
        out_shape=(
            jax.ShapeDtypeStruct((tokens, width), BF),
            jax.ShapeDtypeStruct((heads, tokens), F32),
            jax.ShapeDtypeStruct((heads, tokens), F32),
        ),
        in_specs=[whole] * 3,
        out_specs=(whole,) * 3,
        compiler_params=pltpu.CompilerParams(vmem_limit_bytes=VMEM_LIMIT),
        cost_estimate=pl.CostEstimate(
            flops=4 * tokens * tokens * width,
            bytes_accessed=8 * tokens * width,
            transcendentals=heads * tokens * tokens,
        ),
    )(qkv, starts[:, None], starts[None, :])


def attend_back(qkv, starts, row_max, row_sum, grads):
    tokens, width = grads.shape
    whole = pl.BlockSpec(memory_space=pltpu.VMEM)
    return pl.pallas_call(
        functools.partial(attend_back_kernel, 256),
        out_shape=jax.ShapeDtypeStruct((tokens, 3 * width), BF),
        in_specs=[whole] * 6,
        out_specs=whole,
        scratch_shapes=[
            pltpu.VMEM((tokens, 2 * HEAD), F32),
            pltpu.VMEM((tokens, 2 * HEAD), F32),
        ],
        compiler_params=pltpu.CompilerParams(vmem_limit_bytes=VMEM_LIMIT),
        cost_estimate=pl.CostEstimate(
            flops=10 * tokens * tokens * width,
            bytes_accessed=14 * tokens * width,
            transcendentals=(width // HEAD) * tokens * tokens,
        ),
    )(qkv, starts[:, None], starts[None, :], row_max, row_sum, grads)


def place_kernel(count, order, sizes, *refs):
    pieces, outs = refs[:count], refs[count:]
    me = lax.axis_index("dp")
    for step, piece in zip(order, pieces):
        where = me ^ step
        first = 0
        for member, rows in enumerate(sizes):
            at = pl.multiple_of(where * rows, rows)
            outs[member][pl.ds(at, rows), :] = piece[first : first + rows, :]
            first += rows


def place(pieces, order, sizes):
    columns = pieces[0].shape[1]
    count = len(pieces)
    whole = pl.BlockSpec(memory_space=pltpu.VMEM)
    return pl.pallas_call(
        functools.partial(place_kernel, count, tuple(order), tuple(sizes)),
        out_shape=tuple(jax.ShapeDtypeStruct((count * rows, columns), BF) for rows in sizes),
        in_specs=[whole] * count,
        out_specs=(whole,) * len(sizes),
        compiler_params=pltpu.CompilerParams(vmem_limit_bytes=VMEM_LIMIT),
        cost_estimate=pl.CostEstimate(
            flops=0, bytes_accessed=4 * count * sum(sizes) * columns, transcendentals=0
        ),
    )(*pieces)


def after(array, *others):
    return lax.optimization_barrier((array,) + others)[0]


def solution(mesh):
    n_dp, n_seq = mesh.shape["dp"], mesh.shape["seq"]
    n_dev = n_dp * n_seq
    special = (n_dp, n_seq) == (8, 4)

    def swap(array, bit):
        return lax.ppermute(array, AXES, [(p, p ^ bit) for p in range(n_dev)])

    def bits_of(count, unit=1):
        bits = []
        while count > 1:
            bits.append(unit)
            unit, count = unit * 2, count // 2
        return bits

    seq_bits, dp_bits = bits_of(n_seq), bits_of(n_dp, n_seq)

    def spread(piece, bits):
        pieces, steps = [piece], [0]
        for bit in reversed(bits):
            pieces = pieces + [swap(p, bit) for p in pieces]
            steps = steps + [s ^ bit for s in steps]
        return pieces, steps

    seq_steps = [0]
    for bit in reversed(seq_bits):
        seq_steps = seq_steps + [s ^ bit for s in seq_steps]

    def gather_seq(rows):
        return jnp.concatenate(spread(rows, seq_bits)[0], axis=0)

    def reduce_seq(left, right, own_rows):
        weight, dims = right
        half = left.shape[0] // 2
        sent = dot(left[half:], weight, *dims).astype(BF)
        kept = dot(left[:half], weight, *dims)
        keep = [kept[i * own_rows : (i + 1) * own_rows] for i in range(n_seq // 2)]
        send = [sent[i * own_rows : (i + 1) * own_rows] for i in range(n_seq // 2)]
        order = seq_bits
        for place_in, bit in enumerate(order):
            got = [swap(block, bit) for block in reversed(send)][::-1]
            total = [a + b.astype(F32) for a, b in zip(keep, got)]
            if place_in + 1 < len(order):
                middle = len(total) // 2
                keep, send = total[:middle], [t.astype(BF) for t in total[middle:]]
        return total[0]

    def halve(array, index_bit, bit):
        chosen = index_bit.astype(jnp.bool_)
        send = jnp.where(chosen, array[0], array[1])
        keep = jnp.where(chosen, array[1], array[0])
        return keep, swap(send, bit)

    def local(
        tokens, doc_start, lexical_ids, queries, match_index,
        query_weight, query_bias, key_weight, value_weight, value_bias,
        out_weight, out_bias, norm_gain, norm_bias, expand_weight, expand_bias,
        shrink_weight, shrink_bias, final_gain, final_bias,
        lexical_weight, lexical_bias, score_cot, encoded_cot,
    ):
        layers, part, dim = query_weight.shape
        hidden_dim = expand_weight.shape[2]
        hidden_part = shrink_weight.shape[1]
        rows_here = tokens.shape[0]
        pairs_here = dim // (2 * HEAD) // n_seq
        width = pairs_here * 2 * HEAD
        own_hidden = hidden_dim // n_seq
        block_rows = dim // n_dp
        dp, seq = lax.axis_index("dp"), lax.axis_index("seq")
        flat = dp * n_seq + seq

        def bit_of(index, bit):
            return lax.bitwise_and(lax.div(index, bit), 1)

        def by_origin(pieces):
            for bit in seq_bits:
                chosen = bit_of(seq, bit).astype(jnp.bool_)
                pieces = [jnp.where(chosen, pieces[j ^ bit], pieces[j]) for j in range(n_seq)]
            return pieces

        def exchange_steps(blocks):
            pieces = by_origin(blocks)
            return [pieces[0]] + [swap(pieces[step], step) for step in range(1, n_seq)]

        def exchange_seq(blocks):
            return by_origin(exchange_steps(blocks))

        small_full = (
            query_bias, value_bias, out_bias, norm_gain, norm_bias, shrink_bias, final_gain, final_bias,
        )
        small = jnp.concatenate(list(small_full) + [expand_bias], axis=1).reshape(1, -1)
        small_len = small.shape[1]
        small = jnp.pad(small, ((0, 15), (0, 3 * width - small_len)))

        def head_split(weight):
            cut = [weight[:, i * 2 * HEAD : (i + 1) * 2 * HEAD] for i in range(pairs_here * n_seq)]
            return [cut[s::n_seq] for s in range(n_seq)]

        def hidden_split(weight):
            cut = [
                weight[:, i * hidden_part : (i + 1) * hidden_part] for i in range(n_dp * n_seq)
            ]
            return [cut[s::n_seq] for s in range(n_seq)]

        def qkv_split(layer):
            three = [head_split(w[layer]) for w in (query_weight, key_weight, value_weight)]
            return [jnp.concatenate(three[0][s] + three[1][s] + three[2][s], axis=1) for s in range(n_seq)]

        first = exchange_seq([jnp.concatenate([b, small], axis=0) for b in qkv_split(0)])
        first_rows = jnp.concatenate([p[:part] for p in first], axis=0)
        first_small = jnp.concatenate([p[part : part + 1] for p in first], axis=0)
        first_small = jnp.pad(first_small, ((0, 16 - n_seq), (0, 0)))
        pieces, steps = spread(jnp.concatenate([first_rows, first_small], axis=0), dp_bits)
        dp_steps = [s // n_seq for s in steps]
        qkv_first, small_all = place(pieces, dp_steps, (block_rows, 16))
        first_pieces = pieces
        small_all = small_all.reshape(n_dp, 16, -1)[:, :n_seq, :small_len]
        small_all = small_all.reshape(n_dev, layers, -1)

        hidden_now = tokens.astype(F32)
        group = gather_seq(tokens)

        blocks = [[] for _ in range(n_seq)]
        for layer in range(layers):
            here = hidden_split(expand_weight[layer])
            more = qkv_split(layer) if layer else None
            for s in range(n_seq):
                blocks[s] += ([more[s]] if layer else []) + here[s]
        second = exchange_seq([jnp.concatenate(b, axis=1) for b in blocks])
        second = jnp.concatenate(second, axis=0)

        if special:
            pieces, steps = spread(out_weight, seq_bits)
            pieces = by_origin([pieces[steps.index(step)] for step in range(n_seq)])
            out_all = []
            for layer in range(layers):
                rows = jnp.concatenate([p[layer] for p in pieces], axis=0)
                if layer:
                    rows = after(rows, out_all[0])
                for bit in (1, 2):
                    moved = swap(rows, n_seq * bit)
                    rows = jnp.where(bit_of(seq, bit) == bit_of(dp, bit), rows, moved)
                moved = swap(rows, n_seq * 4)
                upper = bit_of(dp, 4) == 1
                out_all.append(
                    jnp.concatenate(
                        [jnp.where(upper, moved, rows), jnp.where(upper, rows, moved)], axis=0
                    )
                )
        else:
            whole_out = lax.all_gather(out_weight, AXES, axis=1, tiled=True)
            cut = whole_out.reshape(layers, pairs_here, n_seq, 2 * HEAD, dim)
            cut = lax.dynamic_index_in_dim(cut, seq, 2, keepdims=False)
            out_all = [cut[layer].reshape(width, dim) for layer in range(layers)]

        pieces, steps = spread(after(second[:, :own_hidden], first_pieces[1]), dp_bits)
        (expand_first,) = place(pieces, dp_steps, (block_rows,))
        pieces, steps = spread(after(shrink_weight[0], pieces[1]), dp_bits)
        (shrink_first,) = place(pieces, dp_steps, (hidden_part,))

        qkv_all, expand_all, shrink_all = [qkv_first], [expand_first], [shrink_first]
        at = own_hidden
        for layer in range(1, layers):
            rest = second[:, at : at + 3 * width]
            at += 3 * width
            pieces, steps = spread(after(rest, pieces[1]), dp_bits)
            qkv_all += place(pieces, dp_steps, (block_rows,))
            rest = after(second[:, at : at + own_hidden], pieces[1])
            at += own_hidden
            expand_all.append(lax.all_gather(rest, "dp", axis=0, tiled=True))
            rest = after(shrink_weight[layer], pieces[1])
            shrink_all.append(lax.all_gather(rest, "dp", axis=0, tiled=True))

        full = small_all[:, :, : 8 * part].reshape(n_dev, layers, 8, part)
        full = full.transpose(1, 2, 0, 3).reshape(layers, 8, dim).astype(F32)
        by_column = full[:, :2].reshape(layers, 2, pairs_here, n_seq, 2 * HEAD)
        by_column = lax.dynamic_index_in_dim(by_column, seq, 3, keepdims=False)
        by_column = by_column.reshape(layers, 2, width)
        hidden_bias = small_all[:, :, 8 * part :].reshape(n_dp, n_seq, layers, hidden_part)
        hidden_bias = lax.dynamic_index_in_dim(hidden_bias, seq, 1, keepdims=False)
        hidden_bias = hidden_bias.transpose(1, 0, 2).reshape(layers, own_hidden).astype(F32)

        starts_here = doc_start[0].reshape(n_seq, rows_here)
        starts = jnp.concatenate(
            [
                lax.dynamic_index_in_dim(starts_here, seq ^ step, 0, keepdims=False)
                for step in seq_steps
            ]
        )

        def norm_parts(resid):
            center = resid - jnp.mean(resid, axis=-1, keepdims=True)
            inverse = lax.rsqrt(jnp.mean(center * center, axis=-1, keepdims=True) + EPSILON)
            return center * inverse, inverse

        def norm_back(upstream, gain, rhat, inverse):
            scaled = upstream * gain
            mean_one = jnp.mean(scaled, axis=-1, keepdims=True)
            mean_two = jnp.mean(scaled * rhat, axis=-1, keepdims=True)
            grad = (scaled - mean_one - rhat * mean_two) * inverse
            return grad, jnp.sum(upstream * rhat, axis=0), jnp.sum(upstream, axis=0)

        def column_sums(matrix):
            return jnp.sum(matrix.astype(F32), axis=0)

        kept = []
        for layer in range(layers):
            _, _, out_b, gain_one, bias_one, shrink_b, gain_two, bias_two = (
                full[layer, i] for i in range(8)
            )
            if layer:
                group = gather_seq(hidden_now.astype(BF))
            bias_row = jnp.concatenate(
                [by_column[layer, 0], jnp.zeros((width,), F32), by_column[layer, 1]]
            )
            qkv = (dot(group, qkv_all[layer]) + bias_row).astype(BF)
            attended, row_max, row_sum = attend(qkv, starts)
            summed = reduce_seq(attended, (out_all[layer], (1, 0)), rows_here)
            resid_one = hidden_now + (summed + out_b)
            rhat_one, inverse_one = norm_parts(resid_one)
            normed = rhat_one * gain_one + bias_one
            normed_group = gather_seq(normed.astype(BF))
            inner = dot(normed_group, expand_all[layer]) + hidden_bias[layer]
            cdf = 0.5 * (1.0 + lax.erf(inner * math.sqrt(0.5)))
            active = (inner * cdf).astype(BF)
            slope = cdf + inner * jnp.exp(-0.5 * inner * inner) * (1.0 / math.sqrt(2 * math.pi))
            summed = reduce_seq(active, (shrink_all[layer], (1, 0)), rows_here)
            resid_two = normed + (summed + shrink_b)
            rhat_two, inverse_two = norm_parts(resid_two)
            hidden_now = rhat_two * gain_two + bias_two
            kept.append(
                (group, qkv, attended, row_max, row_sum, rhat_one, inverse_one, normed_group,
                 active, slope, rhat_two, inverse_two)
            )
        encoded = hidden_now.astype(BF)

        local_index = match_index[0] - seq * rows_here
        picker = local_index[:, None] == jnp.arange(rows_here, dtype=jnp.int32)[None, :]
        chosen = dot(picker.astype(BF), encoded)
        query_vecs = queries[0].astype(F32)
        scores = jnp.sum(query_vecs * chosen, axis=-1)[None, :]
        for bit in seq_bits:
            scores = scores + swap(scores, bit)
        lexical = jnp.sum(
            encoded.astype(F32) * lexical_weight.astype(F32)[None, :], axis=-1
        ) + lexical_bias.astype(F32)[0]
        keep_mask = (lexical_ids >= 4).astype(F32)
        local_sums = jnp.stack(
            [
                jnp.sum(keep_mask * jax.nn.softplus(lexical)),
                jnp.sum(keep_mask * jax.nn.sigmoid(lexical)),
            ]
        )
        weighted = score_cot[0][:, None] * query_vecs
        grad_now = encoded_cot.astype(F32) + lax.dot_general(
            picker.astype(F32), weighted, (((0,), (0,)), ((), ())), precision=HIGHEST
        )

        def scatter_dp(grad):
            return lax.psum_scatter(grad, "dp", scatter_dimension=0, tiled=True)

        def scatter_dp_steps(grad):
            rest = grad
            index_unit = 1
            for bit in dp_bits:
                keep_rows = rest.reshape(-1, 2, block_rows, rest.shape[-1])
                keep, got = halve(
                    (keep_rows[:, 0], keep_rows[:, 1]), bit_of(dp, index_unit), bit
                )
                total = keep.astype(F32) + got.astype(F32)
                rest = total.astype(BF)
                index_unit *= 2
            return rest.reshape(block_rows, -1)

        def scatter_out(grad):
            if not special:
                placed = grad.reshape(pairs_here, 1, 2 * HEAD, dim)
                hot = (jnp.arange(n_seq) == seq)[None, :, None, None]
                placed = jnp.where(hot, placed, jnp.zeros_like(placed)).reshape(dim, dim)
                return lax.psum_scatter(placed, AXES, scatter_dimension=0, tiled=True)
            halves = grad.reshape(2, 2 * HEAD, dim)
            keep, got = halve((halves[0], halves[1]), bit_of(dp, 4), 4 * n_seq)
            for bit in (2, 1):
                total = (keep.astype(F32) + got.astype(F32)).astype(BF)
                keep, got = total, swap(total, bit * n_seq)
            return (keep.astype(F32) + got.astype(F32)).astype(BF)

        def unsplit(pieces, size):
            count = pieces[0].shape[1] // size
            return jnp.concatenate(
                [pieces[s][:, i * size : (i + 1) * size] for i in range(count) for s in range(n_seq)],
                axis=1,
            )

        def rows_back(scattered):
            return exchange_steps([scattered[s * part : (s + 1) * part] for s in range(n_seq)])

        def spread_columns(vector):
            hot = (jnp.arange(n_seq) == seq)[None, :, None]
            return jnp.where(hot, vector.reshape(pairs_here, 1, 2 * HEAD), 0.0).reshape(dim)

        def spread_hidden(vector):
            hot = (jnp.arange(n_seq) == seq)[None, :, None]
            return jnp.where(hot, vector.reshape(n_dp, 1, hidden_part), 0.0).reshape(hidden_dim)

        big = [None] * layers
        vectors = [None] * layers
        for layer in reversed(range(layers)):
            _, _, _, gain_one, _, _, gain_two, _ = (full[layer, i] for i in range(8))
            (group, qkv, attended, row_max, row_sum, rhat_one, inverse_one, normed_group,
             active, slope, rhat_two, inverse_two) = kept[layer]
            grad_second, fgain, fbias = norm_back(grad_now, gain_two, rhat_two, inverse_two)
            low_second = grad_second.astype(BF)
            second_group = gather_seq(low_second)
            low_inner = (dot(second_group, shrink_all[layer], 1, 1) * slope).astype(BF)
            summed = reduce_seq(low_inner, (expand_all[layer], (1, 1)), rows_here)
            shrink_grad = dot(active, second_group, 0, 0).astype(BF)
            expand_grad = dot(normed_group, low_inner, 0, 0).astype(BF)
            if layer or not special:
                shrink_rows, expand_rows = scatter_dp(shrink_grad), scatter_dp(expand_grad)
            else:
                shrink_rows, expand_rows = scatter_dp_steps(shrink_grad), scatter_dp_steps(expand_grad)
            grad_normed = grad_second + summed
            grad_first, ngain, nbias = norm_back(grad_normed, gain_one, rhat_one, inverse_one)
            low_first = grad_first.astype(BF)
            first_group = gather_seq(low_first)
            low_attn = dot(first_group, out_all[layer], 1, 1).astype(BF)
            out_rows = scatter_out(dot(attended, first_group, 0, 0).astype(BF))
            grad_qkv = attend_back(qkv, starts, row_max, row_sum, low_attn)
            qkv_rows = scatter_dp_steps(dot(group, grad_qkv, 0, 0).astype(BF))
            summed = reduce_seq(grad_qkv, (qkv_all[layer], (1, 1)), rows_here)
            grad_now = grad_first + summed
            qkv_sums = column_sums(grad_qkv)
            vectors[layer] = [
                spread_columns(qkv_sums[:width]),
                spread_columns(qkv_sums[2 * width :]),
                column_sums(low_first),
                ngain,
                nbias,
                column_sums(low_second),
                fgain,
                fbias,
                spread_hidden(column_sums(low_inner)),
            ]
            big[layer] = (qkv_rows, shrink_rows, expand_rows, out_rows)

        tokens_grad = grad_now.astype(BF)

        table = jnp.concatenate(
            [
                v.reshape(n_dev, -1)
                for layer in range(layers)
                for v in vectors[layer]
            ]
            + [jnp.broadcast_to(local_sums[None, :], (n_dev, 2))],
            axis=1,
        )
        for bit in seq_bits + dp_bits:
            pairs = table.reshape(-1, 2, table.shape[-1])
            keep, got = halve((pairs[:, 0], pairs[:, 1]), bit_of(flat, bit), bit)
            table = keep + got
        table = table.reshape(-1)
        lexical_stats = table[-2:] / (rows_here * n_dev)
        table = table[:-2].reshape(layers, 8 * part + hidden_part)

        def vector_out(index):
            return table[:, index * part : (index + 1) * part]

        layer_outs = []
        for layer in range(layers):
            qkv_rows, shrink_rows, expand_rows, out_rows = big[layer]
            parts = [expand_rows] + ([out_rows] if special else [])
            if layer:
                parts.append(qkv_rows)
            got = rows_back(jnp.concatenate(parts, axis=1))
            expand_out = unsplit(by_origin([g[:, :own_hidden] for g in got]), hidden_part)
            at = own_hidden
            if special:
                source = seq ^ lax.rem(dp, n_seq)
                out_out = got[0][:, at : at + dim]
                for step in range(1, n_seq):
                    out_out = jnp.where(source == step, got[step][:, at : at + dim], out_out)
                at += dim
            else:
                out_out = out_rows
            if layer:
                qkv_out = by_origin([g[:, at:] for g in got])
            else:
                qkv_out = by_origin(rows_back(qkv_rows))
            layer_outs.append(
                [
                    unsplit([b[:, i * width : (i + 1) * width] for b in qkv_out], 2 * HEAD)
                    for i in range(3)
                ]
                + [out_out, expand_out, shrink_rows]
            )
        big_out = [jnp.stack([lo[i].astype(F32) for lo in layer_outs]) for i in range(6)]
        return (
            encoded, scores, lexical_stats, tokens_grad,
            big_out[0], vector_out(0), big_out[1], big_out[2], vector_out(1),
            big_out[3], vector_out(2), vector_out(3), vector_out(4),
            big_out[4], table[:, 8 * part :], big_out[5], vector_out(5),
            vector_out(6), vector_out(7),
        )

    rows = P(AXES, None)
    weight = P(None, AXES, None)
    vector = P(None, AXES)
    placed = (
        rows, P("dp", None), P(AXES), P("dp", None, None), P("dp", None),
        weight, vector, weight, weight, vector, weight, vector, vector, vector,
        weight, vector, weight, vector, vector, vector, P(), P(), P("dp", None), rows,
    )
    results = (
        rows, P("dp", None), P(), rows,
        weight, vector, weight, weight, vector, weight, vector, vector, vector,
        weight, vector, weight, vector, vector, vector,
    )
    return jax.shard_map(local, mesh=mesh, in_specs=placed, out_specs=results, check_vma=False)
```

time: 3230 us -> 660 us (0.20)
  waiting for transfers between devices: 2600 us -> 288 us
  matrix products: 323 us -> 84.4 us
  blocking collectives: 128 us -> 0 us
  starting transfers between devices: 1.61 us -> 104 us
  local copies, waits for them, and re-layouts: 105 us -> 46.4 us
  Pallas kernels: 0 us -> 54.4 us
    reduce_scatter x6 -> x2, waiting for transfers between devices: 1010 us -> 0.01 us  [scatter_dp(): return lax.psum_scatter(grad, 'dp', scatter_dimension=0, tiled=True)]
    unnamed x43 -> x4, waiting for transfers between devices: 892 us -> 0.07 us
    all_gather x16 -> x2, waiting for transfers between devices: 609 us -> 0.19 us  [the longest x1 0.18 us: local(): shrink_all.append(lax.all_gather(rest, 'dp', axis=0, tiled=True))]
    ppermute x0 -> x125, waiting for transfers between devices: none -> 288 us  [swap(): return lax.ppermute(array, AXES, [(p, p ^ bit) for p in range(n_dev)])]
    dot_general x148 -> x34, matrix products: 315 us -> 84.4 us  [the longest x33 83.4 us: dot(): lax.dot_general(left, right, (((left_dim,), (right_dim,)), ((), ())), pre...]
    ppermute x0 -> x125, starting transfers between devices: none -> 103 us  [swap(): return lax.ppermute(array, AXES, [(p, p ^ bit) for p in range(n_dev)])]
    psum x1 -> x0, waiting for transfers between devices: 86.3 us -> none  [local(): lexical_stats = lax.psum(local_sums, ('dp', 'seq')) / total_tokens]
    all_gather x2 -> x0, blocking collectives: 78.8 us -> none  [fetch_layer(): lax.all_gather(expand_bias[layer_index], ('dp', 'seq'), axis=0, tiled=True)]
  transfers between devices with their start and end apart: 33 -> 129, of which waited for: 31 -> 53; matrix products, arithmetic and copies ran while one was open for 8% -> 24% of each run, Pallas kernels for 0% -> 8%
where the time goes in v1:
time: 660 us; the launch traced here: 649 us
  waiting for transfers between devices  288 us (44%)
  starting transfers between devices  104 us (16%)
  matrix products  84.4 us (13%)
  Pallas kernels  54.4 us (8%)
  other arithmetic  53.3 us (8%)
  local copies, waits for them, and re-layouts  46.4 us (7%)
  between operations  18.2 us (3%)
    ppermute x125, waiting for transfers between devices, swap(): return lax.ppermute(array, AXES, [(p, p ^ bit) for p in range(n_dev)])  288 us
    ppermute x125, starting transfers between devices, swap(): return lax.ppermute(array, AXES, [(p, p ^ bit) for p in range(n_dev)])  103 us
    dot_general x33, matrix products, dot(): lax.dot_general(left, right, (((left_dim,), (right_dim,)), ((), ())), pre...  83.4 us
    pallas_call x2, Pallas kernels, attend_back(): pl.pallas_call(functools.partial(attend_back_kernel, 256), out_shape=jax....  22.3 us
    pallas_call x2, Pallas kernels, attend(): pl.pallas_call(functools.partial(attend_kernel, 256), out_shape=(jax.Shap...  20.6 us
    unnamed x412, local copies, waits for them, and re-layouts  18.4 us
  transfers between devices with their start and end apart: 129, of which 53 were waited for; matrix products, arithmetic and copies ran while one was open for 24% of the time, Pallas kernels for 8%

profile of v1, /device:TPU:0, one launch (start us, length us, event | category | flops | bytes accessed | tf_op | source)
XLA Modules:
  0.0 648.8 jit_solution(8594683775109077371)
XLA Ops:
  31.1 4.0 collective-permute-done.26
  57.1 3.3 collective-permute-done.10.refs_5_
  60.5 4.7 collective-permute-done.11.refs_6_
  65.2 4.0 collective-permute-done.12.refs_7_
  77.6 3.9 add_convert_fusion.1.qkv_ref
  81.5 10.4 %shard_map.376 = (bf16[768,256]{1,0:T(8,128)(2,1)}, f32[4,768]{1,0:T(4,128)}, f32[4,768]{1,0:T(4,128)}) custom-call(bf16[768,768]{1,0:T(8,128)(2,1)} %add_convert_fusion.1.qkv_ref, s32[768,1]{1,0:T(8,128)} %broadcast_in_dim.162.col_ref, s32[1,768]{1,0:T(1,128)} %broadcast_in_dim.141.row_ref), custom_call_target="tpu_custom_call" | custom-call | flops 603979776 | bytes 1572864 | tf_op jit(solution)/shard_map/pallas_call | solution.py:108
  101.9 7.1 %collective-permute-done.28.refs_1_ = bf16[128,1024]{1,0:T(8,128)(2,1)S(1)} collective-permute-done((bf16[128,1024]{1,0:T(8,128)(2,1)S(1)}, bf16[128,1024]{1,0:T(8,128)(2,1)S(1)}, u32[]{:S(2)}, u32[]{:S(2)}) %collective-permute-start.28) | collective-permute-done | bytes 262176 | tf_op jit(solution)/shard_map/ppermute | solution.py:185
  109.7 4.1 collective-permute-start.30
  116.9 8.3 %collective-permute-done.30.refs_3_ = bf16[128,1024]{1,0:T(8,128)(2,1)} collective-permute-done((bf16[128,1024]{1,0:T(8,128)(2,1)S(1)}, bf16[128,1024]{1,0:T(8,128)(2,1)}, u32[]{:S(2)}, u32[]{:S(2)}) %collective-permute-start.30) | collective-permute-done | bytes 262176 | tf_op jit(solution)/shard_map/ppermute | solution.py:185
  130.4 5.1 collective-permute-done.36.refs_2_
  136.9 8.0 %collective-permute-done.48.refs_1_ = bf16[128,768]{1,0:T(8,128)(2,1)S(1)} collective-permute-done((bf16[128,768]{1,0:T(8,128)(2,1)S(1)}, bf16[128,768]{1,0:T(8,128)(2,1)S(1)}, u32[]{:S(2)}, u32[]{:S(2)}) %collective-permute-start.48) | collective-permute-done | bytes 196640 | tf_op jit(solution)/shard_map/ppermute | solution.py:185
  154.3 5.0 collective-permute-done.41.refs_7_
  163.0 5.0 multiply_convert_fusion.1
  173.7 10.4 %collective-permute-done.55 = bf16[128,1024]{1,0:T(8,128)(2,1)S(1)} collective-permute-done((bf16[128,1024]{1,0:T(8,128)(2,1)S(1)}, bf16[128,1024]{1,0:T(8,128)(2,1)S(1)}, u32[]{:S(2)}, u32[]{:S(2)}) %collective-permute-start.55) | collective-permute-done | bytes 262176 | tf_op jit(solution)/shard_map/ppermute | solution.py:185
  184.2 5.4 collective-permute-start.56
  190.7 13.7 %collective-permute-done.56 = bf16[128,1024]{1,0:T(8,128)(2,1)S(1)} collective-permute-done((bf16[128,1024]{1,0:T(8,128)(2,1)S(1)}, bf16[128,1024]{1,0:T(8,128)(2,1)S(1)}, u32[]{:S(2)}, u32[]{:S(2)}) %collective-permute-start.56) | collective-permute-done | bytes 262176 | tf_op jit(solution)/shard_map/ppermute | solution.py:185
  204.8 4.6 collective-permute-start.50
  220.3 6.7 %collective-permute-done.53.refs_6_ = bf16[128,768]{1,0:T(8,128)(2,1)S(1)} collective-permute-done((bf16[128,768]{1,0:T(8,128)(2,1)}, bf16[128,768]{1,0:T(8,128)(2,1)S(1)}, u32[]{:S(2)}, u32[]{:S(2)}) %collective-permute-start.53) | collective-permute-done | bytes 196640 | tf_op jit(solution)/shard_map/ppermute | solution.py:185
  227.0 3.3 collective-permute-done.54.refs_7_
  233.7 4.2 add_convert_fusion.qkv_ref
  237.9 10.2 %shard_map.380 = (bf16[768,256]{1,0:T(8,128)(2,1)}, f32[4,768]{1,0:T(4,128)}, f32[4,768]{1,0:T(4,128)}) custom-call(bf16[768,768]{1,0:T(8,128)(2,1)} %add_convert_fusion.qkv_ref, s32[768,1]{1,0:T(8,128)} %broadcast_in_dim.162.col_ref, s32[1,768]{1,0:T(1,128)} %broadcast_in_dim.141.row_ref), custom_call_target="tpu_custom_call" | custom-call | flops 603979776 | bytes 1572864 | tf_op jit(solution)/shard_map/pallas_call | solution.py:108
  251.9 10.8 %collective-permute-done.60 = bf16[192,1024]{1,0:T(8,128)(2,1)S(1)} collective-permute-done((bf16[192,1024]{1,0:T(8,128)(2,1)S(1)}, bf16[192,1024]{1,0:T(8,128)(2,1)S(1)}, u32[]{:S(2)}, u32[]{:S(2)}) %collective-permute-start.60) | collective-permute-done | bytes 393248 | tf_op jit(solution)/shard_map/ppermute | solution.py:185
  264.0 10.0 %collective-permute-done.61 = bf16[192,1024]{1,0:T(8,128)(2,1)S(1)} collective-permute-done((bf16[192,1024]{1,0:T(8,128)(2,1)S(1)}, bf16[192,1024]{1,0:T(8,128)(2,1)S(1)}, u32[]{:S(2)}, u32[]{:S(2)}) %collective-permute-start.61) | collective-permute-done | bytes 393248 | tf_op jit(solution)/shard_map/ppermute | solution.py:185
  275.9 6.0 multiply_convert_fusion
  290.2 10.7 %collective-permute-done.66 = bf16[192,1024]{1,0:T(8,128)(2,1)S(1)} collective-permute-done((bf16[192,1024]{1,0:T(8,128)(2,1)}, bf16[192,1024]{1,0:T(8,128)(2,1)S(1)}, u32[]{:S(2)}, u32[]{:S(2)}) %collective-permute-start.66) | collective-permute-done | bytes 393248 | tf_op jit(solution)/shard_map/ppermute | solution.py:185
  305.6 9.7 %collective-permute-done.69 = bf16[192,1024]{1,0:T(8,128)(2,1)S(1)} collective-permute-done((bf16[192,1024]{1,0:T(8,128)(2,1)S(1)}, bf16[192,1024]{1,0:T(8,128)(2,1)S(1)}, u32[]{:S(2)}, u32[]{:S(2)}) %collective-permute-start.69) | collective-permute-done | bytes 393248 | tf_op jit(solution)/shard_map/ppermute | solution.py:185
  317.1 4.4 convert_reduce_fusion
  322.8 4.3 convolution_convert_fusion.3
  338.3 8.2 %collective-permute-done.74 = bf16[192,1024]{1,0:T(8,128)(2,1)} collective-permute-done((bf16[192,1024]{1,0:T(8,128)(2,1)}, bf16[192,1024]{1,0:T(8,128)(2,1)}, u32[]{:S(2)}, u32[]{:S(2)}) %collective-permute-start.74) | collective-permute-done | bytes 393248 | tf_op jit(solution)/shard_map/ppermute | solution.py:185
  355.4 4.6 collective-permute-done.68
  361.1 5.1 convolution_convert_fusion
  370.9 11.3 %shard_map.381 = bf16[768,768]{1,0:T(8,128)(2,1)} custom-call(bf16[768,768]{1,0:T(8,128)(2,1)} %add_convert_fusion.qkv_ref, s32[768,1]{1,0:T(8,128)} %broadcast_in_dim.162.col_ref, s32[1,768]{1,0:T(1,128)} %broadcast_in_dim.141.row_ref, f32[4,768]{1,0:T(4,128)} %get-tuple-element.45.max_ref, f32[4,768]{1,0:T(4,128)} %get-tuple-element.46.sum_ref, ...), custom_call_target="tpu_custom_call" | custom-call | flops 1509949440 | bytes 2752512 | tf_op jit(solution)/shard_map/pallas_call | solution.py:129
  391.7 10.5 %collective-permute-done.104 = bf16[128,1024]{1,0:T(8,128)(2,1)S(1)} collective-permute-done((bf16[128,1024]{1,0:T(8,128)(2,1)S(1)}, bf16[128,1024]{1,0:T(8,128)(2,1)S(1)}, u32[]{:S(2)}, u32[]{:S(2)}) %collective-permute-start.104) | collective-permute-done | bytes 262176 | tf_op jit(solution)/shard_map/ppermute | solution.py:185
  404.3 8.9 %collective-permute-done.105 = bf16[128,1024]{1,0:T(8,128)(2,1)S(1)} collective-permute-done((bf16[128,1024]{1,0:T(8,128)(2,1)S(1)}, bf16[128,1024]{1,0:T(8,128)(2,1)S(1)}, u32[]{:S(2)}, u32[]{:S(2)}) %collective-permute-start.105) | collective-permute-done | bytes 262176 | tf_op jit(solution)/shard_map/ppermute | solution.py:185
  421.0 14.0 %collective-permute-done.108 = bf16[2,128,768]{2,1,0:T(8,128)(2,1)S(1)} collective-permute-done((bf16[2,128,768]{2,1,0:T(8,128)(2,1)S(1)}, bf16[2,128,768]{2,1,0:T(8,128)(2,1)S(1)}, u32[]{:S(2)}, u32[]{:S(2)}) %collective-permute-start.108) | collective-permute-done | bytes 393248 | tf_op jit(solution)/shard_map/ppermute | solution.py:185
  436.4 10.0 %collective-permute-done.109 = bf16[1,128,768]{2,1,0:T(8,128)(2,1)S(1)} collective-permute-done((bf16[1,128,768]{2,1,0:T(8,128)(2,1)S(1)}, bf16[1,128,768]{2,1,0:T(8,128)(2,1)S(1)}, u32[]{:S(2)}, u32[]{:S(2)}) %collective-permute-start.109) | collective-permute-done | bytes 196640 | tf_op jit(solution)/shard_map/ppermute | solution.py:185
  446.5 3.3 convolution_convert_fusion.1
  453.6 5.0 convert_reduce_fusion.1
  467.9 7.7 %collective-permute-done.86 = bf16[192,1024]{1,0:T(8,128)(2,1)S(1)} collective-permute-done((bf16[192,1024]{1,0:T(8,128)(2,1)S(1)}, bf16[192,1024]{1,0:T(8,128)(2,1)S(1)}, u32[]{:S(2)}, u32[]{:S(2)}) %collective-permute-start.86) | collective-permute-done | bytes 393248 | tf_op jit(solution)/shard_map/ppermute | solution.py:185
  485.8 16.4 %collective-permute-done.113 = bf16[4,128,1024]{2,1,0:T(8,128)(2,1)} collective-permute-done((bf16[4,128,1024]{2,1,0:T(8,128)(2,1)}, bf16[4,128,1024]{2,1,0:T(8,128)(2,1)}, u32[]{:S(2)}, u32[]{:S(2)}) %collective-permute-start.113) | collective-permute-done | bytes 1048608 | tf_op jit(solution)/shard_map/ppermute | solution.py:185
  507.7 11.3 %collective-permute-done.123 = bf16[2,128,1024]{2,1,0:T(8,128)(2,1)S(1)} collective-permute-done((bf16[2,128,1024]{2,1,0:T(8,128)(2,1)S(1)}, bf16[2,128,1024]{2,1,0:T(8,128)(2,1)S(1)}, u32[]{:S(2)}, u32[]{:S(2)}) %collective-permute-start.123) | collective-permute-done | bytes 524320 | tf_op jit(solution)/shard_map/ppermute | solution.py:185
  520.4 15.1 %collective-permute-done.114 = bf16[2,128,1024]{2,1,0:T(8,128)(2,1)S(1)} collective-permute-done((bf16[2,128,1024]{2,1,0:T(8,128)(2,1)S(1)}, bf16[2,128,1024]{2,1,0:T(8,128)(2,1)S(1)}, u32[]{:S(2)}, u32[]{:S(2)}) %collective-permute-start.114) | collective-permute-done | bytes 524320 | tf_op jit(solution)/shard_map/ppermute | solution.py:185
  540.0 11.0 %shard_map.382 = bf16[768,768]{1,0:T(8,128)(2,1)} custom-call(bf16[768,768]{1,0:T(8,128)(2,1)} %add_convert_fusion.1.qkv_ref, s32[768,1]{1,0:T(8,128)} %broadcast_in_dim.162.col_ref, s32[1,768]{1,0:T(1,128)} %broadcast_in_dim.141.row_ref, f32[4,768]{1,0:T(4,128)} %get-tuple-element.43.max_ref, f32[4,768]{1,0:T(4,128)} %get-tuple-element.44.sum_ref, ...), custom_call_target="tpu_custom_call" | custom-call | flops 1509949440 | bytes 2752512 | tf_op jit(solution)/shard_map/pallas_call | solution.py:129
  564.4 3.3 convolution_convert_fusion.6
  595.6 3.7 collective-permute-done.117
  602.6 5.2 collective-permute-done.118
  616.9 6.0 collective-permute-done.99
  625.5 8.7 %collective-permute-done.100 = bf16[1,128,768]{2,1,0:T(8,128)(2,1)S(1)} collective-permute-done((bf16[1,128,768]{2,1,0:T(8,128)(2,1)S(1)}, bf16[1,128,768]{2,1,0:T(8,128)(2,1)S(1)}, u32[]{:S(2)}, u32[]{:S(2)}) %collective-permute-start.100) | collective-permute-done | bytes 196640 | tf_op jit(solution)/shard_map/ppermute | solution.py:185
  (902 shorter events, 274.0 us)
Async XLA Ops:
  7.3 266.7 %all-gather.3.cloned.1.call-start = ((), (), s32[]{:S(2)}) async-start(), calls=%async_computation.2 | async-start | bytes 2359296 | tf_op jit(solution)/shard_map/all_gather | solution.py:348
  7.3 18.9 %collective-permute-start.13 = (bf16[2,32,1024]{2,1,0:T(8,128)(2,1)}, bf16[2,32,1024]{2,1,0:T(8,128)(2,1)S(1)}, u32[]{:S(2)}, u32[]{:S(2)}) collective-permute-start(bf16[2,32,1024]{2,1,0:T(8,128)(2,1)} %param.34), channel_id=1, source_target_pairs={{0,2},{1,3},{2,0},{3,1},{4,6},{5,7},{6,4},{7,5},{8,10},{9,11},{10,... | collective-permute-start | bytes 393224 | tf_op jit(solution)/shard_map/ppermute | solution.py:185
  10.3 27.5 %collective-permute-start.15 = (bf16[2,32,1024]{2,1,0:T(8,128)(2,1)}, bf16[2,32,1024]{2,1,0:T(8,128)(2,1)}, u32[]{:S(2)}, u32[]{:S(2)}) collective-permute-start(bf16[2,32,1024]{2,1,0:T(8,128)(2,1)} %param.34), channel_id=1, source_target_pairs={{0,1},{1,0},{2,3},{3,2},{4,5},{5,4},{6,7},{7,6},{8,9},{9,8},{10,11... | collective-permute-start | bytes 393224 | tf_op jit(solution)/shard_map/ppermute | solution.py:185
  26.2 21.8 %collective-permute-start = (bf16[192,1024]{1,0:T(8,128)(2,1)S(1)}, bf16[192,1024]{1,0:T(8,128)(2,1)}, u32[]{:S(2)}, u32[]{:S(2)}) collective-permute-start(bf16[192,1024]{1,0:T(8,128)(2,1)S(1)} %copy-done.16), channel_id=1, source_target_pairs={{0,2},{1,3},{2,0},{3,1},{4,6},{5,7},{6,4},{7,5},{8,10},{9,11},{10,... | collective-permute-start | bytes 1179656 | tf_op jit(solution)/shard_map/ppermute | solution.py:185
  29.5 21.3 %collective-permute-start.1 = (bf16[192,1024]{1,0:T(8,128)(2,1)S(1)}, bf16[192,1024]{1,0:T(8,128)(2,1)S(1)}, u32[]{:S(2)}, u32[]{:S(2)}) collective-permute-start(bf16[192,1024]{1,0:T(8,128)(2,1)S(1)} %copy-done.16), channel_id=1, source_target_pairs={{0,1},{1,0},{2,3},{3,2},{4,5},{5,4},{6,7},{7,6},{8,9},{9,8},{10,11... | collective-permute-start | bytes 1179656 | tf_op jit(solution)/shard_map/ppermute | solution.py:185
  54.0 21.9 %collective-permute-start.2 = (bf16[192,1024]{1,0:T(8,128)(2,1)}, bf16[192,1024]{1,0:T(8,128)(2,1)}, u32[]{:S(2)}, u32[]{:S(2)}) collective-permute-start(bf16[192,1024]{1,0:T(8,128)(2,1)} %collective-permute-done), channel_id=1, source_target_pairs={{0,1},{1,0},{2,3},{3,2},{4,5},{5,4},{6,7},{7,6},{8,9},{9,8},{10,11... | collective-permute-start | bytes 1179656 | tf_op jit(solution)/shard_map/ppermute | solution.py:185
  55.7 19.7 %collective-permute-start.17 = (bf16[128,1024]{1,0:T(8,128)(2,1)S(1)}, bf16[128,1024]{1,0:T(8,128)(2,1)}, u32[]{:S(2)}, u32[]{:S(2)}) collective-permute-start(bf16[128,1024]{1,0:T(8,128)(2,1)S(1)} %broadcast_select_fusion.3), channel_id=1, source_target_pairs={{0,8},{1,9},{2,10},{3,11},{4,12},{5,13},{6,14},{7,15},{8,0},{9,1},... | collective-permute-start | bytes 786440 | tf_op jit(solution)/shard_map/ppermute | solution.py:185
  75.4 16.4 %collective-permute-start.18 = (bf16[128,1024]{1,0:T(8,128)(2,1)S(1)}, bf16[128,1024]{1,0:T(8,128)(2,1)S(1)}, u32[]{:S(2)}, u32[]{:S(2)}) collective-permute-start(bf16[128,1024]{1,0:T(8,128)(2,1)S(1)} %broadcast_select_fusion.5), channel_id=1, source_target_pairs={{0,16},{1,17},{2,18},{3,19},{4,20},{5,21},{6,22},{7,23},{8,24},{9,... | collective-permute-start | bytes 786440 | tf_op jit(solution)/shard_map/ppermute | solution.py:185
  99.1 16.3 %collective-permute-start.21 = (bf16[192,1024]{1,0:T(8,128)(2,1)S(1)}, bf16[192,1024]{1,0:T(8,128)(2,1)S(1)}, u32[]{:S(2)}, u32[]{:S(2)}) collective-permute-start(bf16[192,1024]{1,0:T(8,128)(2,1)S(1)} %fusion.56), channel_id=1, source_target_pairs={{0,2},{1,3},{2,0},{3,1},{4,6},{5,7},{6,4},{7,5},{8,10},{9,11},{10,... | collective-permute-start | bytes 1179656 | tf_op jit(solution)/shard_map/ppermute | solution.py:185
  100.4 16.4 %collective-permute-start.31 = (bf16[128,1024]{1,0:T(8,128)(2,1)S(1)}, bf16[128,1024]{1,0:T(8,128)(2,1)S(1)}, u32[]{:S(2)}, u32[]{:S(2)}) collective-permute-start(bf16[128,1024]{1,0:T(8,128)(2,1)S(1)} %slice.1900.refs_0_), channel_id=1, source_target_pairs={{0,4},{1,5},{2,6},{3,7},{4,0},{5,1},{6,2},{7,3},{8,12},{9,13},{10,... | collective-permute-start | bytes 786440 | tf_op jit(solution)/shard_map/ppermute | solution.py:185
  109.0 21.3 %collective-permute-start.35 = (bf16[128,1024]{1,0:T(8,128)(2,1)S(1)}, bf16[128,1024]{1,0:T(8,128)(2,1)S(1)}, u32[]{:S(2)}, u32[]{:S(2)}) collective-permute-start(bf16[128,1024]{1,0:T(8,128)(2,1)S(1)} %get-tuple-element.37.refs_0_), channel_id=1, source_target_pairs={{0,16},{1,17},{2,18},{3,19},{4,20},{5,21},{6,22},{7,23},{8,24},{9,... | collective-permute-start | bytes 786440 | tf_op jit(solution)/shard_map/ppermute | solution.py:185
  109.7 15.5 %collective-permute-start.30 = (bf16[128,1024]{1,0:T(8,128)(2,1)S(1)}, bf16[128,1024]{1,0:T(8,128)(2,1)}, u32[]{:S(2)}, u32[]{:S(2)}) collective-permute-start(bf16[128,1024]{1,0:T(8,128)(2,1)S(1)} %collective-permute-done.28.refs_1_), channel_id=1, source_target_pairs={{0,8},{1,9},{2,10},{3,11},{4,12},{5,13},{6,14},{7,15},{8,0},{9,1},... | collective-permute-start | bytes 786440 | tf_op jit(solution)/shard_map/ppermute | solution.py:185
  116.8 18.9 %collective-permute-start.22 = (bf16[192,1024]{1,0:T(8,128)(2,1)S(1)}, bf16[192,1024]{1,0:T(8,128)(2,1)}, u32[]{:S(2)}, u32[]{:S(2)}) collective-permute-start(bf16[192,1024]{1,0:T(8,128)(2,1)S(1)} %fusion.62), channel_id=1, source_target_pairs={{0,2},{1,3},{2,0},{3,1},{4,6},{5,7},{6,4},{7,5},{8,10},{9,11},{10,... | collective-permute-start | bytes 1179656 | tf_op jit(solution)/shard_map/ppermute | solution.py:185
  128.8 17.8 %collective-permute-start.34 = (bf16[128,1024]{1,0:T(8,128)(2,1)}, bf16[128,1024]{1,0:T(8,128)(2,1)}, u32[]{:S(2)}, u32[]{:S(2)}) collective-permute-start(bf16[128,1024]{1,0:T(8,128)(2,1)} %collective-permute-done.30.refs_3_), channel_id=1, source_target_pairs={{0,4},{1,5},{2,6},{3,7},{4,0},{5,1},{6,2},{7,3},{8,12},{9,13},{10,... | collective-permute-start | bytes 786440 | tf_op jit(solution)/shard_map/ppermute | solution.py:185
  130.3 16.6 %collective-permute-start.37 = (bf16[128,1024]{1,0:T(8,128)(2,1)S(1)}, bf16[128,1024]{1,0:T(8,128)(2,1)}, u32[]{:S(2)}, u32[]{:S(2)}) collective-permute-start(bf16[128,1024]{1,0:T(8,128)(2,1)S(1)} %collective-permute-done.35.refs_1_), channel_id=1, source_target_pairs={{0,8},{1,9},{2,10},{3,11},{4,12},{5,13},{6,14},{7,15},{8,0},{9,1},... | collective-permute-start | bytes 786440 | tf_op jit(solution)/shard_map/ppermute | solution.py:185
  135.6 27.4 %collective-permute-start.23 = (bf16[192,1024]{1,0:T(8,128)(2,1)S(1)}, bf16[192,1024]{1,0:T(8,128)(2,1)}, u32[]{:S(2)}, u32[]{:S(2)}) collective-permute-start(bf16[192,1024]{1,0:T(8,128)(2,1)S(1)} %fusion.62), channel_id=1, source_target_pairs={{0,1},{1,0},{2,3},{3,2},{4,5},{5,4},{6,7},{7,6},{8,9},{9,8},{10,11... | collective-permute-start | bytes 1179656 | tf_op jit(solution)/shard_map/ppermute | solution.py:185
  135.7 27.3 %collective-permute-start.24 = (bf16[192,1024]{1,0:T(8,128)(2,1)}, bf16[192,1024]{1,0:T(8,128)(2,1)}, u32[]{:S(2)}, u32[]{:S(2)}) collective-permute-start(bf16[192,1024]{1,0:T(8,128)(2,1)} %collective-permute-done.22), channel_id=1, source_target_pairs={{0,1},{1,0},{2,3},{3,2},{4,5},{5,4},{6,7},{7,6},{8,9},{9,8},{10,11... | collective-permute-start | bytes 1179656 | tf_op jit(solution)/shard_map/ppermute | solution.py:185
  148.6 133.4 %all-gather.5.cloned.1.call-start = ((), (), s32[]{:S(2)}) async-start(), calls=%async_computation.3 | async-start | bytes 2359296 | tf_op jit(solution)/shard_map/all_gather | solution.py:350
  172.5 17.1 %collective-permute-start.42 = (bf16[192,1024]{1,0:T(8,128)(2,1)S(1)}, bf16[192,1024]{1,0:T(8,128)(2,1)S(1)}, u32[]{:S(2)}, u32[]{:S(2)}) collective-permute-start(bf16[192,1024]{1,0:T(8,128)(2,1)S(1)} %get-tuple-element.118), channel_id=1, source_target_pairs={{0,1},{1,0},{2,3},{3,2},{4,5},{5,4},{6,7},{7,6},{8,9},{9,8},{10,11... | collective-permute-start | bytes 1179656 | tf_op jit(solution)/shard_map/ppermute | solution.py:185
  173.6 15.9 %collective-permute-start.44 = (bf16[192,1024]{1,0:T(8,128)(2,1)S(1)}, bf16[192,1024]{1,0:T(8,128)(2,1)S(1)}, u32[]{:S(2)}, u32[]{:S(2)}) collective-permute-start(bf16[192,1024]{1,0:T(8,128)(2,1)S(1)} %fusion.49), channel_id=1, source_target_pairs={{0,2},{1,3},{2,0},{3,1},{4,6},{5,7},{6,4},{7,5},{8,10},{9,11},{10,... | collective-permute-start | bytes 1179656 | tf_op jit(solution)/shard_map/ppermute | solution.py:185
  184.2 20.3 %collective-permute-start.56 = (bf16[128,1024]{1,0:T(8,128)(2,1)S(1)}, bf16[128,1024]{1,0:T(8,128)(2,1)S(1)}, u32[]{:S(2)}, u32[]{:S(2)}) collective-permute-start(bf16[128,1024]{1,0:T(8,128)(2,1)S(1)} %broadcast_select_fusion.2), channel_id=1, source_target_pairs={{0,8},{1,9},{2,10},{3,11},{4,12},{5,13},{6,14},{7,15},{8,0},{9,1},... | collective-permute-start | bytes 786440 | tf_op jit(solution)/shard_map/ppermute | solution.py:185
  190.6 20.6 %collective-permute-start.45 = (bf16[192,1024]{1,0:T(8,128)(2,1)S(1)}, bf16[192,1024]{1,0:T(8,128)(2,1)}, u32[]{:S(2)}, u32[]{:S(2)}) collective-permute-start(bf16[192,1024]{1,0:T(8,128)(2,1)S(1)} %fusion.63), channel_id=1, source_target_pairs={{0,2},{1,3},{2,0},{3,1},{4,6},{5,7},{6,4},{7,5},{8,10},{9,11},{10,... | collective-permute-start | bytes 1179656 | tf_op jit(solution)/shard_map/ppermute | solution.py:185
  190.6 20.5 %collective-permute-start.49 = (bf16[128,768]{1,0:T(8,128)(2,1)S(1)}, bf16[128,768]{1,0:T(8,128)(2,1)}, u32[]{:S(2)}, u32[]{:S(2)}) collective-permute-start(bf16[128,768]{1,0:T(8,128)(2,1)S(1)} %pad_maximum_fusion.28.refs_0_), channel_id=1, source_target_pairs={{0,8},{1,9},{2,10},{3,11},{4,12},{5,13},{6,14},{7,15},{8,0},{9,1},... | collective-permute-start | bytes 589832 | tf_op jit(solution)/shard_map/ppermute | solution.py:185
  211.1 22.6 %collective-permute-start.46 = (bf16[192,1024]{1,0:T(8,128)(2,1)S(1)}, bf16[192,1024]{1,0:T(8,128)(2,1)}, u32[]{:S(2)}, u32[]{:S(2)}) collective-permute-start(bf16[192,1024]{1,0:T(8,128)(2,1)S(1)} %fusion.63), channel_id=1, source_target_pairs={{0,1},{1,0},{2,3},{3,2},{4,5},{5,4},{6,7},{7,6},{8,9},{9,8},{10,11... | collective-permute-start | bytes 1179656 | tf_op jit(solution)/shard_map/ppermute | solution.py:185
  211.2 22.5 %collective-permute-start.47 = (bf16[192,1024]{1,0:T(8,128)(2,1)}, bf16[192,1024]{1,0:T(8,128)(2,1)}, u32[]{:S(2)}, u32[]{:S(2)}) collective-permute-start(bf16[192,1024]{1,0:T(8,128)(2,1)} %collective-permute-done.45), channel_id=1, source_target_pairs={{0,1},{1,0},{2,3},{3,2},{4,5},{5,4},{6,7},{7,6},{8,9},{9,8},{10,11... | collective-permute-start | bytes 1179656 | tf_op jit(solution)/shard_map/ppermute | solution.py:185
  211.7 268.9 %reduce-scatter.3.cloned.1.call-start = ((), (), s32[]{:S(2)}) async-start(), calls=%async_computation.4 | async-start | bytes 2359296 | tf_op jit(solution)/shard_map/reduce_scatter | solution.py:438
  327.0 266.5 %reduce-scatter.5.cloned.1.call-start = ((), (), s32[]{:S(2)}) async-start(), calls=%async_computation.5 | async-start | bytes 2359296 | tf_op jit(solution)/shard_map/reduce_scatter | solution.py:438
  385.0 17.4 %collective-permute-start.79 = (bf16[192,1024]{1,0:T(8,128)(2,1)S(1)}, bf16[192,1024]{1,0:T(8,128)(2,1)S(1)}, u32[]{:S(2)}, u32[]{:S(2)}) collective-permute-start(bf16[192,1024]{1,0:T(8,128)(2,1)S(1)} %get-tuple-element.111), channel_id=1, source_target_pairs={{0,1},{1,0},{2,3},{3,2},{4,5},{5,4},{6,7},{7,6},{8,9},{9,8},{10,11... | collective-permute-start | bytes 1179656 | tf_op jit(solution)/shard_map/ppermute | solution.py:185
  385.2 28.1 %collective-permute-start.78 = (bf16[192,1024]{1,0:T(8,128)(2,1)S(1)}, bf16[192,1024]{1,0:T(8,128)(2,1)S(1)}, u32[]{:S(2)}, u32[]{:S(2)}) collective-permute-start(bf16[192,1024]{1,0:T(8,128)(2,1)S(1)} %get-tuple-element.110), channel_id=1, source_target_pairs={{0,1},{1,0},{2,3},{3,2},{4,5},{5,4},{6,7},{7,6},{8,9},{9,8},{10,11... | collective-permute-start | bytes 1179656 | tf_op jit(solution)/shard_map/ppermute | solution.py:185
  390.8 23.4 %collective-permute-start.107 = (bf16[4,128,768]{2,1,0:T(8,128)(2,1)S(1)}, bf16[4,128,768]{2,1,0:T(8,128)(2,1)S(1)}, u32[]{:S(2)}, u32[]{:S(2)}) collective-permute-start(bf16[4,128,768]{2,1,0:T(8,128)(2,1)S(1)} %select_bitcast_fusion.2), channel_id=1, source_target_pairs={{0,4},{1,5},{2,6},{3,7},{4,0},{5,1},{6,2},{7,3},{8,12},{9,13},{10,... | collective-permute-start | bytes 2359304 | tf_op jit(solution)/shard_map/ppermute | solution.py:185
  413.3 22.0 %collective-permute-start.106 = (bf16[128,1024]{1,0:T(8,128)(2,1)S(1)}, bf16[128,1024]{1,0:T(8,128)(2,1)}, u32[]{:S(2)}, u32[]{:S(2)}) collective-permute-start(bf16[128,1024]{1,0:T(8,128)(2,1)S(1)} %add_convert_fusion.7), channel_id=1, source_target_pairs={{0,4},{1,5},{2,6},{3,7},{4,0},{5,1},{6,2},{7,3},{8,12},{9,13},{10,... | collective-permute-start | bytes 786440 | tf_op jit(solution)/shard_map/ppermute | solution.py:185
  414.6 20.4 %collective-permute-start.108 = (bf16[2,128,768]{2,1,0:T(8,128)(2,1)S(1)}, bf16[2,128,768]{2,1,0:T(8,128)(2,1)S(1)}, u32[]{:S(2)}, u32[]{:S(2)}) collective-permute-start(bf16[2,128,768]{2,1,0:T(8,128)(2,1)S(1)} %select_bitcast_fusion.6), channel_id=1, source_target_pairs={{0,8},{1,9},{2,10},{3,11},{4,12},{5,13},{6,14},{7,15},{8,0},{9,1},... | collective-permute-start | bytes 1179656 | tf_op jit(solution)/shard_map/ppermute | solution.py:185
  417.7 17.7 %collective-permute-start.81 = (bf16[192,1024]{1,0:T(8,128)(2,1)}, bf16[192,1024]{1,0:T(8,128)(2,1)}, u32[]{:S(2)}, u32[]{:S(2)}) collective-permute-start(bf16[192,1024]{1,0:T(8,128)(2,1)} %get-tuple-element.82), channel_id=1, source_target_pairs={{0,2},{1,3},{2,0},{3,1},{4,6},{5,7},{6,4},{7,5},{8,10},{9,11},{10,... | collective-permute-start | bytes 1179656 | tf_op jit(solution)/shard_map/ppermute | solution.py:185
  418.9 27.6 %collective-permute-start.82 = (bf16[192,1024]{1,0:T(8,128)(2,1)}, bf16[192,1024]{1,0:T(8,128)(2,1)}, u32[]{:S(2)}, u32[]{:S(2)}) collective-permute-start(bf16[192,1024]{1,0:T(8,128)(2,1)} %get-tuple-element.82), channel_id=1, source_target_pairs={{0,1},{1,0},{2,3},{3,2},{4,5},{5,4},{6,7},{7,6},{8,9},{9,8},{10,11... | collective-permute-start | bytes 1179656 | tf_op jit(solution)/shard_map/ppermute | solution.py:185
  450.9 32.0 %collective-permute-start.122 = (bf16[4,128,1024]{2,1,0:T(8,128)(2,1)}, bf16[4,128,1024]{2,1,0:T(8,128)(2,1)}, u32[]{:S(2)}, u32[]{:S(2)}) collective-permute-start(bf16[4,128,1024]{2,1,0:T(8,128)(2,1)} %select_bitcast_fusion), channel_id=1, source_target_pairs={{0,4},{1,5},{2,6},{3,7},{4,0},{5,1},{6,2},{7,3},{8,12},{9,13},{10,... | collective-permute-start | bytes 3145736 | tf_op jit(solution)/shard_map/ppermute | solution.py:185
  467.0 35.2 %collective-permute-start.113 = (bf16[4,128,1024]{2,1,0:T(8,128)(2,1)}, bf16[4,128,1024]{2,1,0:T(8,128)(2,1)}, u32[]{:S(2)}, u32[]{:S(2)}) collective-permute-start(bf16[4,128,1024]{2,1,0:T(8,128)(2,1)} %select_bitcast_fusion.1), channel_id=1, source_target_pairs={{0,4},{1,5},{2,6},{3,7},{4,0},{5,1},{6,2},{7,3},{8,12},{9,13},{10,... | collective-permute-start | bytes 3145736 | tf_op jit(solution)/shard_map/ppermute | solution.py:185
  477.6 26.6 %collective-permute-start.87 = (bf16[192,1024]{1,0:T(8,128)(2,1)}, bf16[192,1024]{1,0:T(8,128)(2,1)S(1)}, u32[]{:S(2)}, u32[]{:S(2)}) collective-permute-start(bf16[192,1024]{1,0:T(8,128)(2,1)} %get-tuple-element.85), channel_id=1, source_target_pairs={{0,2},{1,3},{2,0},{3,1},{4,6},{5,7},{6,4},{7,5},{8,10},{9,11},{10,... | collective-permute-start | bytes 1179656 | tf_op jit(solution)/shard_map/ppermute | solution.py:185
  478.6 58.7 %collective-permute-start.88 = (bf16[192,1024]{1,0:T(8,128)(2,1)}, bf16[192,1024]{1,0:T(8,128)(2,1)}, u32[]{:S(2)}, u32[]{:S(2)}) collective-permute-start(bf16[192,1024]{1,0:T(8,128)(2,1)} %get-tuple-element.85), channel_id=1, source_target_pairs={{0,1},{1,0},{2,3},{3,2},{4,5},{5,4},{6,7},{7,6},{8,9},{9,8},{10,11... | collective-permute-start | bytes 1179656 | tf_op jit(solution)/shard_map/ppermute | solution.py:185
  481.7 22.6 %collective-permute-start.110 = (bf16[32,2816]{1,0:T(8,128)(2,1)S(1)}, bf16[32,2816]{1,0:T(8,128)(2,1)S(1)}, u32[]{:S(2)}, u32[]{:S(2)}) collective-permute-start(bf16[32,2816]{1,0:T(8,128)(2,1)S(1)} %get-tuple-element.132), channel_id=1, source_target_pairs={{0,3},{1,2},{2,1},{3,0},{4,7},{5,6},{6,5},{7,4},{8,11},{9,10},{10,... | collective-permute-start | bytes 540680 | tf_op jit(solution)/shard_map/ppermute | solution.py:185
  482.9 23.4 %collective-permute-start.111 = (bf16[32,2816]{1,0:T(8,128)(2,1)S(1)}, bf16[32,2816]{1,0:T(8,128)(2,1)S(1)}, u32[]{:S(2)}, u32[]{:S(2)}) collective-permute-start(bf16[32,2816]{1,0:T(8,128)(2,1)S(1)} %get-tuple-element.133), channel_id=1, source_target_pairs={{0,2},{1,3},{2,0},{3,1},{4,6},{5,7},{6,4},{7,5},{8,10},{9,11},{10,... | collective-permute-start | bytes 540680 | tf_op jit(solution)/shard_map/ppermute | solution.py:185
  504.3 31.2 %collective-permute-start.114 = (bf16[2,128,1024]{2,1,0:T(8,128)(2,1)S(1)}, bf16[2,128,1024]{2,1,0:T(8,128)(2,1)S(1)}, u32[]{:S(2)}, u32[]{:S(2)}) collective-permute-start(bf16[2,128,1024]{2,1,0:T(8,128)(2,1)S(1)} %select_bitcast_fusion.5), channel_id=1, source_target_pairs={{0,8},{1,9},{2,10},{3,11},{4,12},{5,13},{6,14},{7,15},{8,0},{9,1},... | collective-permute-start | bytes 1572872 | tf_op jit(solution)/shard_map/ppermute | solution.py:185
  506.3 31.0 %collective-permute-start.89 = (bf16[192,1024]{1,0:T(8,128)(2,1)S(1)}, bf16[192,1024]{1,0:T(8,128)(2,1)S(1)}, u32[]{:S(2)}, u32[]{:S(2)}) collective-permute-start(bf16[192,1024]{1,0:T(8,128)(2,1)S(1)} %collective-permute-done.87), channel_id=1, source_target_pairs={{0,1},{1,0},{2,3},{3,2},{4,5},{5,4},{6,7},{7,6},{8,9},{9,8},{10,11... | collective-permute-start | bytes 1179656 | tf_op jit(solution)/shard_map/ppermute | solution.py:185
  520.0 67.2 %collective-permute-start.124 = (bf16[1,128,1024]{2,1,0:T(8,128)(2,1)}, bf16[1,128,1024]{2,1,0:T(8,128)(2,1)}, u32[]{:S(2)}, u32[]{:S(2)}) collective-permute-start(bf16[1,128,1024]{2,1,0:T(8,128)(2,1)} %select_bitcast_fusion.8), channel_id=1, source_target_pairs={{0,16},{1,17},{2,18},{3,19},{4,20},{5,21},{6,22},{7,23},{8,24},{9,... | collective-permute-start | bytes 786440 | tf_op jit(solution)/shard_map/ppermute | solution.py:185
  537.3 54.5 %collective-permute-start.115 = (bf16[1,128,1024]{2,1,0:T(8,128)(2,1)}, bf16[1,128,1024]{2,1,0:T(8,128)(2,1)}, u32[]{:S(2)}, u32[]{:S(2)}) collective-permute-start(bf16[1,128,1024]{2,1,0:T(8,128)(2,1)} %select_bitcast_fusion.9), channel_id=1, source_target_pairs={{0,16},{1,17},{2,18},{3,19},{4,20},{5,21},{6,22},{7,23},{8,24},{9,... | collective-permute-start | bytes 786440 | tf_op jit(solution)/shard_map/ppermute | solution.py:185
  570.5 19.2 %collective-permute-start.116 = (bf16[128,1024]{1,0:T(8,128)(2,1)S(1)}, bf16[128,1024]{1,0:T(8,128)(2,1)}, u32[]{:S(2)}, u32[]{:S(2)}) collective-permute-start(bf16[128,1024]{1,0:T(8,128)(2,1)S(1)} %broadcast_select_fusion), channel_id=1, source_target_pairs={{0,16},{1,17},{2,18},{3,19},{4,20},{5,21},{6,22},{7,23},{8,24},{9,... | collective-permute-start | bytes 786440 | tf_op jit(solution)/shard_map/ppermute | solution.py:185
  576.3 32.4 %collective-permute-start.98 = (bf16[4,128,768]{2,1,0:T(8,128)(2,1)}, bf16[4,128,768]{2,1,0:T(8,128)(2,1)}, u32[]{:S(2)}, u32[]{:S(2)}) collective-permute-start(bf16[4,128,768]{2,1,0:T(8,128)(2,1)} %select_bitcast_fusion.3), channel_id=1, source_target_pairs={{0,4},{1,5},{2,6},{3,7},{4,0},{5,1},{6,2},{7,3},{8,12},{9,13},{10,... | collective-permute-start | bytes 2359304 | tf_op jit(solution)/shard_map/ppermute | solution.py:185
  585.5 15.6 %collective-permute-start.96 = (bf16[192,1024]{1,0:T(8,128)(2,1)}, bf16[192,1024]{1,0:T(8,128)(2,1)}, u32[]{:S(2)}, u32[]{:S(2)}) collective-permute-start(bf16[192,1024]{1,0:T(8,128)(2,1)} %get-tuple-element.107), channel_id=1, source_target_pairs={{0,1},{1,0},{2,3},{3,2},{4,5},{5,4},{6,7},{7,6},{8,9},{9,8},{10,11... | collective-permute-start | bytes 1179656 | tf_op jit(solution)/shard_map/ppermute | solution.py:185
  587.3 24.4 %collective-permute-start.95 = (bf16[192,1024]{1,0:T(8,128)(2,1)}, bf16[192,1024]{1,0:T(8,128)(2,1)}, u32[]{:S(2)}, u32[]{:S(2)}) collective-permute-start(bf16[192,1024]{1,0:T(8,128)(2,1)} %get-tuple-element.106), channel_id=1, source_target_pairs={{0,1},{1,0},{2,3},{3,2},{4,5},{5,4},{6,7},{7,6},{8,9},{9,8},{10,11... | collective-permute-start | bytes 1179656 | tf_op jit(solution)/shard_map/ppermute | solution.py:185
  (232 other events, 2043.9 us)
Sparse Core Ops, SparseCore 0:
  148.7 54.0 all-gather.2
  211.8 48.0 all-gather.4
  327.2 66.1 reduce-scatter.2
  396.8 83.4 reduce-scatter.4

commit v2 on v1

v2 whole, which is shorter than its diff:
```python
import functools
import math

import jax
import jax.numpy as jnp
from jax import lax
from jax.experimental import pallas as pl
from jax.experimental.pallas import tpu as pltpu
from jax.sharding import PartitionSpec as P

HEAD = 64
EPSILON = 1e-05
NEGATIVE = -1e30
HIGHEST = lax.Precision.HIGHEST
AXES = ("dp", "seq")
BF = jnp.bfloat16
F32 = jnp.float32
VMEM_LIMIT = 56 * 1024 * 1024


def dot(left, right, left_dim=1, right_dim=0):
    return lax.dot_general(
        left, right, (((left_dim,), (right_dim,)), ((), ())), preferred_element_type=F32
    )


def head_lanes(shape, half):
    lane = lax.broadcasted_iota(jnp.int32, shape, 1)
    return (lane < HEAD) if half == 0 else (lane >= HEAD)


def attend_kernel(block, qkv_ref, col_ref, row_ref, out_ref, max_ref, sum_ref):
    tokens, width = out_ref.shape
    pairs = width // (2 * HEAD)
    scale = 1.0 / math.sqrt(HEAD)
    for pair in range(pairs):
        lo = pair * 2 * HEAD
        keys = qkv_ref[:, width + lo : width + lo + 2 * HEAD]
        values = qkv_ref[:, 2 * width + lo : 2 * width + lo + 2 * HEAD]
        values_t = values.astype(F32).T.astype(BF)
        for start in range(0, tokens, block):
            queries = qkv_ref[start : start + block, lo : lo + 2 * HEAD] * scale
            queries = queries.astype(BF)
            same = col_ref[...] == row_ref[:, start : start + block]
            halves = []
            for half in range(2):
                lanes = head_lanes(queries.shape, half)
                scores = dot(keys, jnp.where(lanes, queries, jnp.zeros_like(queries)), 1, 1)
                scores = jnp.where(same, scores, NEGATIVE)
                top = jnp.max(scores, axis=0, keepdims=True)
                raised = jnp.exp(scores - top)
                total = jnp.sum(raised, axis=0, keepdims=True)
                probs = (raised * (1.0 / total)).astype(BF)
                mixed = dot(values_t, probs)
                halves.append(mixed[half * HEAD : (half + 1) * HEAD])
                head = 2 * pair + half
                max_ref[head : head + 1, start : start + block] = top
                sum_ref[head : head + 1, start : start + block] = total
            joined = jnp.concatenate(halves, axis=0)
            out_ref[start : start + block, lo : lo + 2 * HEAD] = joined.T.astype(BF)


def attend_back_kernel(
    block, qkv_ref, col_ref, row_ref, max_ref, sum_ref, grad_ref, out_ref, key_acc, value_acc
):
    tokens, width = grad_ref.shape
    pairs = width // (2 * HEAD)
    scale = 1.0 / math.sqrt(HEAD)
    for pair in range(pairs):
        lo = pair * 2 * HEAD
        keys = qkv_ref[:, width + lo : width + lo + 2 * HEAD]
        values = qkv_ref[:, 2 * width + lo : 2 * width + lo + 2 * HEAD]
        keys_t = keys.astype(F32).T.astype(BF)
        key_acc[...] = jnp.zeros_like(key_acc)
        value_acc[...] = jnp.zeros_like(value_acc)
        for start in range(0, tokens, block):
            queries = (qkv_ref[start : start + block, lo : lo + 2 * HEAD] * scale).astype(BF)
            grads = grad_ref[start : start + block, lo : lo + 2 * HEAD]
            same = col_ref[...] == row_ref[:, start : start + block]
            halves = []
            for half in range(2):
                lanes = head_lanes(queries.shape, half)
                own_queries = jnp.where(lanes, queries, jnp.zeros_like(queries))
                own_grads = jnp.where(lanes, grads, jnp.zeros_like(grads))
                head = 2 * pair + half
                top = max_ref[head : head + 1, start : start + block]
                total = sum_ref[head : head + 1, start : start + block]
                scores = dot(keys, own_queries, 1, 1)
                scores = jnp.where(same, scores, NEGATIVE)
                probs = jnp.exp(scores - top) * (1.0 / total)
                grad_probs = dot(values, own_grads, 1, 1)
                shared = jnp.sum(probs * grad_probs, axis=0, keepdims=True)
                grad_scores = (probs * (grad_probs - shared)).astype(BF)
                value_acc[...] += dot(probs.astype(BF), own_grads)
                key_acc[...] += dot(grad_scores, own_queries)
                mixed = dot(keys_t, grad_scores)
                halves.append(mixed[half * HEAD : (half + 1) * HEAD])
            joined = jnp.concatenate(halves, axis=0) * scale
            out_ref[start : start + block, lo : lo + 2 * HEAD] = joined.T.astype(BF)
        out_ref[:, width + lo : width + lo + 2 * HEAD] = key_acc[...].astype(BF)
        out_ref[:, 2 * width + lo : 2 * width + lo + 2 * HEAD] = value_acc[...].astype(BF)


def attend(qkv, starts):
    tokens, width = qkv.shape[0], qkv.shape[1] // 3
    heads = width // HEAD
    whole = pl.BlockSpec(memory_space=pltpu.VMEM)
    return pl.pallas_call(
        functools.partial(attend_kernel, 256),
        out_shape=(
            jax.ShapeDtypeStruct((tokens, width), BF),
            jax.ShapeDtypeStruct((heads, tokens), F32),
            jax.ShapeDtypeStruct((heads, tokens), F32),
        ),
        in_specs=[whole] * 3,
        out_specs=(whole,) * 3,
        compiler_params=pltpu.CompilerParams(vmem_limit_bytes=VMEM_LIMIT),
        cost_estimate=pl.CostEstimate(
            flops=40 * tokens * tokens * width, bytes_accessed=16 * tokens * width, transcendentals=0
        ),
    )(qkv, starts[:, None], starts[None, :])


def attend_back(qkv, starts, row_max, row_sum, grads):
    tokens, width = grads.shape
    whole = pl.BlockSpec(memory_space=pltpu.VMEM)
    return pl.pallas_call(
        functools.partial(attend_back_kernel, 256),
        out_shape=jax.ShapeDtypeStruct((tokens, 3 * width), BF),
        in_specs=[whole] * 6,
        out_specs=whole,
        scratch_shapes=[
            pltpu.VMEM((tokens, 2 * HEAD), F32),
            pltpu.VMEM((tokens, 2 * HEAD), F32),
        ],
        compiler_params=pltpu.CompilerParams(vmem_limit_bytes=VMEM_LIMIT),
        cost_estimate=pl.CostEstimate(
            flops=40 * tokens * tokens * width, bytes_accessed=16 * tokens * width, transcendentals=0
        ),
    )(qkv, starts[:, None], starts[None, :], row_max, row_sum, grads)


def place_rows(order, sizes, pieces, outs):
    me = lax.axis_index("dp")
    for steps, piece in zip(order, pieces):
        first = 0
        for step in steps:
            if isinstance(step, tuple):
                where = step[0] * 2 + (lax.rem(me, 2) ^ step[1])
            else:
                where = me ^ step
            for member, rows in enumerate(sizes):
                at = pl.multiple_of(where * rows, rows)
                outs[member][pl.ds(at, rows), :] = piece[first : first + rows, :]
                first += rows


def place_kernel(order, sizes, *refs):
    place_rows(order, sizes, refs[: len(order)], refs[len(order) :])


def place_first_kernel(order, sizes, pairs, layers, *refs):
    pieces, (weights, smalls, full, heads, inner) = refs[: len(order)], refs[len(order) :]
    place_rows(order, sizes, pieces, (weights, smalls))
    seq, n_seq = lax.axis_index("seq"), 4
    n_dp = smalls.shape[0] // 16
    lane = lax.broadcasted_iota(jnp.int32, (4, 128), 1)
    for dp in range(n_dp):
        rows = smalls[dp * 16 : dp * 16 + 16, :].astype(F32)
        for block in range(6):
            part = rows[:, block * 128 : block * 128 + 128]
            total = part[:4]
            for s in range(1, n_seq):
                moved = pltpu.roll(part, 32 * s, 1)[4 * s : 4 * s + 4]
                total = jnp.where(lane // 32 == s, moved, total)
            full[block, 0:4, dp * 128 : dp * 128 + 128] = total
            if block == 2:
                own = part[:4]
                for s in range(1, n_seq):
                    own = jnp.where(seq == s, part[4 * s : 4 * s + 4], own)
                inner[0:layers, dp * 128 : dp * 128 + 128] = own[layers : 2 * layers]
    heads[...] = jnp.zeros_like(heads)
    width = pairs * 128
    for which, base in ((0, 0), (1, 2 * width)):
        for pair in range(pairs):
            column = pl.multiple_of((pair * n_seq + seq) * 128, 128)
            heads[0:layers, base + pair * 128 : base + pair * 128 + 128] = full[
                which, 0:layers, pl.ds(column, 128)
            ]


def place(pieces, order, sizes, unpack=None):
    columns = pieces[0].shape[1]
    order = tuple(tuple(o) if isinstance(o, (list, tuple)) else (o,) for o in order)
    count = sum(len(o) for o in order)
    whole = pl.BlockSpec(memory_space=pltpu.VMEM)
    shapes = [jax.ShapeDtypeStruct((count * rows, columns), BF) for rows in sizes]
    body = functools.partial(place_kernel, order, tuple(sizes))
    if unpack is not None:
        pairs, layers, dim, inner = unpack
        shapes += [
            jax.ShapeDtypeStruct((6, 8, dim), F32),
            jax.ShapeDtypeStruct((8, pairs * 3 * 128), F32),
            jax.ShapeDtypeStruct((8, inner), F32),
        ]
        body = functools.partial(place_first_kernel, order, tuple(sizes), pairs, layers)
    return pl.pallas_call(
        body,
        out_shape=tuple(shapes),
        in_specs=[whole] * len(pieces),
        out_specs=(whole,) * len(shapes),
        compiler_params=pltpu.CompilerParams(vmem_limit_bytes=VMEM_LIMIT),
        cost_estimate=pl.CostEstimate(flops=0, bytes_accessed=0, transcendentals=0),
    )(*pieces)


def split_kernel(n_seq, plan, part, smalls, *refs):
    n_in = 1 + max(p[0] for p in plan)
    weights, rest = refs[:n_in], refs[n_in:]
    small_refs, rest = rest[:smalls], rest[smalls:]
    outs = rest[:n_seq]
    seq = lax.axis_index("seq")
    if smalls:
        table = rest[n_seq]
        table[...] = jnp.zeros_like(table)
        across = table.shape[1] // 128
        for j, small in enumerate(small_refs):
            row, lane = 2 * (j // across), 128 * (j % across)
            table[row : row + 2, lane : lane + small.shape[1]] = small[...].astype(F32)
    for step in range(n_seq):
        target = seq ^ step
        at = 0
        for ref, layer, block, count in plan:
            if not count:
                outs[step][:part, at : at + block] = weights[ref][layer]
                at += block
            for i in range(count):
                column = pl.multiple_of((i * n_seq + target) * block, 128)
                outs[step][:part, at : at + block] = weights[ref][layer, :, pl.ds(column, block)]
                at += block
        if smalls:
            outs[step][part:, :] = table[...].astype(BF)


def split_weights(weights, plan, n_seq, smalls=()):
    part = weights[0].shape[1]
    columns = sum(block * max(count, 1) for _, _, block, count in plan)
    rows = part + (16 if smalls else 0)
    whole = pl.BlockSpec(memory_space=pltpu.VMEM)
    return pl.pallas_call(
        functools.partial(split_kernel, n_seq, tuple(plan), part, len(smalls)),
        out_shape=tuple(jax.ShapeDtypeStruct((rows, columns), BF) for _ in range(n_seq)),
        in_specs=[whole] * (len(weights) + len(smalls)),
        out_specs=(whole,) * n_seq,
        scratch_shapes=[pltpu.VMEM((16, columns), F32)] if smalls else [],
        compiler_params=pltpu.CompilerParams(vmem_limit_bytes=VMEM_LIMIT),
    )(*weights, *smalls)


def join_kernel(n_seq, part, cuts, with_small, extra, *refs):
    pieces, rest = refs[:n_seq], refs[n_seq:]
    if extra:
        extra_ref, rest = rest[0], rest[1:]
    outs = rest[: len(cuts)]
    seq = lax.axis_index("seq")
    for step in range(n_seq):
        row = pl.multiple_of((seq ^ step) * part, part)
        at = 0
        for out, columns in zip(outs, cuts):
            out[pl.ds(row, part), :] = pieces[step][:part, at : at + columns]
            at += columns
    if with_small:
        table = rest[len(cuts)]
        smalls = [pieces[step][part:, :].astype(F32)[:4] for step in range(n_seq)]
        for origin in range(n_seq):
            total = jnp.zeros_like(smalls[0])
            for step in range(n_seq):
                total = jnp.where((seq ^ step) == origin, smalls[step], total)
            table[4 * origin : 4 * origin + 4, :] = total
        outs[0][n_seq * part :, :] = table[...].astype(BF)
    if extra:
        outs[0][n_seq * part :, :] = extra_ref[0]


def join_pieces(pieces, part, cuts, with_small=False, extra=None):
    n_seq = len(pieces)
    rows = [n_seq * part] * len(cuts)
    if with_small:
        rows[0] += 4 * n_seq
    if extra is not None:
        rows[0] += extra.shape[1]
    whole = pl.BlockSpec(memory_space=pltpu.VMEM)
    more = [] if extra is None else [extra]
    return pl.pallas_call(
        functools.partial(
            join_kernel, n_seq, part, tuple(cuts), with_small, extra is not None
        ),
        out_shape=tuple(jax.ShapeDtypeStruct((r, c), BF) for r, c in zip(rows, cuts)),
        in_specs=[whole] * (n_seq + len(more)),
        out_specs=(whole,) * len(cuts),
        scratch_shapes=[pltpu.VMEM((4 * n_seq, cuts[0]), F32)] if with_small else [],
        compiler_params=pltpu.CompilerParams(vmem_limit_bytes=VMEM_LIMIT),
    )(*pieces, *more)


def after(array, *others):
    return lax.optimization_barrier((array,) + others)[0] if others else array


def solution(mesh):
    n_dp, n_seq = mesh.shape["dp"], mesh.shape["seq"]
    n_dev = n_dp * n_seq
    special = (n_dp, n_seq) == (8, 4)

    def swap(array, bit):
        return lax.ppermute(array, AXES, [(p, p ^ bit) for p in range(n_dev)])

    def bits_of(count, unit=1):
        bits = []
        while count > 1:
            bits.append(unit)
            unit, count = unit * 2, count // 2
        return bits

    seq_bits, dp_bits = bits_of(n_seq), bits_of(n_dp, n_seq)

    z_lines = [[d for d in range(n_dp) if d % 2 == y] for y in range(2)]

    seq_steps = [0]
    for bit in reversed(seq_bits):
        seq_steps = seq_steps + [s ^ bit for s in seq_steps]

    def spread(piece, bits):
        pieces, steps = [piece], [0]
        for bit in reversed(bits):
            pieces = pieces + [swap(p, bit) for p in pieces]
            steps = steps + [s ^ bit for s in steps]
        return pieces, steps

    def launch(moves, gate):
        return [
            (home, name, swap(after(array, gate), bit) if bit else array)
            for home, name, array, bit in moves
        ]

    def settle(array, moving):
        if not moving:
            return array
        out = lax.optimization_barrier((array,) + tuple(m[2] for m in moving))
        for (home, name, _), value in zip(moving, out[1:]):
            setattr(home, name, value)
        return out[0]

    def gather_seq(rows, moves=(), gate=None):
        moving = launch(moves, rows if gate is None else gate)
        for bit in reversed(seq_bits):
            got = settle(swap(rows, bit), moving)
            moving = []
            rows = jnp.concatenate([rows, got], axis=0)
        return rows

    def reduce_seq(left, right, moves=(), gate=None):
        weight, dims = right
        moving = launch(moves, left if gate is None else gate)
        half = left.shape[0] // 2
        got = swap(dot(left[half:], weight, *dims).astype(BF), seq_bits[0])
        total = dot(left[:half], weight, *dims) + got.astype(F32)
        for i, bit in enumerate(seq_bits[1:]):
            half = total.shape[0] // 2
            got = swap(total[half:].astype(BF), bit)
            if i + 2 == len(seq_bits):
                got = settle(got, moving)
            total = total[:half] + got.astype(F32)
        return total

    def halve(array, index_bit, bit):
        chosen = index_bit.astype(jnp.bool_)
        send = jnp.where(chosen, array[0], array[1])
        keep = jnp.where(chosen, array[1], array[0])
        return keep, swap(send, bit)

    def local(
        tokens, doc_start, lexical_ids, queries, match_index,
        query_weight, query_bias, key_weight, value_weight, value_bias,
        out_weight, out_bias, norm_gain, norm_bias, expand_weight, expand_bias,
        shrink_weight, shrink_bias, final_gain, final_bias,
        lexical_weight, lexical_bias, score_cot, encoded_cot,
    ):
        layers, part, dim = query_weight.shape
        hidden_dim = expand_weight.shape[2]
        hidden_part = shrink_weight.shape[1]
        rows_here = tokens.shape[0]
        pairs_here = dim // (2 * HEAD) // n_seq
        width = pairs_here * 2 * HEAD
        own_hidden = hidden_dim // n_seq
        block_rows = dim // n_dp
        dp, seq = lax.axis_index("dp"), lax.axis_index("seq")
        flat = dp * n_seq + seq

        def bit_of(index, bit):
            return lax.bitwise_and(lax.div(index, bit), 1)

        def by_origin(pieces):
            for bit in seq_bits:
                chosen = bit_of(seq, bit).astype(jnp.bool_)
                pieces = [jnp.where(chosen, pieces[j ^ bit], pieces[j]) for j in range(n_seq)]
            return pieces

        def exchange_steps(blocks):
            pieces = by_origin(blocks)
            return [pieces[0]] + [swap(pieces[step], step) for step in range(1, n_seq)]

        def exchange_seq(blocks):
            return by_origin(exchange_steps(blocks))

        def head_split(weight):
            cut = [weight[:, i * 2 * HEAD : (i + 1) * 2 * HEAD] for i in range(pairs_here * n_seq)]
            return [cut[s::n_seq] for s in range(n_seq)]

        def hidden_split(weight):
            cut = [
                weight[:, i * hidden_part : (i + 1) * hidden_part] for i in range(n_dp * n_seq)
            ]
            return [cut[s::n_seq] for s in range(n_seq)]

        def qkv_split(layer):
            three = [head_split(w[layer]) for w in (query_weight, key_weight, value_weight)]
            return [jnp.concatenate(three[0][s] + three[1][s] + three[2][s], axis=1) for s in range(n_seq)]

        small_full = (
            query_bias, value_bias, out_bias, norm_gain, norm_bias, shrink_bias, final_gain, final_bias,
        )
        three = [query_weight, key_weight, value_weight]
        hidden_now = tokens.astype(F32)
        if special:
            heads_plan = [(i, 0, 2 * HEAD, pairs_here) for i in range(3)]
            sent = split_weights(three, heads_plan, n_seq, small_full + (expand_bias,))
            got = [sent[0]] + [swap(sent[step], step) for step in range(1, n_seq)]
            (shard,) = join_pieces(got, part, (3 * width,), True)
            class Stream:
                def __init__(self, shard):
                    self.shard = shard

                def far(self):
                    return [(self, "came", self.shard, n_seq * 4)]

                def middle(self):
                    self.line = jnp.concatenate([self.shard, self.came], axis=0)
                    return [
                        (self, "near", self.line, n_seq * 2),
                        (self, "y_line", self.line, n_seq),
                    ]

                def last(self):
                    return [(self, "y_near", self.near, n_seq)]

                def ready(self, sizes):
                    return [(self, "full", self.whole(sizes)[0], 0)]

                def whole(self, sizes, unpack=None):
                    pieces = [self.line, self.near, self.y_line, self.y_near]
                    return place(pieces, [[0, 4], [2, 6], [1, 5], [3, 7]], sizes, unpack)

            first_stream = Stream(shard)
            group = gather_seq(tokens)
            plan = [(3, 0, hidden_part, n_dp)]
            cuts = [own_hidden]
            for layer in range(1, layers):
                plan += [(i, layer, 2 * HEAD, pairs_here) for i in range(3)]
                plan += [(3, layer, hidden_part, n_dp)]
                cuts += [3 * width, own_hidden]
            plan += [(4, layer, dim, 0) for layer in range(layers)]
            cuts += [dim] * layers
            sent = split_weights(three + [expand_weight, out_weight], plan, n_seq)
            sent = [after(p, got[1], got[2], got[3]) for p in sent]
            got = [sent[0]] + [swap(sent[step], step) for step in range(1, n_seq)]
            second = join_pieces(got, part, cuts)

            class OutRows:
                def __init__(self, rows):
                    self.rows, self.moved, self.bit = rows, None, 0

                def take(self):
                    bit, moved = self.bit, self.moved
                    if bit in (1, 2):
                        here = bit_of(seq, bit) == bit_of(dp, bit)
                        self.rows = jnp.where(here, self.rows, moved)
                    elif bit == 4:
                        upper = bit_of(dp, 4) == 1
                        self.rows = jnp.concatenate(
                            [jnp.where(upper, moved, self.rows), jnp.where(upper, self.rows, moved)],
                            axis=0,
                        )
                    self.bit = 0
                    self.rows = lax.optimization_barrier(self.rows)
                    return self.rows

                def step(self, bit):
                    rows = self.take()
                    self.bit = bit
                    return [(self, "moved", rows, n_seq * bit)]

            outs = [OutRows(second[2 * layers - 1 + i]) for i in range(layers)]
            streams = [
                Stream(x)
                for x in (second[0], shrink_weight[0], second[1], second[2], shrink_weight[1])
            ]
            expand_0, shrink_0, qkv_1, expand_1, shrink_1 = streams
            shard = settle(shard, launch(first_stream.far(), shard))
            moving = launch(first_stream.middle(), first_stream.came)
            out_y = launch(outs[0].step(1), first_stream.came)
            settle(shard, moving)
            gate = first_stream.near
            moving = launch(first_stream.last(), first_stream.y_line)
            settle(shard, out_y)
            moving += launch(expand_0.far() + outs[0].step(2), gate)
            group = settle(group, moving)
            qkv_first, _, small_full, small_heads, small_inner = first_stream.whole(
                (block_rows, 16), (pairs_here, layers, dim, own_hidden)
            )
            head_bias, hidden_bias = small_heads[:layers], small_inner[:layers]

            def vector_of(layer, j):
                return small_full[j % 6, layers * (j // 6) + layer]

        else:
            small = lax.all_gather(
                jnp.concatenate(list(small_full) + [expand_bias], axis=1), AXES, axis=0, tiled=False
            )
            full = small[:, :, : 8 * part].reshape(n_dev, layers, 8, part).transpose(1, 2, 0, 3)
            hidden_bias = small[:, :, 8 * part :].transpose(1, 0, 2)
            group = gather_seq(tokens)
            full = full.reshape(layers, 8, dim).astype(F32)
            by_column = full[:, :2].reshape(layers, 2, pairs_here, n_seq, 2 * HEAD)
            by_column = lax.dynamic_index_in_dim(by_column, seq, 3, keepdims=False)
            by_column = by_column.reshape(layers, 2, width)
            head_bias = jnp.concatenate(
                [by_column[:, 0], jnp.zeros((layers, width), F32), by_column[:, 1]], axis=1
            )
            hidden_bias = hidden_bias.reshape(layers, n_dp, n_seq, hidden_part)
            hidden_bias = lax.dynamic_index_in_dim(hidden_bias, seq, 2, keepdims=False)
            hidden_bias = hidden_bias.reshape(layers, own_hidden).astype(F32)

            def vector_of(layer, j):
                return full[layer, j]

        if special:
            out_all = []
        else:
            whole_out = lax.all_gather(out_weight, AXES, axis=1, tiled=True)
            cut = whole_out.reshape(layers, pairs_here, n_seq, 2 * HEAD, dim)
            cut = lax.dynamic_index_in_dim(cut, seq, 2, keepdims=False)
            out_all = [cut[layer].reshape(width, dim) for layer in range(layers)]

        if special:
            qkv_all, expand_all, shrink_all = [qkv_first], [], []

            def beside_of(layer, point):
                if (layer, point) == (0, "attend"):
                    return expand_0.middle() + outs[0].step(4)
                if (layer, point) == (0, "out"):
                    out_all.append(outs[0].take())
                    return expand_0.last() + shrink_0.far()
                if (layer, point) == (0, "normed"):
                    return shrink_0.middle() + expand_0.ready((block_rows,))
                if (layer, point) == (0, "active"):
                    expand_all.append(expand_0.full)
                    return shrink_0.last() + qkv_1.far()
                if (layer, point) == (0, "shrink"):
                    shrink_all.append(shrink_0.whole((hidden_part,))[0])
                    return qkv_1.middle() + outs[1].step(1)
                if (layer, point) == (1, "group"):
                    return qkv_1.last() + expand_1.far() + outs[1].step(2)
                if (layer, point) == (1, "attend"):
                    qkv_all.append(qkv_1.whole((block_rows,))[0])
                    return outs[1].step(4) + expand_1.middle()
                if (layer, point) == (1, "out"):
                    out_all.append(outs[1].take())
                    return expand_1.last() + shrink_1.far()
                if (layer, point) == (1, "normed"):
                    return shrink_1.middle() + expand_1.ready((block_rows,))
                if (layer, point) == (1, "active"):
                    expand_all.append(expand_1.full)
                    return shrink_1.last()
                if (layer, point) == (1, "shrink"):
                    shrink_all.append(shrink_1.whole((hidden_part,))[0])
                return []
        else:
            qkv_all, expand_all, shrink_all = [], [], []

            def beside_of(layer, point):
                return []

            for layer in range(layers):
                mine = exchange_seq(qkv_split(layer))
                mine = lax.all_gather(jnp.concatenate(mine, axis=0), "dp", axis=0, tiled=True)
                qkv_all.append(mine)
                mine = [jnp.concatenate(b, axis=1) for b in hidden_split(expand_weight[layer])]
                mine = jnp.concatenate(exchange_seq(mine), axis=0)
                expand_all.append(lax.all_gather(mine, "dp", axis=0, tiled=True))
                shrink_all.append(lax.all_gather(shrink_weight[layer], "dp", axis=0, tiled=True))

        starts_here = doc_start[0].reshape(n_seq, rows_here)
        starts = jnp.concatenate(
            [
                lax.dynamic_index_in_dim(starts_here, seq ^ step, 0, keepdims=False)
                for step in seq_steps
            ]
        )

        def norm_parts(resid):
            center = resid - jnp.mean(resid, axis=-1, keepdims=True)
            inverse = lax.rsqrt(jnp.mean(center * center, axis=-1, keepdims=True) + EPSILON)
            return center * inverse, inverse

        def norm_back(upstream, gain, rhat, inverse):
            scaled = upstream * gain
            mean_one = jnp.mean(scaled, axis=-1, keepdims=True)
            mean_two = jnp.mean(scaled * rhat, axis=-1, keepdims=True)
            grad = (scaled - mean_one - rhat * mean_two) * inverse
            return grad, jnp.sum(upstream * rhat, axis=0), jnp.sum(upstream, axis=0)

        def column_sums(matrix):
            return jnp.sum(matrix.astype(F32), axis=0)

        kept = []
        for layer in range(layers):
            _, _, out_b, gain_one, bias_one, shrink_b, gain_two, bias_two = (
                vector_of(layer, i) for i in range(8)
            )
            if layer:
                group = gather_seq(hidden_now.astype(BF), beside_of(layer, "group"), summed)
            moving = launch(beside_of(layer, "attend"), group)
            qkv = (dot(group, qkv_all[layer]) + head_bias[layer]).astype(BF)
            attended, row_max, row_sum = attend(qkv, starts)
            attended = settle(attended, moving)
            moves = beside_of(layer, "out")
            summed = reduce_seq(attended, (out_all[layer], (1, 0)), moves)
            resid_one = hidden_now + (summed + out_b)
            rhat_one, inverse_one = norm_parts(resid_one)
            normed = rhat_one * gain_one + bias_one
            normed_group = gather_seq(normed.astype(BF), beside_of(layer, "normed"), summed)
            moves = beside_of(layer, "active")
            moving = launch(moves, moves[0][2] if moves else normed_group)
            inner = dot(normed_group, expand_all[layer]) + hidden_bias[layer]
            cdf = 0.5 * (1.0 + lax.erf(inner * math.sqrt(0.5)))
            active = (inner * cdf).astype(BF)
            slope = cdf + inner * jnp.exp(-0.5 * inner * inner) * (1.0 / math.sqrt(2 * math.pi))
            active = settle(active, moving)
            moves = beside_of(layer, "shrink")
            summed = reduce_seq(active, (shrink_all[layer], (1, 0)), moves)
            resid_two = normed + (summed + shrink_b)
            rhat_two, inverse_two = norm_parts(resid_two)
            hidden_now = rhat_two * gain_two + bias_two
            kept.append(
                (group, qkv, attended, row_max, row_sum, rhat_one, inverse_one, normed_group,
                 active, slope, rhat_two, inverse_two)
            )
        encoded = hidden_now.astype(BF)

        local_index = match_index[0] - seq * rows_here
        picker = local_index[:, None] == jnp.arange(rows_here, dtype=jnp.int32)[None, :]
        chosen = dot(picker.astype(BF), encoded)
        query_vecs = queries[0].astype(F32)
        scores = jnp.sum(query_vecs * chosen, axis=-1)[None, :]
        lexical = jnp.sum(
            encoded.astype(F32) * lexical_weight.astype(F32)[None, :], axis=-1
        ) + lexical_bias.astype(F32)[0]
        keep_mask = (lexical_ids >= 4).astype(F32)
        local_sums = jnp.stack(
            [
                jnp.sum(keep_mask * jax.nn.softplus(lexical)),
                jnp.sum(keep_mask * jax.nn.sigmoid(lexical)),
            ]
        )
        weighted = score_cot[0][:, None] * query_vecs
        grad_now = encoded_cot.astype(F32) + lax.dot_general(
            picker.astype(F32), weighted, (((0,), (0,)), ((), ())), precision=HIGHEST
        )

        def scatter_dp(grad):
            return lax.psum_scatter(grad, "dp", scatter_dimension=0, tiled=True)

        class Sums:
            def __init__(self, grads, rows=block_rows):
                self.blocks = [g.reshape(2, 2, 2, rows, g.shape[-1]) for g in grads]

            def first(self):
                low, up = bit_of(dp, 2) == 1, bit_of(dp, 1) == 1

                def of(flip_low, flip_up):
                    parts = []
                    for b in self.blocks:
                        b = jnp.where(low ^ flip_low, b[:, 1], b[:, 0])
                        parts.append(jnp.where(up ^ flip_up, b[:, 1], b[:, 0]))
                    return jnp.concatenate(parts, axis=-1)

                self.of = of
                self.keep = of(True, False)
                return [(self, "came", of(True, True), n_seq)]

            def middle(self):
                total = (self.keep.astype(F32) + self.came.astype(F32)).astype(BF)
                self.keep = self.of(False, False)
                return [
                    (self, "near", total, 2 * n_seq),
                    (self, "came", self.of(False, True), n_seq),
                ]

            def last(self):
                total = (
                    self.keep.astype(F32) + self.came.astype(F32) + self.near.astype(F32)
                ).astype(BF)
                high = bit_of(dp, 4) == 1
                self.keep = jnp.where(high, total[1], total[0])
                return [(self, "came", jnp.where(high, total[0], total[1]), 4 * n_seq)]

            def rows(self):
                return self.keep.astype(F32) + self.came.astype(F32)

        def scatter_out(grad):
            if not special:
                placed = grad.reshape(pairs_here, 1, 2 * HEAD, dim)
                hot = (jnp.arange(n_seq) == seq)[None, :, None, None]
                placed = jnp.where(hot, placed, jnp.zeros_like(placed)).reshape(dim, dim)
                return lax.psum_scatter(placed, AXES, scatter_dimension=0, tiled=True)
            return None

        def unsplit(pieces, size):
            count = pieces[0].shape[1] // size
            return jnp.concatenate(
                [pieces[s][:, i * size : (i + 1) * size] for i in range(count) for s in range(n_seq)],
                axis=1,
            )

        class Grads:
            pass

        class Back:
            def __init__(self, blocks):
                pieces = by_origin(blocks)
                self.step_0, self.pieces = pieces[0], pieces

            def moves(self):
                return [(self, "step_%d" % i, self.pieces[i], i) for i in range(1, n_seq)]

            def got(self):
                return [getattr(self, "step_%d" % i) for i in range(n_seq)]

        class Table:
            def __init__(self, rows, more):
                self.keep, self.more = rows, more
                self.bits = [4 * n_seq, 2 * n_seq, n_seq] + seq_bits

            def take(self):
                if hasattr(self, "came"):
                    self.keep = self.keep + self.came

            def step(self):
                self.take()
                bit = self.bits.pop(0)
                sent = self.keep
                if bit >= n_seq:
                    middle = self.keep.shape[1] // 2
                    low, up = self.keep[:, :middle], self.keep[:, middle:]
                    chosen = bit_of(dp, bit // n_seq) == 1
                    sent, self.keep = jnp.where(chosen, low, up), jnp.where(chosen, up, low)
                elif bit == seq_bits[0]:
                    columns = self.keep.shape[1]
                    more = jnp.pad(self.more, ((0, 0), (0, columns - self.more.shape[1])))
                    sent = self.keep = jnp.concatenate([self.keep, more], axis=0)
                return [(self, "came", sent, bit)]

        def rows_back(scattered):
            return exchange_steps([scattered[s * part : (s + 1) * part] for s in range(n_seq)])

        def columns_row(vector):
            hot = (jnp.arange(n_seq) == seq)[None, :, None]
            return jnp.where(hot, vector.reshape(pairs_here, 1, 2 * HEAD), 0.0).reshape(1, dim)

        def hidden_rows(vector):
            hot = (jnp.arange(n_seq) == seq)[:, None]
            return jnp.where(hot, vector[None, :], 0.0)

        def reduce_rows(rows, extra=None):
            unit = n_dp
            while unit > 1:
                unit //= 2
                middle = rows.shape[1] // 2
                keep, got = halve(
                    (rows[:, :middle], rows[:, middle:]), bit_of(dp, unit), unit * n_seq
                )
                rows = keep + got
            if extra is not None:
                extra = jnp.pad(extra, ((0, 0), (0, rows.shape[1] - extra.shape[1])))
                rows = jnp.concatenate([rows, extra], axis=0)
            for bit in seq_bits:
                rows = rows + swap(rows, bit)
            return rows

        def own_part(row):
            return lax.dynamic_slice_in_dim(row, seq * part, part)

        big = [None] * layers
        vectors, inner_vectors = [None] * layers, [None] * layers
        lex_row = jnp.zeros((1, n_dp, dim // n_dp), F32).at[0, :, :2].set(local_sums)
        lex_row = lex_row.reshape(1, dim)
        for layer in reversed(range(layers)):
            gain_one, gain_two = vector_of(layer, 3), vector_of(layer, 6)
            (group, qkv, attended, row_max, row_sum, rhat_one, inverse_one, normed_group,
             active, slope, rhat_two, inverse_two) = kept[layer]
            grad_second, fgain, fbias = norm_back(grad_now, gain_two, rhat_two, inverse_two)
            low_second = grad_second.astype(BF)

            def token_rows():
                return jnp.stack(
                    [column_sums(low_first), ngain, nbias, column_sums(low_second), fgain, fbias]
                )

            def layer_rows():
                vectors[0], inner_vectors[0] = token_rows(), hidden_rows(column_sums(low_inner))
                return jnp.concatenate(vectors + [lex_row] + inner_vectors, axis=0)

            above = big[layer + 1] if special and layer + 1 < layers else None
            moves = above.expand.last() + above.qkv.first() if above else []
            second_group = gather_seq(low_second, moves, grad_now)
            low_inner = (dot(second_group, shrink_all[layer], 1, 1) * slope).astype(BF)
            shrink_grad = dot(active, second_group, 0, 0).astype(BF)
            expand_grad = dot(normed_group, low_inner, 0, 0).astype(BF)
            if special:
                big[layer] = mine = Grads()
                mine.shrink, mine.expand = Sums([shrink_grad]), Sums([expand_grad])
                moves = above.qkv.middle() if above else mine.shrink.first()
            else:
                moves = []
            summed = reduce_seq(low_inner, (expand_all[layer], (1, 1)), moves)
            grad_normed = grad_second + summed
            grad_first, ngain, nbias = norm_back(grad_normed, gain_one, rhat_one, inverse_one)
            low_first = grad_first.astype(BF)
            if special:
                moves = above.qkv.last() + mine.shrink.first() if above else mine.shrink.middle()
            first_group = gather_seq(low_first, moves, summed)
            if special:
                moves = mine.shrink.middle() if above else mine.shrink.last() + mine.expand.first()
                moving = launch(moves, first_group)
            low_attn = dot(first_group, out_all[layer], 1, 1).astype(BF)
            out_grad = dot(attended, first_group, 0, 0).astype(BF)
            if special:
                quarter = dim // n_seq
                pieces = exchange_steps(
                    [out_grad[:, s * quarter : (s + 1) * quarter] for s in range(n_seq)]
                )
                pieces = [p.reshape(pairs_here, 1, 2 * HEAD, quarter) for p in by_origin(pieces)]
                out_columns = jnp.concatenate(pieces, axis=1).reshape(dim, quarter)
            grad_qkv = attend_back(qkv, starts, row_max, row_sum, low_attn)
            if special:
                grad_qkv = settle(grad_qkv, moving)
            qkv_grad = dot(group, grad_qkv, 0, 0).astype(BF)
            qkv_sums = column_sums(grad_qkv)
            if special:
                joined = [qkv_grad, out_columns]
                extra = 0
                if layer == 0:
                    extra = 16
                    rows = jnp.concatenate(
                        [
                            qkv_sums[:width].reshape(pairs_here, 2 * HEAD),
                            qkv_sums[2 * width :].reshape(pairs_here, 2 * HEAD),
                        ],
                        axis=1,
                    )
                    hot = (jnp.arange(n_seq) == seq)[None, :, None]
                    rows = jnp.where(hot, rows[:, None, :], 0.0).reshape(n_dp, 1, 4 * HEAD)
                    rows = jnp.pad(rows, ((0, 0), (0, 15), (0, 3 * width - 4 * HEAD))).astype(BF)
                    joined = [
                        jnp.pad(g.reshape(n_dp, block_rows, -1), ((0, 0), (0, 16), (0, 0)))
                        for g in joined
                    ]
                    joined[0] = jnp.concatenate([joined[0][:, :block_rows], rows], axis=1)
                mine.qkv = Sums(joined, block_rows + extra)
                if layer:
                    moves = mine.expand.middle()
                else:
                    table = Table(layer_rows(), scores)
                    moves = mine.shrink.last() + mine.qkv.first() + table.step()
            else:
                moves = []
            summed = reduce_seq(after(grad_qkv, qkv_grad), (qkv_all[layer], (1, 1)), moves)
            if special and layer == 0:

                def back_of(grads, extra=0):
                    grads = [g.astype(BF) for g in grads]
                    blocks = []
                    for s in range(n_seq):
                        rows = [g[s * part : (s + 1) * part] for g in grads]
                        if extra:
                            rows = [jnp.concatenate([r, g[block_rows:]], axis=0) for r, g in zip(rows, grads)]
                        blocks.append(jnp.concatenate(rows, axis=1) if len(rows) > 1 else rows[0])
                    return Back(blocks)

                backs = [None] + [back_of([m.expand.rows(), m.qkv.rows()]) for m in big[1:]]
                moves = mine.qkv.middle() + table.step()
                gate = settle(summed, launch(moves, summed))
                moves = mine.qkv.last() + mine.expand.first() + table.step()
                gate = settle(gate, launch(moves, gate))
                backs[0] = back_of([mine.qkv.rows()], 16)
                moves = mine.expand.middle() + backs[0].moves()
                gate = settle(gate, launch(moves, gate))
                moves = mine.expand.last() + table.step()
                for back in backs[1:]:
                    moves += back.moves()
                gate = settle(gate, launch(moves, gate))
                last_back = back_of([mine.expand.rows()])
                settle(gate, launch(last_back.moves() + table.step(), gate))
            if not special:
                big[layer] = (
                    scatter_dp(shrink_grad),
                    scatter_dp(expand_grad),
                    scatter_out(out_grad),
                    scatter_dp(qkv_grad),
                )
            grad_now = grad_first + summed
            head_rows = [columns_row(qkv_sums[:width]), columns_row(qkv_sums[2 * width :])]
            if layer or not special:
                vectors[layer] = token_rows()
                if layer:
                    vectors[layer] = jnp.concatenate([vectors[layer]] + head_rows, axis=0)
                inner_vectors[layer] = hidden_rows(column_sums(low_inner))

        tokens_grad = grad_now.astype(BF)

        counts = [v.shape[0] for v in vectors] + [1] + [n_seq] * layers
        if special:
            table.take()
            table = table.keep
            scores = table[-1:, : scores.shape[1]]
        else:
            table = reduce_rows(jnp.concatenate(vectors + [lex_row], axis=0), scores)
            scores = table[-1:, : scores.shape[1]]
            inner = reduce_rows(jnp.concatenate(inner_vectors, axis=0))
            last = reduce_rows(jnp.concatenate(head_rows, axis=0))
        cut = [0]
        for count in counts:
            cut.append(cut[-1] + count)
        tables = [table[cut[i] : cut[i + 1]] for i in range(len(counts))]
        if special:
            inner_tables = tables[layers + 1 :]
        else:
            inner_tables = [inner[i * n_seq : (i + 1) * n_seq] for i in range(layers)]
        lexical_stats = tables[layers][0, :2] / (rows_here * n_dev)
        inner_out = jnp.stack(
            [lax.dynamic_index_in_dim(t, seq, 0, keepdims=False) for t in inner_tables]
        )

        layer_outs = []
        for layer in range(layers):
            if special:
                shrink_rows = big[layer].shrink.rows()
                got = backs[layer].got()
                if layer:
                    got = by_origin(got)
                    expand_out, got = [g[:, :own_hidden] for g in got], [g[:, own_hidden:] for g in got]
                else:
                    source = seq ^ lax.rem(dp, n_seq)
                    row = got[0][part : part + 1, : 4 * HEAD]
                    for step in range(1, n_seq):
                        row = jnp.where(source == step, got[step][part : part + 1, : 4 * HEAD], row)
                    last = row.reshape(2, 2 * HEAD).astype(F32)
                    got = by_origin([g[:part] for g in got])
                    expand_out = by_origin(last_back.got())
                out_out = jnp.concatenate([g[:, 3 * width :] for g in got], axis=1)
            else:
                shrink_rows, expand_rows, out_out, qkv_rows = big[layer]
                got, expand_out = by_origin(rows_back(qkv_rows)), by_origin(rows_back(expand_rows))
            layer_outs.append(
                [
                    unsplit([g[:, i * width : (i + 1) * width] for g in got], 2 * HEAD)
                    for i in range(3)
                ]
                + [out_out, unsplit(expand_out, hidden_part), shrink_rows]
            )
        def vector_out(index):
            if index < 2:
                return jnp.stack(
                    [own_part(tables[i][6 + index] if i else last[index]) for i in range(layers)]
                )
            return jnp.stack([own_part(tables[i][index - 2]) for i in range(layers)])

        big_out = [jnp.stack([lo[i].astype(F32) for lo in layer_outs]) for i in range(6)]
        return (
            encoded, scores, lexical_stats, tokens_grad,
            big_out[0], vector_out(0), big_out[1], big_out[2], vector_out(1),
            big_out[3], vector_out(2), vector_out(3), vector_out(4),
            big_out[4], inner_out, big_out[5], vector_out(5),
            vector_out(6), vector_out(7),
        )

    rows = P(AXES, None)
    weight = P(None, AXES, None)
    vector = P(None, AXES)
    placed = (
        rows, P("dp", None), P(AXES), P("dp", None, None), P("dp", None),
        weight, vector, weight, weight, vector, weight, vector, vector, vector,
        weight, vector, weight, vector, vector, vector, P(), P(), P("dp", None), rows,
    )
    results = (
        rows, P("dp", None), P(), rows,
        weight, vector, weight, weight, vector, weight, vector, vector, vector,
        weight, vector, weight, vector, vector, vector,
    )
    return jax.shard_map(local, mesh=mesh, in_specs=placed, out_specs=results, check_vma=False)
```

time: 660 us -> 595 us (0.902)
  waiting for transfers between devices: 288 us -> 262 us
  local copies, waits for them, and re-layouts: 46.4 us -> 28.7 us
  Pallas kernels: 54.4 us -> 68.4 us
  between operations: 18.2 us -> 4.41 us
  matrix products: 84.4 us -> 71.3 us
  starting transfers between devices: 104 us -> 94.1 us
    ppermute x125 -> x112, waiting for transfers between devices: 288 us -> 262 us  [swap(): return lax.ppermute(array, AXES, [(p, p ^ bit) for p in range(n_dev)])]
    pallas_call x4 -> x10, Pallas kernels: 11.6 us -> 26.1 us  [the longest x6 17.7 us: place(): pl.pallas_call(body, out_shape=tuple(shapes), in_specs=[whole] * len(piec...]
    dot_general x33, matrix products: 83.4 us -> 69.8 us  [dot(): lax.dot_general(left, right, (((left_dim,), (right_dim,)), ((), ())), pre...]
    ppermute x125 -> x112, starting transfers between devices: 103 us -> 94.1 us  [swap(): return lax.ppermute(array, AXES, [(p, p ^ bit) for p in range(n_dev)])]
    concatenate x29 -> x8, local copies, waits for them, and re-layouts: 10.5 us -> 1.97 us  [the longest x1 1.89 us: layer_rows(): return jnp.concatenate(vectors + [lex_row] + inner_vectors, axis=0)]
    convert_element_type x25 -> x20, other arithmetic: 14.9 us -> 6.61 us  [the longest x6 2.42 us: middle(): total = (self.keep.astype(F32) + self.came.astype(F32)).astype(BF)]
    unnamed x412 -> x318, local copies, waits for them, and re-layouts: 18.4 us -> 17.5 us
  transfers between devices with their start and end apart: 129 -> 112, of which waited for: 53 -> 53; matrix products, arithmetic and copies ran while one was open for 24% -> 14% of each run, Pallas kernels for 8% -> 10%
where the time goes in v2:
time: 595 us; the launch traced here: 585 us
  waiting for transfers between devices  262 us (44%)
  starting transfers between devices  94.1 us (16%)
  matrix products  71.3 us (12%)
  Pallas kernels  68.4 us (11%)
  other arithmetic  55.4 us (9%)
  local copies, waits for them, and re-layouts  28.7 us (5%)
    ppermute x112, waiting for transfers between devices, swap(): return lax.ppermute(array, AXES, [(p, p ^ bit) for p in range(n_dev)])  262 us
    ppermute x112, starting transfers between devices, swap(): return lax.ppermute(array, AXES, [(p, p ^ bit) for p in range(n_dev)])  94.1 us
    dot_general x33, matrix products, dot(): lax.dot_general(left, right, (((left_dim,), (right_dim,)), ((), ())), pre...  69.8 us
    pallas_call x2, Pallas kernels, attend_back(): pl.pallas_call(functools.partial(attend_back_kernel, 256), out_shape=jax....  21.9 us
    pallas_call x2, Pallas kernels, attend(): pl.pallas_call(functools.partial(attend_kernel, 256), out_shape=(jax.Shap...  20.4 us
    pallas_call x6, Pallas kernels, place(): pl.pallas_call(body, out_shape=tuple(shapes), in_specs=[whole] * len(piec...  17.7 us
    unnamed x318, local copies, waits for them, and re-layouts  17.5 us
  transfers between devices with their start and end apart: 112, of which 53 were waited for; matrix products, arithmetic and copies ran while one was open for 14% of the time, Pallas kernels for 10%

profile of v2, /device:TPU:0, one launch (start us, length us, event | category | flops | bytes accessed | tf_op | source)
XLA Modules:
  0.0 584.6 jit_solution(13896120767827142684)
XLA Ops:
  12.5 2.8 collective-permute-start.5
  19.8 6.2 %collective-permute-done.5 = bf16[144,768]{1,0:T(8,128)(2,1)S(1)} collective-permute-done((bf16[144,768]{1,0:T(8,128)(2,1)}, bf16[144,768]{1,0:T(8,128)(2,1)S(1)}, u32[]{:S(2)}, u32[]{:S(2)}) %collective-permute-start.5) | collective-permute-done | bytes 221216 | tf_op jit(solution)/shard_map/ppermute | solution.py:316
  29.6 3.5 collective-permute-done.11.refs_3_
  40.1 6.1 %collective-permute-done.13 = bf16[128,1024]{1,0:T(8,128)(2,1)S(1)} collective-permute-done((bf16[128,1024]{1,0:T(8,128)(2,1)}, bf16[128,1024]{1,0:T(8,128)(2,1)S(1)}, u32[]{:S(2)}, u32[]{:S(2)}) %collective-permute-start.13) | collective-permute-done | bytes 262176 | tf_op jit(solution)/shard_map/ppermute | solution.py:316
  53.5 7.0 %collective-permute-done.14 = bf16[128,1024]{1,0:T(8,128)(2,1)S(1)} collective-permute-done((bf16[128,1024]{1,0:T(8,128)(2,1)S(1)}, bf16[128,1024]{1,0:T(8,128)(2,1)S(1)}, u32[]{:S(2)}, u32[]{:S(2)}) %collective-permute-start.14) | collective-permute-done | bytes 262176 | tf_op jit(solution)/shard_map/ppermute | solution.py:316
  60.5 4.0 collective-permute-done.12
  68.0 2.8 shard_map.379
  71.7 3.8 add_convert_fusion.1.qkv_ref
  75.5 10.2 %shard_map.380 = (bf16[768,256]{1,0:T(8,128)(2,1)}, f32[4,768]{1,0:T(4,128)}, f32[4,768]{1,0:T(4,128)}) custom-call(bf16[768,768]{1,0:T(8,128)(2,1)} %add_convert_fusion.1.qkv_ref, s32[768,1]{1,0:T(8,128)} %broadcast_in_dim.145.col_ref, s32[1,768]{1,0:T(1,128)} %broadcast_in_dim.129.row_ref), custom_call_target="tpu_custom_call" | custom-call | flops 6039797760 | bytes 3145728 | tf_op jit(solution)/shard_map/pallas_call | solution.py:108
  94.3 12.0 %collective-permute-done.21 = bf16[128,1024]{1,0:T(8,128)(2,1)S(1)} collective-permute-done((bf16[128,1024]{1,0:T(8,128)(2,1)S(1)}, bf16[128,1024]{1,0:T(8,128)(2,1)S(1)}, u32[]{:S(2)}, u32[]{:S(2)}) %collective-permute-start.21) | collective-permute-done | bytes 262176 | tf_op jit(solution)/shard_map/ppermute | solution.py:316
  109.0 3.0 shard_map.381
  112.0 7.5 %collective-permute-done.22 = bf16[192,1024]{1,0:T(8,128)(2,1)S(1)} collective-permute-done((bf16[192,1024]{1,0:T(8,128)(2,1)S(1)}, bf16[192,1024]{1,0:T(8,128)(2,1)S(1)}, u32[]{:S(2)}, u32[]{:S(2)}) %collective-permute-start.22) | collective-permute-done | bytes 393248 | tf_op jit(solution)/shard_map/ppermute | solution.py:316
  125.2 6.8 %multiply_convert_fusion.1 = (bf16[768,1024]{1,0:T(8,128)(2,1)}, f32[768,1024]{1,0:T(8,128)}) fusion(f32[1024]{0:T(1024)S(1)} %bitcast.795, bf16[1024,1024]{1,0:T(8,128)(2,1)} %shard_map.381, bf16[384,1024]{1,0:T(8,128)(2,1)S(1)} %collective-permute-done.25, bf16[192,1024]{1,0:T(8,128)(2,1)S(1)} %collective-permute-done.22, bf16[192,1024]{1,0:T(8,128)(2,1)S(1)} %fusion.37), kind=kOutput, calls=%fused_computation.18 | convolution fusion | flops 1620049920 | bytes 8392704 | tf_op jit(solution)/shard_map/dot_general | solution.py:22
  134.5 4.1 collective-permute-done.26.refs_3_
  139.4 3.2 shard_map.382
  142.6 2.7 convolution_convert_fusion.13
  149.9 12.9 %collective-permute-done.32 = bf16[128,1024]{1,0:T(8,128)(2,1)S(1)} collective-permute-done((bf16[128,1024]{1,0:T(8,128)(2,1)S(1)}, bf16[128,1024]{1,0:T(8,128)(2,1)S(1)}, u32[]{:S(2)}, u32[]{:S(2)}) %collective-permute-start.32) | collective-permute-done | bytes 262176 | tf_op jit(solution)/shard_map/ppermute | solution.py:316
  167.4 9.6 %collective-permute-done.36 = bf16[128,1024]{1,0:T(8,128)(2,1)S(1)} collective-permute-done((bf16[128,1024]{1,0:T(8,128)(2,1)S(1)}, bf16[128,1024]{1,0:T(8,128)(2,1)S(1)}, u32[]{:S(2)}, u32[]{:S(2)}) %collective-permute-start.36) | collective-permute-done | bytes 262176 | tf_op jit(solution)/shard_map/ppermute | solution.py:316
  177.0 2.9 collective-permute-done.35
  187.1 4.1 add_convert_fusion.qkv_ref
  191.2 10.2 %shard_map.384 = (bf16[768,256]{1,0:T(8,128)(2,1)}, f32[4,768]{1,0:T(4,128)}, f32[4,768]{1,0:T(4,128)}) custom-call(bf16[768,768]{1,0:T(8,128)(2,1)} %add_convert_fusion.qkv_ref, s32[768,1]{1,0:T(8,128)} %broadcast_in_dim.145.col_ref, s32[1,768]{1,0:T(1,128)} %broadcast_in_dim.129.row_ref), custom_call_target="tpu_custom_call" | custom-call | flops 6039797760 | bytes 3145728 | tf_op jit(solution)/shard_map/pallas_call | solution.py:108
  210.0 13.4 %collective-permute-done.44 = bf16[128,1024]{1,0:T(8,128)(2,1)S(1)} collective-permute-done((bf16[128,1024]{1,0:T(8,128)(2,1)S(1)}, bf16[128,1024]{1,0:T(8,128)(2,1)S(1)}, u32[]{:S(2)}, u32[]{:S(2)}) %collective-permute-start.44) | collective-permute-done | bytes 262176 | tf_op jit(solution)/shard_map/ppermute | solution.py:316
  226.5 3.0 shard_map.385
  229.5 7.3 %collective-permute-done.45 = bf16[192,1024]{1,0:T(8,128)(2,1)S(1)} collective-permute-done((bf16[192,1024]{1,0:T(8,128)(2,1)S(1)}, bf16[192,1024]{1,0:T(8,128)(2,1)S(1)}, u32[]{:S(2)}, u32[]{:S(2)}) %collective-permute-start.45) | collective-permute-done | bytes 393248 | tf_op jit(solution)/shard_map/ppermute | solution.py:316
  240.2 6.9 %multiply_convert_fusion = (bf16[768,1024]{1,0:T(8,128)(2,1)}, f32[768,1024]{1,0:T(8,128)}) fusion(f32[1024]{0:T(1024)S(1)} %bitcast.797, bf16[1024,1024]{1,0:T(8,128)(2,1)} %shard_map.385, bf16[384,1024]{1,0:T(8,128)(2,1)S(1)} %collective-permute-done.48, bf16[192,1024]{1,0:T(8,128)(2,1)S(1)} %collective-permute-done.45, bf16[192,1024]{1,0:T(8,128)(2,1)S(1)} %fusion.39), kind=kOutput, calls=%fused_computation.16 | convolution fusion | flops 1620049920 | bytes 8392704 | tf_op jit(solution)/shard_map/dot_general | solution.py:22
  247.1 5.1 collective-permute-done.49.refs_3_
  253.1 3.1 shard_map.386
  256.2 2.7 convolution_convert_fusion.12
  264.6 11.1 %collective-permute-done.51 = bf16[192,1024]{1,0:T(8,128)(2,1)} collective-permute-done((bf16[192,1024]{1,0:T(8,128)(2,1)}, bf16[192,1024]{1,0:T(8,128)(2,1)}, u32[]{:S(2)}, u32[]{:S(2)}) %collective-permute-start.51) | collective-permute-done | bytes 393248 | tf_op jit(solution)/shard_map/ppermute | solution.py:316
  281.5 10.0 %collective-permute-done.52 = bf16[192,1024]{1,0:T(8,128)(2,1)S(1)} collective-permute-done((bf16[192,1024]{1,0:T(8,128)(2,1)S(1)}, bf16[192,1024]{1,0:T(8,128)(2,1)S(1)}, u32[]{:S(2)}, u32[]{:S(2)}) %collective-permute-start.52) | collective-permute-done | bytes 393248 | tf_op jit(solution)/shard_map/ppermute | solution.py:316
  297.6 3.8 convolution_convert_fusion.3
  303.2 3.8 convert_reduce_fusion
  314.0 8.7 %collective-permute-done.56 = bf16[2,128,1024]{2,1,0:T(8,128)(2,1)S(1)} collective-permute-done((bf16[2,128,1024]{2,1,0:T(8,128)(2,1)S(1)}, bf16[2,128,1024]{2,1,0:T(8,128)(2,1)S(1)}, u32[]{:S(2)}, u32[]{:S(2)}) %collective-permute-start.56) | collective-permute-done | bytes 524320 | tf_op jit(solution)/shard_map/ppermute | solution.py:316
  330.3 9.2 %collective-permute-done.57 = bf16[192,1024]{1,0:T(8,128)(2,1)S(1)} collective-permute-done((bf16[192,1024]{1,0:T(8,128)(2,1)S(1)}, bf16[192,1024]{1,0:T(8,128)(2,1)S(1)}, u32[]{:S(2)}, u32[]{:S(2)}) %collective-permute-start.57) | collective-permute-done | bytes 393248 | tf_op jit(solution)/shard_map/ppermute | solution.py:316
  348.9 11.1 %shard_map.387 = bf16[768,768]{1,0:T(8,128)(2,1)} custom-call(bf16[768,768]{1,0:T(8,128)(2,1)} %add_convert_fusion.qkv_ref, s32[768,1]{1,0:T(8,128)} %broadcast_in_dim.145.col_ref, s32[1,768]{1,0:T(1,128)} %broadcast_in_dim.129.row_ref, f32[4,768]{1,0:T(4,128)} %get-tuple-element.310.max_ref, f32[4,768]{1,0:T(4,128)} %get-tuple-element.311.sum_ref, ...), custom_call_target="tpu_custom_call" | custom-call | flops 6039797760 | bytes 3145728 | tf_op jit(solution)/shard_map/pallas_call | solution.py:127
  371.8 7.6 %collective-permute-done.66 = bf16[2,128,1024]{2,1,0:T(8,128)(2,1)S(1)} collective-permute-done((bf16[2,128,1024]{2,1,0:T(8,128)(2,1)S(1)}, bf16[2,128,1024]{2,1,0:T(8,128)(2,1)S(1)}, u32[]{:S(2)}, u32[]{:S(2)}) %collective-permute-start.66) | collective-permute-done | bytes 524320 | tf_op jit(solution)/shard_map/ppermute | solution.py:316
  387.8 10.2 %collective-permute-done.68 = bf16[128,1024]{1,0:T(8,128)(2,1)S(1)} collective-permute-done((bf16[128,1024]{1,0:T(8,128)(2,1)S(1)}, bf16[128,1024]{1,0:T(8,128)(2,1)S(1)}, u32[]{:S(2)}, u32[]{:S(2)}) %collective-permute-start.68) | collective-permute-done | bytes 262176 | tf_op jit(solution)/shard_map/ppermute | solution.py:316
  406.0 4.6 convert_reduce_fusion.1
  418.9 6.8 %collective-permute-done.77 = bf16[2,128,1024]{2,1,0:T(8,128)(2,1)S(1)} collective-permute-done((bf16[2,128,1024]{2,1,0:T(8,128)(2,1)S(1)}, bf16[2,128,1024]{2,1,0:T(8,128)(2,1)S(1)}, u32[]{:S(2)}, u32[]{:S(2)}) %collective-permute-start.77) | collective-permute-done | bytes 524320 | tf_op jit(solution)/shard_map/ppermute | solution.py:316
  438.8 7.3 %collective-permute-done.79 = bf16[128,1024]{1,0:T(8,128)(2,1)} collective-permute-done((bf16[128,1024]{1,0:T(8,128)(2,1)}, bf16[128,1024]{1,0:T(8,128)(2,1)}, u32[]{:S(2)}, u32[]{:S(2)}) %collective-permute-start.79) | collective-permute-done | bytes 262176 | tf_op jit(solution)/shard_map/ppermute | solution.py:316
  459.7 10.8 %shard_map.388 = bf16[768,768]{1,0:T(8,128)(2,1)} custom-call(bf16[768,768]{1,0:T(8,128)(2,1)} %add_convert_fusion.1.qkv_ref, s32[768,1]{1,0:T(8,128)} %broadcast_in_dim.145.col_ref, s32[1,768]{1,0:T(1,128)} %broadcast_in_dim.129.row_ref, f32[4,768]{1,0:T(4,128)} %get-tuple-element.335.max_ref, f32[4,768]{1,0:T(4,128)} %get-tuple-element.336.sum_ref, ...), custom_call_target="tpu_custom_call" | custom-call | flops 6039797760 | bytes 3145728 | tf_op jit(solution)/shard_map/pallas_call | solution.py:127
  486.7 13.4 %collective-permute-done.86 = bf16[128,1024]{1,0:T(8,128)(2,1)S(1)} collective-permute-done((bf16[128,1024]{1,0:T(8,128)(2,1)S(1)}, bf16[128,1024]{1,0:T(8,128)(2,1)S(1)}, u32[]{:S(2)}, u32[]{:S(2)}) %collective-permute-start.86) | collective-permute-done | bytes 262176 | tf_op jit(solution)/shard_map/ppermute | solution.py:316
  505.0 12.5 %collective-permute-done.94 = f32[23,256]{1,0:T(8,128)S(1)} collective-permute-done((f32[23,256]{1,0:T(8,128)S(1)}, f32[23,256]{1,0:T(8,128)S(1)}, u32[]{:S(2)}, u32[]{:S(2)}) %collective-permute-start.94) | collective-permute-done | bytes 23584 | tf_op jit(solution)/shard_map/ppermute | solution.py:316
  521.9 8.7 %collective-permute-done.97 = f32[23,128]{1,0:T(8,128)S(1)} collective-permute-done((f32[23,128]{1,0:T(8,128)S(1)}, f32[23,128]{1,0:T(8,128)S(1)}, u32[]{:S(2)}, u32[]{:S(2)}) %collective-permute-start.97) | collective-permute-done | bytes 11808 | tf_op jit(solution)/shard_map/ppermute | solution.py:316
  530.6 3.4 collective-permute-done.95
  541.6 8.5 %collective-permute-done.99 = bf16[2,128,1024]{2,1,0:T(8,128)(2,1)S(1)} collective-permute-done((bf16[2,128,1024]{2,1,0:T(8,128)(2,1)S(1)}, bf16[2,128,1024]{2,1,0:T(8,128)(2,1)S(1)}, u32[]{:S(2)}, u32[]{:S(2)}) %collective-permute-start.99) | collective-permute-done | bytes 524320 | tf_op jit(solution)/shard_map/ppermute | solution.py:316
  556.5 3.0 collective-permute-done.106
  559.5 8.7 %collective-permute-done.103 = bf16[128,1024]{1,0:T(8,128)(2,1)S(1)} collective-permute-done((bf16[128,1024]{1,0:T(8,128)(2,1)S(1)}, bf16[128,1024]{1,0:T(8,128)(2,1)S(1)}, u32[]{:S(2)}, u32[]{:S(2)}) %collective-permute-start.103) | collective-permute-done | bytes 262176 | tf_op jit(solution)/shard_map/ppermute | solution.py:316
  (761 shorter events, 250.1 us)
Async XLA Ops:
  5.7 22.2 %collective-permute-start = (bf16[192,1024]{1,0:T(8,128)(2,1)}, bf16[192,1024]{1,0:T(8,128)(2,1)S(1)}, u32[]{:S(2)}, u32[]{:S(2)}) collective-permute-start(bf16[192,1024]{1,0:T(8,128)(2,1)} %param.26), channel_id=1, source_target_pairs={{0,2},{1,3},{2,0},{3,1},{4,6},{5,7},{6,4},{7,5},{8,10},{9,11},{10,... | collective-permute-start | bytes 1179656 | tf_op jit(solution)/shard_map/ppermute | solution.py:316
  18.9 14.2 %collective-permute-start.11 = (bf16[32,4864]{1,0:T(8,128)(2,1)}, bf16[32,4864]{1,0:T(8,128)(2,1)S(1)}, u32[]{:S(2)}, u32[]{:S(2)}) collective-permute-start(bf16[32,4864]{1,0:T(8,128)(2,1)} %get-tuple-element.235), channel_id=1, source_target_pairs={{0,3},{1,2},{2,1},{3,0},{4,7},{5,6},{6,5},{7,4},{8,11},{9,10},{10,... | collective-permute-start | bytes 933896 | tf_op jit(solution)/shard_map/ppermute | solution.py:316
  19.0 14.1 %collective-permute-start.9 = (bf16[32,4864]{1,0:T(8,128)(2,1)}, bf16[32,4864]{1,0:T(8,128)(2,1)S(1)}, u32[]{:S(2)}, u32[]{:S(2)}) collective-permute-start(bf16[32,4864]{1,0:T(8,128)(2,1)} %get-tuple-element.231), channel_id=1, source_target_pairs={{0,1},{1,0},{2,3},{3,2},{4,5},{5,4},{6,7},{7,6},{8,9},{9,8},{10,11... | collective-permute-start | bytes 933896 | tf_op jit(solution)/shard_map/ppermute | solution.py:316
  27.0 19.2 %collective-permute-start.6 = (bf16[288,768]{1,0:T(8,128)(2,1)S(1)}, bf16[288,768]{1,0:T(8,128)(2,1)}, u32[]{:S(2)}, u32[]{:S(2)}) collective-permute-start(bf16[288,768]{1,0:T(8,128)(2,1)S(1)} %pad_maximum_fusion.36.refs_0_), channel_id=1, source_target_pairs={{0,8},{1,9},{2,10},{3,11},{4,12},{5,13},{6,14},{7,15},{8,0},{9,1},... | collective-permute-start | bytes 1327112 | tf_op jit(solution)/shard_map/ppermute | solution.py:316
  27.9 18.3 %collective-permute-start.7 = (bf16[288,768]{1,0:T(8,128)(2,1)S(1)}, bf16[288,768]{1,0:T(8,128)(2,1)S(1)}, u32[]{:S(2)}, u32[]{:S(2)}) collective-permute-start(bf16[288,768]{1,0:T(8,128)(2,1)S(1)} %pad_maximum_fusion.36.refs_0_), channel_id=1, source_target_pairs={{0,4},{1,5},{2,6},{3,7},{4,0},{5,1},{6,2},{7,3},{8,12},{9,13},{10,... | collective-permute-start | bytes 1327112 | tf_op jit(solution)/shard_map/ppermute | solution.py:316
  29.5 23.8 %collective-permute-start.1 = (bf16[384,1024]{1,0:T(8,128)(2,1)S(1)}, bf16[384,1024]{1,0:T(8,128)(2,1)S(1)}, u32[]{:S(2)}, u32[]{:S(2)}) collective-permute-start(bf16[384,1024]{1,0:T(8,128)(2,1)S(1)} %pad_maximum_fusion.10), channel_id=1, source_target_pairs={{0,1},{1,0},{2,3},{3,2},{4,5},{5,4},{6,7},{7,6},{8,9},{9,8},{10,11... | collective-permute-start | bytes 2359304 | tf_op jit(solution)/shard_map/ppermute | solution.py:316
  46.9 17.6 %collective-permute-start.8 = (bf16[288,768]{1,0:T(8,128)(2,1)}, bf16[288,768]{1,0:T(8,128)(2,1)S(1)}, u32[]{:S(2)}, u32[]{:S(2)}) collective-permute-start(bf16[288,768]{1,0:T(8,128)(2,1)} %collective-permute-done.6.refs_1_), channel_id=1, source_target_pairs={{0,4},{1,5},{2,6},{3,7},{4,0},{5,1},{6,2},{7,3},{8,12},{9,13},{10,... | collective-permute-start | bytes 1327112 | tf_op jit(solution)/shard_map/ppermute | solution.py:316
  64.6 21.1 %collective-permute-start.15 = (bf16[256,1024]{1,0:T(8,128)(2,1)S(1)}, bf16[256,1024]{1,0:T(8,128)(2,1)S(1)}, u32[]{:S(2)}, u32[]{:S(2)}) collective-permute-start(bf16[256,1024]{1,0:T(8,128)(2,1)S(1)} %constant_dynamic-update-slice_fusion.refs_0_), channel_id=1, source_target_pairs={{0,8},{1,9},{2,10},{3,11},{4,12},{5,13},{6,14},{7,15},{8,0},{9,1},... | collective-permute-start | bytes 1572872 | tf_op jit(solution)/shard_map/ppermute | solution.py:316
  64.7 21.0 %collective-permute-start.16 = (bf16[256,1024]{1,0:T(8,128)(2,1)S(1)}, bf16[256,1024]{1,0:T(8,128)(2,1)S(1)}, u32[]{:S(2)}, u32[]{:S(2)}) collective-permute-start(bf16[256,1024]{1,0:T(8,128)(2,1)S(1)} %constant_dynamic-update-slice_fusion.refs_0_), channel_id=1, source_target_pairs={{0,4},{1,5},{2,6},{3,7},{4,0},{5,1},{6,2},{7,3},{8,12},{9,13},{10,... | collective-permute-start | bytes 1572872 | tf_op jit(solution)/shard_map/ppermute | solution.py:316
  66.2 19.5 %collective-permute-start.17 = (bf16[128,1024]{1,0:T(8,128)(2,1)S(1)}, bf16[128,1024]{1,0:T(8,128)(2,1)S(1)}, u32[]{:S(2)}, u32[]{:S(2)}) collective-permute-start(bf16[128,1024]{1,0:T(8,128)(2,1)S(1)} %broadcast_select_fusion.5), channel_id=1, source_target_pairs={{0,16},{1,17},{2,18},{3,19},{4,20},{5,21},{6,22},{7,23},{8,24},{9,... | collective-permute-start | bytes 786440 | tf_op jit(solution)/shard_map/ppermute | solution.py:316
  87.4 19.0 %collective-permute-start.20 = (bf16[256,1024]{1,0:T(8,128)(2,1)S(1)}, bf16[256,1024]{1,0:T(8,128)(2,1)S(1)}, u32[]{:S(2)}, u32[]{:S(2)}) collective-permute-start(bf16[256,1024]{1,0:T(8,128)(2,1)S(1)} %collective-permute-done.15.refs_1_), channel_id=1, source_target_pairs={{0,4},{1,5},{2,6},{3,7},{4,0},{5,1},{6,2},{7,3},{8,12},{9,13},{10,... | collective-permute-start | bytes 1572872 | tf_op jit(solution)/shard_map/ppermute | solution.py:316
  90.1 16.3 %collective-permute-start.19 = (bf16[192,1024]{1,0:T(8,128)(2,1)S(1)}, bf16[192,1024]{1,0:T(8,128)(2,1)S(1)}, u32[]{:S(2)}, u32[]{:S(2)}) collective-permute-start(bf16[192,1024]{1,0:T(8,128)(2,1)S(1)} %slice.2399), channel_id=1, source_target_pairs={{0,2},{1,3},{2,0},{3,1},{4,6},{5,7},{6,4},{7,5},{8,10},{9,11},{10,... | collective-permute-start | bytes 1179656 | tf_op jit(solution)/shard_map/ppermute | solution.py:316
  92.0 14.3 %collective-permute-start.21 = (bf16[128,1024]{1,0:T(8,128)(2,1)S(1)}, bf16[128,1024]{1,0:T(8,128)(2,1)S(1)}, u32[]{:S(2)}, u32[]{:S(2)}) collective-permute-start(bf16[128,1024]{1,0:T(8,128)(2,1)S(1)} %get-tuple-element.255), channel_id=1, source_target_pairs={{0,16},{1,17},{2,18},{3,19},{4,20},{5,21},{6,22},{7,23},{8,24},{9,... | collective-permute-start | bytes 786440 | tf_op jit(solution)/shard_map/ppermute | solution.py:316
  145.5 17.3 %collective-permute-start.30 = (bf16[256,768]{1,0:T(8,128)(2,1)S(1)}, bf16[256,768]{1,0:T(8,128)(2,1)S(1)}, u32[]{:S(2)}, u32[]{:S(2)}) collective-permute-start(bf16[256,768]{1,0:T(8,128)(2,1)S(1)} %constant_dynamic-update-slice_fusion.2.refs_0_), channel_id=1, source_target_pairs={{0,8},{1,9},{2,10},{3,11},{4,12},{5,13},{6,14},{7,15},{8,0},{9,1},... | collective-permute-start | bytes 1179656 | tf_op jit(solution)/shard_map/ppermute | solution.py:316
  145.8 16.9 %collective-permute-start.31 = (bf16[256,768]{1,0:T(8,128)(2,1)S(1)}, bf16[256,768]{1,0:T(8,128)(2,1)S(1)}, u32[]{:S(2)}, u32[]{:S(2)}) collective-permute-start(bf16[256,768]{1,0:T(8,128)(2,1)S(1)} %constant_dynamic-update-slice_fusion.2.refs_0_), channel_id=1, source_target_pairs={{0,4},{1,5},{2,6},{3,7},{4,0},{5,1},{6,2},{7,3},{8,12},{9,13},{10,... | collective-permute-start | bytes 1179656 | tf_op jit(solution)/shard_map/ppermute | solution.py:316
  163.2 16.8 %collective-permute-start.34 = (bf16[256,768]{1,0:T(8,128)(2,1)S(1)}, bf16[256,768]{1,0:T(8,128)(2,1)S(1)}, u32[]{:S(2)}, u32[]{:S(2)}) collective-permute-start(bf16[256,768]{1,0:T(8,128)(2,1)S(1)} %collective-permute-done.30.refs_1_), channel_id=1, source_target_pairs={{0,4},{1,5},{2,6},{3,7},{4,0},{5,1},{6,2},{7,3},{8,12},{9,13},{10,... | collective-permute-start | bytes 1179656 | tf_op jit(solution)/shard_map/ppermute | solution.py:316
  164.4 15.5 %collective-permute-start.33 = (bf16[192,1024]{1,0:T(8,128)(2,1)S(1)}, bf16[192,1024]{1,0:T(8,128)(2,1)S(1)}, u32[]{:S(2)}, u32[]{:S(2)}) collective-permute-start(bf16[192,1024]{1,0:T(8,128)(2,1)S(1)} %fusion.38), channel_id=1, source_target_pairs={{0,2},{1,3},{2,0},{3,1},{4,6},{5,7},{6,4},{7,5},{8,10},{9,11},{10,... | collective-permute-start | bytes 1179656 | tf_op jit(solution)/shard_map/ppermute | solution.py:316
  183.4 19.5 %collective-permute-start.39 = (bf16[256,1024]{1,0:T(8,128)(2,1)S(1)}, bf16[256,1024]{1,0:T(8,128)(2,1)S(1)}, u32[]{:S(2)}, u32[]{:S(2)}) collective-permute-start(bf16[256,1024]{1,0:T(8,128)(2,1)S(1)} %constant_dynamic-update-slice_fusion.4.refs_0_), channel_id=1, source_target_pairs={{0,8},{1,9},{2,10},{3,11},{4,12},{5,13},{6,14},{7,15},{8,0},{9,1},... | collective-permute-start | bytes 1572872 | tf_op jit(solution)/shard_map/ppermute | solution.py:316
  183.4 19.4 %collective-permute-start.40 = (bf16[256,1024]{1,0:T(8,128)(2,1)S(1)}, bf16[256,1024]{1,0:T(8,128)(2,1)S(1)}, u32[]{:S(2)}, u32[]{:S(2)}) collective-permute-start(bf16[256,1024]{1,0:T(8,128)(2,1)S(1)} %constant_dynamic-update-slice_fusion.4.refs_0_), channel_id=1, source_target_pairs={{0,4},{1,5},{2,6},{3,7},{4,0},{5,1},{6,2},{7,3},{8,12},{9,13},{10,... | collective-permute-start | bytes 1572872 | tf_op jit(solution)/shard_map/ppermute | solution.py:316
  185.0 16.5 %collective-permute-start.38 = (bf16[128,1024]{1,0:T(8,128)(2,1)S(1)}, bf16[128,1024]{1,0:T(8,128)(2,1)S(1)}, u32[]{:S(2)}, u32[]{:S(2)}) collective-permute-start(bf16[128,1024]{1,0:T(8,128)(2,1)S(1)} %broadcast_select_fusion.4), channel_id=1, source_target_pairs={{0,16},{1,17},{2,18},{3,19},{4,20},{5,21},{6,22},{7,23},{8,24},{9,... | collective-permute-start | bytes 786440 | tf_op jit(solution)/shard_map/ppermute | solution.py:316
  204.4 19.0 %collective-permute-start.43 = (bf16[256,1024]{1,0:T(8,128)(2,1)S(1)}, bf16[256,1024]{1,0:T(8,128)(2,1)S(1)}, u32[]{:S(2)}, u32[]{:S(2)}) collective-permute-start(bf16[256,1024]{1,0:T(8,128)(2,1)S(1)} %collective-permute-done.39.refs_1_), channel_id=1, source_target_pairs={{0,4},{1,5},{2,6},{3,7},{4,0},{5,1},{6,2},{7,3},{8,12},{9,13},{10,... | collective-permute-start | bytes 1572872 | tf_op jit(solution)/shard_map/ppermute | solution.py:316
  207.1 16.3 %collective-permute-start.42 = (bf16[192,1024]{1,0:T(8,128)(2,1)S(1)}, bf16[192,1024]{1,0:T(8,128)(2,1)S(1)}, u32[]{:S(2)}, u32[]{:S(2)}) collective-permute-start(bf16[192,1024]{1,0:T(8,128)(2,1)S(1)} %slice.2397), channel_id=1, source_target_pairs={{0,2},{1,3},{2,0},{3,1},{4,6},{5,7},{6,4},{7,5},{8,10},{9,11},{10,... | collective-permute-start | bytes 1179656 | tf_op jit(solution)/shard_map/ppermute | solution.py:316
  208.8 14.6 %collective-permute-start.44 = (bf16[128,1024]{1,0:T(8,128)(2,1)S(1)}, bf16[128,1024]{1,0:T(8,128)(2,1)S(1)}, u32[]{:S(2)}, u32[]{:S(2)}) collective-permute-start(bf16[128,1024]{1,0:T(8,128)(2,1)S(1)} %get-tuple-element.295), channel_id=1, source_target_pairs={{0,16},{1,17},{2,18},{3,19},{4,20},{5,21},{6,22},{7,23},{8,24},{9,... | collective-permute-start | bytes 786440 | tf_op jit(solution)/shard_map/ppermute | solution.py:316
  237.9 14.3 %collective-permute-start.49 = (bf16[256,1024]{1,0:T(8,128)(2,1)S(1)}, bf16[256,1024]{1,0:T(8,128)(2,1)S(1)}, u32[]{:S(2)}, u32[]{:S(2)}) collective-permute-start(bf16[256,1024]{1,0:T(8,128)(2,1)S(1)} %collective-permute-done.46.refs_1_), channel_id=1, source_target_pairs={{0,4},{1,5},{2,6},{3,7},{4,0},{5,1},{6,2},{7,3},{8,12},{9,13},{10,... | collective-permute-start | bytes 1572872 | tf_op jit(solution)/shard_map/ppermute | solution.py:316
  324.1 15.4 %collective-permute-start.59 = (bf16[2,128,1024]{2,1,0:T(8,128)(2,1)S(1)}, bf16[2,128,1024]{2,1,0:T(8,128)(2,1)S(1)}, u32[]{:S(2)}, u32[]{:S(2)}) collective-permute-start(bf16[2,128,1024]{2,1,0:T(8,128)(2,1)S(1)} %select_bitcast_fusion.18), channel_id=1, source_target_pairs={{0,4},{1,5},{2,6},{3,7},{4,0},{5,1},{6,2},{7,3},{8,12},{9,13},{10,... | collective-permute-start | bytes 1572872 | tf_op jit(solution)/shard_map/ppermute | solution.py:316
  342.5 17.8 %collective-permute-start.62 = (bf16[2,128,1024]{2,1,0:T(8,128)(2,1)}, bf16[2,128,1024]{2,1,0:T(8,128)(2,1)S(1)}, u32[]{:S(2)}, u32[]{:S(2)}) collective-permute-start(bf16[2,128,1024]{2,1,0:T(8,128)(2,1)} %select_bitcast_fusion.17), channel_id=1, source_target_pairs={{0,4},{1,5},{2,6},{3,7},{4,0},{5,1},{6,2},{7,3},{8,12},{9,13},{10,... | collective-permute-start | bytes 1572872 | tf_op jit(solution)/shard_map/ppermute | solution.py:316
  343.0 17.3 %collective-permute-start.61 = (bf16[128,1024]{1,0:T(8,128)(2,1)}, bf16[128,1024]{1,0:T(8,128)(2,1)S(1)}, u32[]{:S(2)}, u32[]{:S(2)}) collective-permute-start(bf16[128,1024]{1,0:T(8,128)(2,1)} %select_bitcast_fusion.36), channel_id=1, source_target_pairs={{0,16},{1,17},{2,18},{3,19},{4,20},{5,21},{6,22},{7,23},{8,24},{9,... | collective-permute-start | bytes 786440 | tf_op jit(solution)/shard_map/ppermute | solution.py:316
  345.6 14.4 %collective-permute-start.69 = (bf16[256,256]{1,0:T(8,128)(2,1)S(1)}, bf16[256,256]{1,0:T(8,128)(2,1)S(1)}, u32[]{:S(2)}, u32[]{:S(2)}) collective-permute-start(bf16[256,256]{1,0:T(8,128)(2,1)S(1)} %get-tuple-element.525), channel_id=1, source_target_pairs={{0,3},{1,2},{2,1},{3,0},{4,7},{5,6},{6,5},{7,4},{8,11},{9,10},{10,... | collective-permute-start | bytes 393224 | tf_op jit(solution)/shard_map/ppermute | solution.py:316
  345.7 14.3 %collective-permute-start.70 = (bf16[256,256]{1,0:T(8,128)(2,1)S(1)}, bf16[256,256]{1,0:T(8,128)(2,1)S(1)}, u32[]{:S(2)}, u32[]{:S(2)}) collective-permute-start(bf16[256,256]{1,0:T(8,128)(2,1)S(1)} %get-tuple-element.450), channel_id=1, source_target_pairs={{0,2},{1,3},{2,0},{3,1},{4,6},{5,7},{6,4},{7,5},{8,10},{9,11},{10,... | collective-permute-start | bytes 393224 | tf_op jit(solution)/shard_map/ppermute | solution.py:316
  365.3 14.0 %collective-permute-start.66 = (bf16[2,128,1024]{2,1,0:T(8,128)(2,1)S(1)}, bf16[2,128,1024]{2,1,0:T(8,128)(2,1)S(1)}, u32[]{:S(2)}, u32[]{:S(2)}) collective-permute-start(bf16[2,128,1024]{2,1,0:T(8,128)(2,1)S(1)} %copy-done.47), channel_id=1, source_target_pairs={{0,4},{1,5},{2,6},{3,7},{4,0},{5,1},{6,2},{7,3},{8,12},{9,13},{10,... | collective-permute-start | bytes 1572872 | tf_op jit(solution)/shard_map/ppermute | solution.py:316
  382.5 15.5 %collective-permute-start.72 = (bf16[2,128,1024]{2,1,0:T(8,128)(2,1)S(1)}, bf16[2,128,1024]{2,1,0:T(8,128)(2,1)S(1)}, u32[]{:S(2)}, u32[]{:S(2)}) collective-permute-start(bf16[2,128,1024]{2,1,0:T(8,128)(2,1)S(1)} %pad_maximum_fusion.33), channel_id=1, source_target_pairs={{0,4},{1,5},{2,6},{3,7},{4,0},{5,1},{6,2},{7,3},{8,12},{9,13},{10,... | collective-permute-start | bytes 1572872 | tf_op jit(solution)/shard_map/ppermute | solution.py:316
  411.7 14.0 %collective-permute-start.77 = (bf16[2,128,1024]{2,1,0:T(8,128)(2,1)S(1)}, bf16[2,128,1024]{2,1,0:T(8,128)(2,1)S(1)}, u32[]{:S(2)}, u32[]{:S(2)}) collective-permute-start(bf16[2,128,1024]{2,1,0:T(8,128)(2,1)S(1)} %pad_maximum_fusion.34), channel_id=1, source_target_pairs={{0,4},{1,5},{2,6},{3,7},{4,0},{5,1},{6,2},{7,3},{8,12},{9,13},{10,... | collective-permute-start | bytes 1572872 | tf_op jit(solution)/shard_map/ppermute | solution.py:316
  429.3 17.1 %collective-permute-start.80 = (bf16[2,128,1024]{2,1,0:T(8,128)(2,1)}, bf16[2,128,1024]{2,1,0:T(8,128)(2,1)}, u32[]{:S(2)}, u32[]{:S(2)}) collective-permute-start(bf16[2,128,1024]{2,1,0:T(8,128)(2,1)} %select_bitcast_fusion.15), channel_id=1, source_target_pairs={{0,4},{1,5},{2,6},{3,7},{4,0},{5,1},{6,2},{7,3},{8,12},{9,13},{10,... | collective-permute-start | bytes 1572872 | tf_op jit(solution)/shard_map/ppermute | solution.py:316
  431.6 14.5 %collective-permute-start.79 = (bf16[128,1024]{1,0:T(8,128)(2,1)}, bf16[128,1024]{1,0:T(8,128)(2,1)}, u32[]{:S(2)}, u32[]{:S(2)}) collective-permute-start(bf16[128,1024]{1,0:T(8,128)(2,1)} %select_bitcast_fusion.32), channel_id=1, source_target_pairs={{0,16},{1,17},{2,18},{3,19},{4,20},{5,21},{6,22},{7,23},{8,24},{9,... | collective-permute-start | bytes 786440 | tf_op jit(solution)/shard_map/ppermute | solution.py:316
  452.0 20.2 %collective-permute-start.83 = (bf16[2,128,1024]{2,1,0:T(8,128)(2,1)S(1)}, bf16[2,128,1024]{2,1,0:T(8,128)(2,1)S(1)}, u32[]{:S(2)}, u32[]{:S(2)}) collective-permute-start(bf16[2,128,1024]{2,1,0:T(8,128)(2,1)S(1)} %copy-done.46), channel_id=1, source_target_pairs={{0,4},{1,5},{2,6},{3,7},{4,0},{5,1},{6,2},{7,3},{8,12},{9,13},{10,... | collective-permute-start | bytes 1572872 | tf_op jit(solution)/shard_map/ppermute | solution.py:316
  453.5 18.7 %collective-permute-start.82 = (bf16[2,128,1024]{2,1,0:T(8,128)(2,1)S(1)}, bf16[2,128,1024]{2,1,0:T(8,128)(2,1)S(1)}, u32[]{:S(2)}, u32[]{:S(2)}) collective-permute-start(bf16[2,128,1024]{2,1,0:T(8,128)(2,1)S(1)} %fusion.18), channel_id=1, source_target_pairs={{0,8},{1,9},{2,10},{3,11},{4,12},{5,13},{6,14},{7,15},{8,0},{9,1},... | collective-permute-start | bytes 1572872 | tf_op jit(solution)/shard_map/ppermute | solution.py:316
  455.3 15.2 %collective-permute-start.87 = (bf16[256,256]{1,0:T(8,128)(2,1)S(1)}, bf16[256,256]{1,0:T(8,128)(2,1)S(1)}, u32[]{:S(2)}, u32[]{:S(2)}) collective-permute-start(bf16[256,256]{1,0:T(8,128)(2,1)S(1)} %get-tuple-element.518), channel_id=1, source_target_pairs={{0,3},{1,2},{2,1},{3,0},{4,7},{5,6},{6,5},{7,4},{8,11},{9,10},{10,... | collective-permute-start | bytes 393224 | tf_op jit(solution)/shard_map/ppermute | solution.py:316
  455.7 14.8 %collective-permute-start.88 = (bf16[256,256]{1,0:T(8,128)(2,1)S(1)}, bf16[256,256]{1,0:T(8,128)(2,1)S(1)}, u32[]{:S(2)}, u32[]{:S(2)}) collective-permute-start(bf16[256,256]{1,0:T(8,128)(2,1)S(1)} %get-tuple-element.519), channel_id=1, source_target_pairs={{0,2},{1,3},{2,0},{3,1},{4,6},{5,7},{6,4},{7,5},{8,10},{9,11},{10,... | collective-permute-start | bytes 393224 | tf_op jit(solution)/shard_map/ppermute | solution.py:316
  482.3 17.7 %collective-permute-start.90 = (bf16[2,144,1024]{2,1,0:T(8,128)(2,1)S(1)}, bf16[2,144,1024]{2,1,0:T(8,128)(2,1)S(1)}, u32[]{:S(2)}, u32[]{:S(2)}) collective-permute-start(bf16[2,144,1024]{2,1,0:T(8,128)(2,1)S(1)} %pad_maximum_fusion.26), channel_id=1, source_target_pairs={{0,4},{1,5},{2,6},{3,7},{4,0},{5,1},{6,2},{7,3},{8,12},{9,13},{10,... | collective-permute-start | bytes 1769480 | tf_op jit(solution)/shard_map/ppermute | solution.py:316
  484.8 15.3 %collective-permute-start.85 = (bf16[192,1024]{1,0:T(8,128)(2,1)S(1)}, bf16[192,1024]{1,0:T(8,128)(2,1)S(1)}, u32[]{:S(2)}, u32[]{:S(2)}) collective-permute-start(bf16[192,1024]{1,0:T(8,128)(2,1)S(1)} %slice.2392), channel_id=1, source_target_pairs={{0,2},{1,3},{2,0},{3,1},{4,6},{5,7},{6,4},{7,5},{8,10},{9,11},{10,... | collective-permute-start | bytes 1179656 | tf_op jit(solution)/shard_map/ppermute | solution.py:316
  485.4 14.7 %collective-permute-start.86 = (bf16[128,1024]{1,0:T(8,128)(2,1)S(1)}, bf16[128,1024]{1,0:T(8,128)(2,1)S(1)}, u32[]{:S(2)}, u32[]{:S(2)}) collective-permute-start(bf16[128,1024]{1,0:T(8,128)(2,1)S(1)} %select_bitcast_fusion.31), channel_id=1, source_target_pairs={{0,16},{1,17},{2,18},{3,19},{4,20},{5,21},{6,22},{7,23},{8,24},{9,... | collective-permute-start | bytes 786440 | tf_op jit(solution)/shard_map/ppermute | solution.py:316
  501.0 16.5 %collective-permute-start.93 = (bf16[2,144,1024]{2,1,0:T(8,128)(2,1)S(1)}, bf16[2,144,1024]{2,1,0:T(8,128)(2,1)S(1)}, u32[]{:S(2)}, u32[]{:S(2)}) collective-permute-start(bf16[2,144,1024]{2,1,0:T(8,128)(2,1)S(1)} %pad_maximum_fusion.27), channel_id=1, source_target_pairs={{0,4},{1,5},{2,6},{3,7},{4,0},{5,1},{6,2},{7,3},{8,12},{9,13},{10,... | collective-permute-start | bytes 1769480 | tf_op jit(solution)/shard_map/ppermute | solution.py:316
  502.0 15.6 %collective-permute-start.92 = (bf16[2,144,1024]{2,1,0:T(8,128)(2,1)S(1)}, bf16[2,144,1024]{2,1,0:T(8,128)(2,1)S(1)}, u32[]{:S(2)}, u32[]{:S(2)}) collective-permute-start(bf16[2,144,1024]{2,1,0:T(8,128)(2,1)S(1)} %add_convert_fusion.3), channel_id=1, source_target_pairs={{0,8},{1,9},{2,10},{3,11},{4,12},{5,13},{6,14},{7,15},{8,0},{9,1},... | collective-permute-start | bytes 1769480 | tf_op jit(solution)/shard_map/ppermute | solution.py:316
  502.9 14.7 %collective-permute-start.94 = (f32[23,256]{1,0:T(8,128)S(1)}, f32[23,256]{1,0:T(8,128)S(1)}, u32[]{:S(2)}, u32[]{:S(2)}) collective-permute-start(f32[23,256]{1,0:T(8,128)S(1)} %slice_select_fusion.1), channel_id=1, source_target_pairs={{0,8},{1,9},{2,10},{3,11},{4,12},{5,13},{6,14},{7,15},{8,0},{9,1},... | collective-permute-start | bytes 70664 | tf_op jit(solution)/shard_map/ppermute | solution.py:316
  517.5 16.5 %collective-permute-start.96 = (bf16[2,128,1024]{2,1,0:T(8,128)(2,1)S(1)}, bf16[2,128,1024]{2,1,0:T(8,128)(2,1)S(1)}, u32[]{:S(2)}, u32[]{:S(2)}) collective-permute-start(bf16[2,128,1024]{2,1,0:T(8,128)(2,1)S(1)} %copy-done.45), channel_id=1, source_target_pairs={{0,4},{1,5},{2,6},{3,7},{4,0},{5,1},{6,2},{7,3},{8,12},{9,13},{10,... | collective-permute-start | bytes 1572872 | tf_op jit(solution)/shard_map/ppermute | solution.py:316
  519.2 14.8 %collective-permute-start.95 = (bf16[144,1024]{1,0:T(8,128)(2,1)S(1)}, bf16[144,1024]{1,0:T(8,128)(2,1)S(1)}, u32[]{:S(2)}, u32[]{:S(2)}) collective-permute-start(bf16[144,1024]{1,0:T(8,128)(2,1)S(1)} %select_bitcast_fusion.28), channel_id=1, source_target_pairs={{0,16},{1,17},{2,18},{3,19},{4,20},{5,21},{6,22},{7,23},{8,24},{9,... | collective-permute-start | bytes 884744 | tf_op jit(solution)/shard_map/ppermute | solution.py:316
  536.0 14.1 %collective-permute-start.99 = (bf16[2,128,1024]{2,1,0:T(8,128)(2,1)S(1)}, bf16[2,128,1024]{2,1,0:T(8,128)(2,1)S(1)}, u32[]{:S(2)}, u32[]{:S(2)}) collective-permute-start(bf16[2,128,1024]{2,1,0:T(8,128)(2,1)S(1)} %copy-done.44), channel_id=1, source_target_pairs={{0,4},{1,5},{2,6},{3,7},{4,0},{5,1},{6,2},{7,3},{8,12},{9,13},{10,... | collective-permute-start | bytes 1572872 | tf_op jit(solution)/shard_map/ppermute | solution.py:316
  553.6 14.7 %collective-permute-start.103 = (bf16[128,1024]{1,0:T(8,128)(2,1)S(1)}, bf16[128,1024]{1,0:T(8,128)(2,1)S(1)}, u32[]{:S(2)}, u32[]{:S(2)}) collective-permute-start(bf16[128,1024]{1,0:T(8,128)(2,1)S(1)} %select_bitcast_fusion.30), channel_id=1, source_target_pairs={{0,16},{1,17},{2,18},{3,19},{4,20},{5,21},{6,22},{7,23},{8,24},{9,... | collective-permute-start | bytes 786440 | tf_op jit(solution)/shard_map/ppermute | solution.py:316
  (187 other events, 1369.2 us)

commit v3 on v2

--- a/solution.py
+++ b/solution.py
@@ -106,7 +106,7 @@
     heads = width // HEAD
     whole = pl.BlockSpec(memory_space=pltpu.VMEM)
     return pl.pallas_call(
-        functools.partial(attend_kernel, 256),
+        functools.partial(attend_kernel, math.gcd(tokens, 768)),
         out_shape=(
             jax.ShapeDtypeStruct((tokens, width), BF),
             jax.ShapeDtypeStruct((heads, tokens), F32),
@@ -125,7 +125,7 @@
     tokens, width = grads.shape
     whole = pl.BlockSpec(memory_space=pltpu.VMEM)
     return pl.pallas_call(
-        functools.partial(attend_back_kernel, 256),
+        functools.partial(attend_back_kernel, math.gcd(tokens, 768)),
         out_shape=jax.ShapeDtypeStruct((tokens, 3 * width), BF),
         in_specs=[whole] * 6,
         out_specs=whole,
@@ -326,9 +326,10 @@
 
     z_lines = [[d for d in range(n_dp) if d % 2 == y] for y in range(2)]
 
-    seq_steps = [0]
-    for bit in reversed(seq_bits):
-        seq_steps = seq_steps + [s ^ bit for s in seq_steps]
+    x_steps = [0]
+    for bit in reversed(seq_bits[1:]):
+        x_steps = x_steps + [s ^ bit for s in x_steps]
+    seq_steps = [step ^ core for step in x_steps for core in (0, 1)]
 
     def spread(piece, bits):
         pieces, steps = [piece], [0]
@@ -346,32 +347,47 @@
     def settle(array, moving):
         if not moving:
             return array
-        out = lax.optimization_barrier((array,) + tuple(m[2] for m in moving))
-        for (home, name, _), value in zip(moving, out[1:]):
+        arrays = tuple(array) if isinstance(array, (tuple, list)) else (array,)
+        out = lax.optimization_barrier(arrays + tuple(m[2] for m in moving))
+        for (home, name, _), value in zip(moving, out[len(arrays) :]):
             setattr(home, name, value)
-        return out[0]
+        return list(out[: len(arrays)]) if isinstance(array, (tuple, list)) else out[0]
 
     def gather_seq(rows, moves=(), gate=None):
         moving = launch(moves, rows if gate is None else gate)
-        for bit in reversed(seq_bits):
-            got = settle(swap(rows, bit), moving)
+        pieces = [rows]
+        for bit in reversed(seq_bits[1:]):
+            came = [swap(p, bit) for p in pieces]
+            came[0] = settle(came[0], moving)
             moving = []
-            rows = jnp.concatenate([rows, got], axis=0)
-        return rows
+            pieces = pieces + came
+        pairs = [jnp.concatenate([p, swap(p, 1)], axis=0) for p in pieces]
+        return pairs[0], (jnp.concatenate(pairs[1:], axis=0) if len(pairs) > 2 else pairs[1])
+
+    def both(halves):
+        return jnp.concatenate(halves, axis=0)
 
     def reduce_seq(left, right, moves=(), gate=None):
-        weight, dims = right
-        moving = launch(moves, left if gate is None else gate)
-        half = left.shape[0] // 2
-        got = swap(dot(left[half:], weight, *dims).astype(BF), seq_bits[0])
-        total = dot(left[:half], weight, *dims) + got.astype(F32)
+        near, far = left
+        moving = launch(moves, far if gate is None else gate)
+        size = near.shape[0] // 2
+
+        def chip(rows, own):
+            parts = right(rows, own) if callable(right) else dot(rows, right[0], *right[1])
+            return parts[:size] + swap(parts[size:].astype(BF), 1).astype(F32)
+
+        total = [None] + [
+            chip(far[i * 2 * size : (i + 1) * 2 * size], False) for i in range(len(x_steps) - 1)
+        ]
         for i, bit in enumerate(seq_bits[1:]):
-            half = total.shape[0] // 2
-            got = swap(total[half:].astype(BF), bit)
+            middle = len(total) // 2
+            got = [swap(t.astype(BF), bit) for t in total[middle:]]
             if i + 2 == len(seq_bits):
-                got = settle(got, moving)
-            total = total[:half] + got.astype(F32)
-        return total
+                got[0] = settle(got[0], moving)
+            if total[0] is None:
+                total[0] = chip(near, True)
+            total = [a + b.astype(F32) for a, b in zip(total[:middle], got)]
+        return total[0]
 
     def halve(array, index_bit, bit):
         chosen = index_bit.astype(jnp.bool_)
@@ -462,7 +478,6 @@
                     return place(pieces, [[0, 4], [2, 6], [1, 5], [3, 7]], sizes, unpack)
 
             first_stream = Stream(shard)
-            group = gather_seq(tokens)
             plan = [(3, 0, hidden_part, n_dp)]
             cuts = [own_hidden]
             for layer in range(1, layers):
@@ -475,6 +490,7 @@
             sent = [after(p, got[1], got[2], got[3]) for p in sent]
             got = [sent[0]] + [swap(sent[step], step) for step in range(1, n_seq)]
             second = join_pieces(got, part, cuts)
+            group = both(gather_seq(after(tokens, *got[2:])))
 
             class OutRows:
                 def __init__(self, rows):
@@ -509,11 +525,10 @@
             shard = settle(shard, launch(first_stream.far(), shard))
             moving = launch(first_stream.middle(), first_stream.came)
             out_y = launch(outs[0].step(1), first_stream.came)
-            settle(shard, moving)
-            gate = first_stream.near
-            moving = launch(first_stream.last(), first_stream.y_line)
-            settle(shard, out_y)
-            moving += launch(expand_0.far() + outs[0].step(2), gate)
+            shard = settle(shard, moving[:1])
+            moving = moving[1:] + launch(first_stream.last() + expand_0.far(), first_stream.near)
+            shard = settle(shard, out_y)
+            moving += launch(outs[0].step(2), outs[0].moved)
             group = settle(group, moving)
             qkv_first, _, small_full, small_heads, small_inner = first_stream.whole(
                 (block_rows, 16), (pairs_here, layers, dim, own_hidden)
@@ -529,7 +544,7 @@
             )
             full = small[:, :, : 8 * part].reshape(n_dev, layers, 8, part).transpose(1, 2, 0, 3)
             hidden_bias = small[:, :, 8 * part :].transpose(1, 0, 2)
-            group = gather_seq(tokens)
+            group = both(gather_seq(tokens))
             full = full.reshape(layers, 8, dim).astype(F32)
             by_column = full[:, :2].reshape(layers, 2, pairs_here, n_seq, 2 * HEAD)
             by_column = lax.dynamic_index_in_dim(by_column, seq, 3, keepdims=False)
@@ -557,23 +572,23 @@
 
             def beside_of(layer, point):
                 if (layer, point) == (0, "attend"):
-                    return expand_0.middle() + outs[0].step(4)
+                    return outs[0].step(4) + expand_0.middle()
                 if (layer, point) == (0, "out"):
                     out_all.append(outs[0].take())
-                    return expand_0.last() + shrink_0.far()
+                    return expand_0.last() + shrink_0.far() + outs[1].step(1)
                 if (layer, point) == (0, "normed"):
                     return shrink_0.middle() + expand_0.ready((block_rows,))
                 if (layer, point) == (0, "active"):
                     expand_all.append(expand_0.full)
-                    return shrink_0.last() + qkv_1.far()
+                    return shrink_0.last() + qkv_1.far() + outs[1].step(2)
                 if (layer, point) == (0, "shrink"):
                     shrink_all.append(shrink_0.whole((hidden_part,))[0])
-                    return qkv_1.middle() + outs[1].step(1)
+                    return qkv_1.middle() + outs[1].step(4)
                 if (layer, point) == (1, "group"):
-                    return qkv_1.last() + expand_1.far() + outs[1].step(2)
+                    return qkv_1.last() + expand_1.far()
                 if (layer, point) == (1, "attend"):
                     qkv_all.append(qkv_1.whole((block_rows,))[0])
-                    return outs[1].step(4) + expand_1.middle()
+                    return expand_1.middle()
                 if (layer, point) == (1, "out"):
                     out_all.append(outs[1].take())
                     return expand_1.last() + shrink_1.far()
@@ -629,26 +644,33 @@
                 vector_of(layer, i) for i in range(8)
             )
             if layer:
-                group = gather_seq(hidden_now.astype(BF), beside_of(layer, "group"), summed)
+                group = both(gather_seq(hidden_now.astype(BF), beside_of(layer, "group"), summed))
             moving = launch(beside_of(layer, "attend"), group)
             qkv = (dot(group, qkv_all[layer]) + head_bias[layer]).astype(BF)
             attended, row_max, row_sum = attend(qkv, starts)
             attended = settle(attended, moving)
             moves = beside_of(layer, "out")
-            summed = reduce_seq(attended, (out_all[layer], (1, 0)), moves)
+            chip_rows = 2 * rows_here
+            halves = (attended[:chip_rows], attended[chip_rows:])
+            summed = reduce_seq(halves, (out_all[layer], (1, 0)), moves)
             resid_one = hidden_now + (summed + out_b)
             rhat_one, inverse_one = norm_parts(resid_one)
             normed = rhat_one * gain_one + bias_one
-            normed_group = gather_seq(normed.astype(BF), beside_of(layer, "normed"), summed)
+            normed_halves = gather_seq(normed.astype(BF), beside_of(layer, "normed"), summed)
             moves = beside_of(layer, "active")
-            moving = launch(moves, moves[0][2] if moves else normed_group)
-            inner = dot(normed_group, expand_all[layer]) + hidden_bias[layer]
-            cdf = 0.5 * (1.0 + lax.erf(inner * math.sqrt(0.5)))
-            active = (inner * cdf).astype(BF)
-            slope = cdf + inner * jnp.exp(-0.5 * inner * inner) * (1.0 / math.sqrt(2 * math.pi))
+            moving = launch(moves, moves[0][2] if moves else normed_halves[1])
+            active, slope = [], []
+            for rows in normed_halves:
+                inner = dot(rows, expand_all[layer]) + hidden_bias[layer]
+                cdf = 0.5 * (1.0 + lax.erf(inner * math.sqrt(0.5)))
+                active.append((inner * cdf).astype(BF))
+                slope.append(
+                    cdf + inner * jnp.exp(-0.5 * inner * inner) * (1.0 / math.sqrt(2 * math.pi))
+                )
             active = settle(active, moving)
             moves = beside_of(layer, "shrink")
             summed = reduce_seq(active, (shrink_all[layer], (1, 0)), moves)
+            normed_group, active = both(normed_halves), both(active)
             resid_two = normed + (summed + shrink_b)
             rhat_two, inverse_two = norm_parts(resid_two)
             hidden_now = rhat_two * gain_two + bias_two
@@ -699,13 +721,16 @@
                 self.keep = of(True, False)
                 return [(self, "came", of(True, True), n_seq)]
 
+            def middle_z(self):
+                total = (self.keep.astype(F32) + self.came.astype(F32)).astype(BF)
+                return [(self, "near", total, 2 * n_seq)]
+
+            def middle_y(self):
+                self.keep = self.of(False, False)
+                return [(self, "came", self.of(False, True), n_seq)]
+
             def middle(self):
-                total = (self.keep.astype(F32) + self.came.astype(F32)).astype(BF)
-                self.keep = self.of(False, False)
-                return [
-                    (self, "near", total, 2 * n_seq),
-                    (self, "came", self.of(False, True), n_seq),
-                ]
+                return self.middle_z() + self.middle_y()
 
             def last(self):
                 total = (
@@ -750,7 +775,7 @@
         class Table:
             def __init__(self, rows, more):
                 self.keep, self.more = rows, more
-                self.bits = [4 * n_seq, 2 * n_seq, n_seq] + seq_bits
+                self.bits = [4 * n_seq, 2 * n_seq, n_seq]
 
             def take(self):
                 if hasattr(self, "came"):
@@ -759,17 +784,21 @@
             def step(self):
                 self.take()
                 bit = self.bits.pop(0)
-                sent = self.keep
-                if bit >= n_seq:
-                    middle = self.keep.shape[1] // 2
-                    low, up = self.keep[:, :middle], self.keep[:, middle:]
-                    chosen = bit_of(dp, bit // n_seq) == 1
-                    sent, self.keep = jnp.where(chosen, low, up), jnp.where(chosen, up, low)
-                elif bit == seq_bits[0]:
-                    columns = self.keep.shape[1]
-                    more = jnp.pad(self.more, ((0, 0), (0, columns - self.more.shape[1])))
-                    sent = self.keep = jnp.concatenate([self.keep, more], axis=0)
-                return [(self, "came", sent, bit)]
+                middle = self.keep.shape[1] // 2
+                low, up = self.keep[:, :middle], self.keep[:, middle:]
+                chosen = bit_of(dp, bit // n_seq) == 1
+                self.keep = jnp.where(chosen, up, low)
+                return [(self, "came", jnp.where(chosen, low, up), bit)]
+
+            def group_step(self):
+                self.take()
+                more = jnp.pad(self.more, ((0, 0), (0, self.keep.shape[1] - self.more.shape[1])))
+                self.keep = jnp.concatenate([self.keep, more], axis=0)
+                return [(self, "came_%d" % i, self.keep, i) for i in range(1, n_seq)]
+
+            def whole(self):
+                rest = [getattr(self, "came_%d" % i) for i in range(1, n_seq)]
+                return sum(by_origin([self.keep] + rest))
 
         def rows_back(scattered):
             return exchange_steps([scattered[s * part : (s + 1) * part] for s in range(n_seq)])
@@ -818,38 +847,57 @@
                 )
 
             def layer_rows():
-                vectors[0], inner_vectors[0] = token_rows(), hidden_rows(column_sums(low_inner))
+                vectors[0], inner_vectors[0] = token_rows(), hidden_rows(inner_sums)
                 return jnp.concatenate(vectors + [lex_row] + inner_vectors, axis=0)
 
             above = big[layer + 1] if special and layer + 1 < layers else None
             moves = above.expand.last() + above.qkv.first() if above else []
-            second_group = gather_seq(low_second, moves, grad_now)
-            low_inner = (dot(second_group, shrink_all[layer], 1, 1) * slope).astype(BF)
+            halves = gather_seq(low_second, moves, grad_now)
+            moving = launch(above.qkv.middle(), above.qkv.came) if above else []
+            low_inner = [
+                (dot(rows, shrink_all[layer], 1, 1) * slope[i]).astype(BF)
+                for i, rows in enumerate(halves)
+            ]
+            low_inner[1] = settle(low_inner[1], moving)
+            second_group = both(halves)
+            inner_group = both(low_inner)
             shrink_grad = dot(active, second_group, 0, 0).astype(BF)
-            expand_grad = dot(normed_group, low_inner, 0, 0).astype(BF)
+            expand_grad = dot(normed_group, inner_group, 0, 0).astype(BF)
+            moves = []
             if special:
                 big[layer] = mine = Grads()
                 mine.shrink, mine.expand = Sums([shrink_grad]), Sums([expand_grad])
-                moves = above.qkv.middle() if above else mine.shrink.first()
-            else:
-                moves = []
+                moves = (above.qkv.last() if above else []) + mine.shrink.first()
             summed = reduce_seq(low_inner, (expand_all[layer], (1, 1)), moves)
+            inner_sums = sum(column_sums(half) for half in low_inner)
             grad_normed = grad_second + summed
             grad_first, ngain, nbias = norm_back(grad_normed, gain_one, rhat_one, inverse_one)
             low_first = grad_first.astype(BF)
             if special:
-                moves = above.qkv.last() + mine.shrink.first() if above else mine.shrink.middle()
-            first_group = gather_seq(low_first, moves, summed)
+                moves = mine.shrink.middle()
+            first_group = both(gather_seq(low_first, moves, summed))
             if special:
-                moves = mine.shrink.middle() if above else mine.shrink.last() + mine.expand.first()
+                moves = mine.shrink.last() + mine.expand.first()
                 moving = launch(moves, first_group)
             low_attn = dot(first_group, out_all[layer], 1, 1).astype(BF)
             out_grad = dot(attended, first_group, 0, 0).astype(BF)
             if special:
                 quarter = dim // n_seq
-                pieces = exchange_steps(
-                    [out_grad[:, s * quarter : (s + 1) * quarter] for s in range(n_seq)]
-                )
+                pieces = [out_grad[:, s * quarter : (s + 1) * quarter] for s in range(n_seq)]
+                if layer == 0:
+                    done = [
+                        g.rows().astype(BF) for m in big[1:] for g in (m.expand, m.qkv)
+                    ]
+                    for s in range(n_seq):
+                        rows = jnp.concatenate([g[s * part : (s + 1) * part] for g in done], axis=1)
+                        cut = [
+                            rows[:, i : i + quarter] for i in range(0, rows.shape[1], quarter)
+                        ]
+                        pieces[s] = jnp.concatenate([pieces[s]] + cut, axis=0)
+                pieces = exchange_steps(pieces)
+                if layer == 0:
+                    upper_rows = by_origin([p[width:] for p in pieces])
+                    pieces = [p[:width] for p in pieces]
                 pieces = [p.reshape(pairs_here, 1, 2 * HEAD, quarter) for p in by_origin(pieces)]
                 out_columns = jnp.concatenate(pieces, axis=1).reshape(dim, quarter)
             grad_qkv = attend_back(qkv, starts, row_max, row_sum, low_attn)
@@ -882,10 +930,13 @@
                     moves = mine.expand.middle()
                 else:
                     table = Table(layer_rows(), scores)
-                    moves = mine.shrink.last() + mine.qkv.first() + table.step()
+                    qkv_grad = settle(qkv_grad, launch(table.step(), grad_qkv))
+                    moves = mine.qkv.first() + mine.expand.middle_z() + table.step()
             else:
                 moves = []
-            summed = reduce_seq(after(grad_qkv, qkv_grad), (qkv_all[layer], (1, 1)), moves)
+            left = after(grad_qkv, qkv_grad)
+            left = (left[:chip_rows], left[chip_rows:])
+            summed = reduce_seq(left, (qkv_all[layer], (1, 1)), moves, qkv_grad)
             if special and layer == 0:
 
                 def back_of(grads, extra=0):
@@ -898,20 +949,16 @@
                         blocks.append(jnp.concatenate(rows, axis=1) if len(rows) > 1 else rows[0])
                     return Back(blocks)
 
-                backs = [None] + [back_of([m.expand.rows(), m.qkv.rows()]) for m in big[1:]]
+                gate = summed
                 moves = mine.qkv.middle() + table.step()
-                gate = settle(summed, launch(moves, summed))
-                moves = mine.qkv.last() + mine.expand.first() + table.step()
                 gate = settle(gate, launch(moves, gate))
-                backs[0] = back_of([mine.qkv.rows()], 16)
-                moves = mine.expand.middle() + backs[0].moves()
+                moves = mine.qkv.last() + mine.expand.middle_y() + table.group_step()
                 gate = settle(gate, launch(moves, gate))
-                moves = mine.expand.last() + table.step()
-                for back in backs[1:]:
-                    moves += back.moves()
+                last_back = back_of([mine.qkv.rows()], 16)
+                moves = mine.expand.last() + last_back.moves()
                 gate = settle(gate, launch(moves, gate))
-                last_back = back_of([mine.expand.rows()])
-                settle(gate, launch(last_back.moves() + table.step(), gate))
+                expand_back = back_of([mine.expand.rows()])
+                settle(gate, launch(expand_back.moves(), gate))
             if not special:
                 big[layer] = (
                     scatter_dp(shrink_grad),
@@ -925,14 +972,13 @@
                 vectors[layer] = token_rows()
                 if layer:
                     vectors[layer] = jnp.concatenate([vectors[layer]] + head_rows, axis=0)
-                inner_vectors[layer] = hidden_rows(column_sums(low_inner))
+                inner_vectors[layer] = hidden_rows(inner_sums)
 
         tokens_grad = grad_now.astype(BF)
 
         counts = [v.shape[0] for v in vectors] + [1] + [n_seq] * layers
         if special:
-            table.take()
-            table = table.keep
+            table = table.whole()
             scores = table[-1:, : scores.shape[1]]
         else:
             table = reduce_rows(jnp.concatenate(vectors + [lex_row], axis=0), scores)
@@ -956,18 +1002,24 @@
         for layer in range(layers):
             if special:
                 shrink_rows = big[layer].shrink.rows()
-                got = backs[layer].got()
                 if layer:
-                    got = by_origin(got)
-                    expand_out, got = [g[:, :own_hidden] for g in got], [g[:, own_hidden:] for g in got]
+                    count = (own_hidden + 3 * width + quarter) // quarter
+                    got = []
+                    for g in upper_rows:
+                        g = g[(layer - 1) * count * part : layer * count * part]
+                        cut = [g[i * part : (i + 1) * part] for i in range(count)]
+                        got.append(jnp.concatenate(cut, axis=1))
+                    expand_out = [g[:, :own_hidden] for g in got]
+                    got = [g[:, own_hidden:] for g in got]
                 else:
+                    got = last_back.got()
                     source = seq ^ lax.rem(dp, n_seq)
                     row = got[0][part : part + 1, : 4 * HEAD]
                     for step in range(1, n_seq):
                         row = jnp.where(source == step, got[step][part : part + 1, : 4 * HEAD], row)
                     last = row.reshape(2, 2 * HEAD).astype(F32)
                     got = by_origin([g[:part] for g in got])
-                    expand_out = by_origin(last_back.got())
+                    expand_out = by_origin(expand_back.got())
                 out_out = jnp.concatenate([g[:, 3 * width :] for g in got], axis=1)
             else:
                 shrink_rows, expand_rows, out_out, qkv_rows = big[layer]

time: 595 us -> 553 us (0.929)
  waiting for transfers between devices: 262 us -> 228 us
  starting transfers between devices: 94.1 us -> 109 us
  Pallas kernels: 68.4 us -> 58.9 us
  local copies, waits for them, and re-layouts: 28.7 us -> 21.6 us
    ppermute x112 -> x126, waiting for transfers between devices: 262 us -> 228 us  [swap(): return lax.ppermute(array, AXES, [(p, p ^ bit) for p in range(n_dev)])]
    ppermute x112 -> x126, starting transfers between devices: 94.1 us -> 109 us  [swap(): return lax.ppermute(array, AXES, [(p, p ^ bit) for p in range(n_dev)])]
    pallas_call x4, Pallas kernels: 42.3 us -> 32.9 us  [the longest x2 19.8 us: attend_back(): pl.pallas_call(functools.partial(attend_back_kernel, math.gcd(tokens, 768...]
    unnamed x318 -> x344, local copies, waits for them, and re-layouts: 17.5 us -> 11.1 us
    dot_general x33 -> x37, matrix products: 69.8 us -> 66.5 us  [dot(): lax.dot_general(left, right, (((left_dim,), (right_dim,)), ((), ())), pre...]
  transfers between devices with their start and end apart: 112 -> 126, of which waited for: 53 -> 60; matrix products, arithmetic and copies ran while one was open for 14% -> 18% of each run, Pallas kernels for 10% -> 9%
where the time goes in v3:
time: 553 us; the launch traced here: 543 us
  waiting for transfers between devices  228 us (41%)
  starting transfers between devices  109 us (20%)
  matrix products  68 us (12%)
  Pallas kernels  58.9 us (11%)
  other arithmetic  52.3 us (9%)
  local copies, waits for them, and re-layouts  21.6 us (4%)
    ppermute x126, waiting for transfers between devices, swap(): return lax.ppermute(array, AXES, [(p, p ^ bit) for p in range(n_dev)])  228 us
    ppermute x126, starting transfers between devices, swap(): return lax.ppermute(array, AXES, [(p, p ^ bit) for p in range(n_dev)])  109 us
    dot_general x37, matrix products, dot(): lax.dot_general(left, right, (((left_dim,), (right_dim,)), ((), ())), pre...  66.5 us
    pallas_call x2, Pallas kernels, attend_back(): pl.pallas_call(functools.partial(attend_back_kernel, math.gcd(tokens, 768...  19.8 us
    pallas_call x6, Pallas kernels, place(): pl.pallas_call(body, out_shape=tuple(shapes), in_specs=[whole] * len(piec...  17.6 us
    pallas_call x2, Pallas kernels, attend(): pl.pallas_call(functools.partial(attend_kernel, math.gcd(tokens, 768)), o...  13.1 us
    unnamed x344, local copies, waits for them, and re-layouts  11.1 us
  transfers between devices with their start and end apart: 126, of which 60 were waited for; matrix products, arithmetic and copies ran while one was open for 18% of the time, Pallas kernels for 9%

profile of v3, /device:TPU:0, one launch (start us, length us, event | category | flops | bytes accessed | tf_op | source)
XLA Modules:
  0.0 543.4 jit_solution(14238487811952674880)
XLA Ops:
  13.6 2.8 collective-permute-start.8
  16.4 10.7 %collective-permute-done.8 = bf16[144,768]{1,0:T(8,128)(2,1)S(1)} collective-permute-done((bf16[144,768]{1,0:T(8,128)(2,1)}, bf16[144,768]{1,0:T(8,128)(2,1)S(1)}, u32[]{:S(2)}, u32[]{:S(2)}) %collective-permute-start.8) | collective-permute-done | bytes 221216 | tf_op jit(solution)/shard_map/ppermute | solution.py:316
  44.8 3.1 collective-permute-start.13
  49.1 3.1 collective-permute-done.9.refs_2_
  53.9 4.2 collective-permute-done.13
  58.0 3.2 collective-permute-done.11.refs_3_
  64.5 2.9 shard_map.379
  68.2 3.1 collective-permute-start.16
  71.4 3.9 add_convert_fusion.1.qkv_ref
  75.3 6.6 %shard_map.380 = (bf16[768,256]{1,0:T(8,128)(2,1)}, f32[4,768]{1,0:T(4,128)}, f32[4,768]{1,0:T(4,128)}) custom-call(bf16[768,768]{1,0:T(8,128)(2,1)} %add_convert_fusion.1.qkv_ref, s32[768,1]{1,0:T(8,128)} %broadcast_in_dim.145.col_ref, s32[1,768]{1,0:T(1,128)} %broadcast_in_dim.129.row_ref), custom_call_target="tpu_custom_call" | custom-call | flops 6039797760 | bytes 3145728 | tf_op jit(solution)/shard_map/pallas_call | solution.py:108
  90.4 13.1 %collective-permute-done.24 = bf16[128,1024]{1,0:T(8,128)(2,1)S(1)} collective-permute-done((bf16[128,1024]{1,0:T(8,128)(2,1)S(1)}, bf16[128,1024]{1,0:T(8,128)(2,1)S(1)}, u32[]{:S(2)}, u32[]{:S(2)}) %collective-permute-start.24) | collective-permute-done | bytes 262176 | tf_op jit(solution)/shard_map/ppermute | solution.py:316
  109.6 3.0 shard_map.381
  112.6 5.0 collective-permute-done.26
  123.1 4.4 multiply_convert_fusion.3
  132.3 3.0 collective-permute-done.30.refs_3_
  136.1 3.1 shard_map.382
  139.2 2.7 fusion.194
  148.1 10.2 %collective-permute-done.38 = bf16[128,1024]{1,0:T(8,128)(2,1)S(1)} collective-permute-done((bf16[128,1024]{1,0:T(8,128)(2,1)S(1)}, bf16[128,1024]{1,0:T(8,128)(2,1)S(1)}, u32[]{:S(2)}, u32[]{:S(2)}) %collective-permute-start.38) | collective-permute-done | bytes 262176 | tf_op jit(solution)/shard_map/ppermute | solution.py:316
  165.0 11.8 %collective-permute-done.42 = bf16[128,1024]{1,0:T(8,128)(2,1)S(1)} collective-permute-done((bf16[128,1024]{1,0:T(8,128)(2,1)S(1)}, bf16[128,1024]{1,0:T(8,128)(2,1)S(1)}, u32[]{:S(2)}, u32[]{:S(2)}) %collective-permute-start.42) | collective-permute-done | bytes 262176 | tf_op jit(solution)/shard_map/ppermute | solution.py:316
  178.6 2.6 shard_map.383
  181.3 4.0 add_convert_fusion.qkv_ref
  185.3 6.6 %shard_map.384 = (bf16[768,256]{1,0:T(8,128)(2,1)}, f32[4,768]{1,0:T(4,128)}, f32[4,768]{1,0:T(4,128)}) custom-call(bf16[768,768]{1,0:T(8,128)(2,1)} %add_convert_fusion.qkv_ref, s32[768,1]{1,0:T(8,128)} %broadcast_in_dim.145.col_ref, s32[1,768]{1,0:T(1,128)} %broadcast_in_dim.129.row_ref), custom_call_target="tpu_custom_call" | custom-call | flops 6039797760 | bytes 3145728 | tf_op jit(solution)/shard_map/pallas_call | solution.py:108
  200.0 12.9 %collective-permute-done.50 = bf16[128,1024]{1,0:T(8,128)(2,1)S(1)} collective-permute-done((bf16[128,1024]{1,0:T(8,128)(2,1)S(1)}, bf16[128,1024]{1,0:T(8,128)(2,1)S(1)}, u32[]{:S(2)}, u32[]{:S(2)}) %collective-permute-start.50) | collective-permute-done | bytes 262176 | tf_op jit(solution)/shard_map/ppermute | solution.py:316
  216.0 3.1 shard_map.385
  219.0 6.1 %collective-permute-done.52 = bf16[192,1024]{1,0:T(8,128)(2,1)S(1)} collective-permute-done((bf16[192,1024]{1,0:T(8,128)(2,1)S(1)}, bf16[192,1024]{1,0:T(8,128)(2,1)S(1)}, u32[]{:S(2)}, u32[]{:S(2)}) %collective-permute-start.52) | collective-permute-done | bytes 393248 | tf_op jit(solution)/shard_map/ppermute | solution.py:316
  228.9 4.1 multiply_convert_fusion.1
  235.4 6.3 %collective-permute-done.56.refs_3_ = bf16[256,1024]{1,0:T(8,128)(2,1)S(1)} collective-permute-done((bf16[256,1024]{1,0:T(8,128)(2,1)S(1)}, bf16[256,1024]{1,0:T(8,128)(2,1)S(1)}, u32[]{:S(2)}, u32[]{:S(2)}) %collective-permute-start.56) | collective-permute-done | bytes 524320 | tf_op jit(solution)/shard_map/ppermute | solution.py:316
  242.5 3.0 shard_map.386
  245.5 2.7 fusion.196
  252.8 10.1 %collective-permute-done.59 = bf16[192,1024]{1,0:T(8,128)(2,1)} collective-permute-done((bf16[192,1024]{1,0:T(8,128)(2,1)}, bf16[192,1024]{1,0:T(8,128)(2,1)}, u32[]{:S(2)}, u32[]{:S(2)}) %collective-permute-start.59) | collective-permute-done | bytes 393248 | tf_op jit(solution)/shard_map/ppermute | solution.py:316
  275.0 4.2 collective-permute-done.62
  279.2 3.8 convert_reduce_fusion.3
  284.8 3.1 convolution_convert_fusion.3
  299.3 8.6 %collective-permute-done.66 = bf16[2,128,1024]{2,1,0:T(8,128)(2,1)S(1)} collective-permute-done((bf16[2,128,1024]{2,1,0:T(8,128)(2,1)S(1)}, bf16[2,128,1024]{2,1,0:T(8,128)(2,1)S(1)}, u32[]{:S(2)}, u32[]{:S(2)}) %collective-permute-start.66) | collective-permute-done | bytes 524320 | tf_op jit(solution)/shard_map/ppermute | solution.py:316
  314.9 8.4 %collective-permute-done.68 = bf16[192,1024]{1,0:T(8,128)(2,1)S(1)} collective-permute-done((bf16[192,1024]{1,0:T(8,128)(2,1)S(1)}, bf16[192,1024]{1,0:T(8,128)(2,1)S(1)}, u32[]{:S(2)}, u32[]{:S(2)}) %collective-permute-start.68) | collective-permute-done | bytes 393248 | tf_op jit(solution)/shard_map/ppermute | solution.py:316
  333.8 10.1 %shard_map.387 = bf16[768,768]{1,0:T(8,128)(2,1)} custom-call(bf16[768,768]{1,0:T(8,128)(2,1)} %add_convert_fusion.qkv_ref, s32[768,1]{1,0:T(8,128)} %broadcast_in_dim.145.col_ref, s32[1,768]{1,0:T(1,128)} %broadcast_in_dim.129.row_ref, f32[4,768]{1,0:T(4,128)} %get-tuple-element.307.max_ref, f32[4,768]{1,0:T(4,128)} %get-tuple-element.308.sum_ref, ...), custom_call_target="tpu_custom_call" | custom-call | flops 6039797760 | bytes 3145728 | tf_op jit(solution)/shard_map/pallas_call | solution.py:127
  356.4 6.4 %collective-permute-done.78 = bf16[2,128,1024]{2,1,0:T(8,128)(2,1)S(1)} collective-permute-done((bf16[2,128,1024]{2,1,0:T(8,128)(2,1)S(1)}, bf16[2,128,1024]{2,1,0:T(8,128)(2,1)S(1)}, u32[]{:S(2)}, u32[]{:S(2)}) %collective-permute-start.78) | collective-permute-done | bytes 524320 | tf_op jit(solution)/shard_map/ppermute | solution.py:316
  373.8 10.6 %collective-permute-done.82 = bf16[128,1024]{1,0:T(8,128)(2,1)S(1)} collective-permute-done((bf16[128,1024]{1,0:T(8,128)(2,1)S(1)}, bf16[128,1024]{1,0:T(8,128)(2,1)S(1)}, u32[]{:S(2)}, u32[]{:S(2)}) %collective-permute-start.82) | collective-permute-done | bytes 262176 | tf_op jit(solution)/shard_map/ppermute | solution.py:316
  392.5 6.7 %collective-permute-done.89 = bf16[2,128,1024]{2,1,0:T(8,128)(2,1)S(1)} collective-permute-done((bf16[2,128,1024]{2,1,0:T(8,128)(2,1)S(1)}, bf16[2,128,1024]{2,1,0:T(8,128)(2,1)S(1)}, u32[]{:S(2)}, u32[]{:S(2)}) %collective-permute-start.89) | collective-permute-done | bytes 524320 | tf_op jit(solution)/shard_map/ppermute | solution.py:316
  409.2 7.9 %collective-permute-done.92 = bf16[128,1024]{1,0:T(8,128)(2,1)S(1)} collective-permute-done((bf16[128,1024]{1,0:T(8,128)(2,1)S(1)}, bf16[128,1024]{1,0:T(8,128)(2,1)S(1)}, u32[]{:S(2)}, u32[]{:S(2)}) %collective-permute-start.92) | collective-permute-done | bytes 262176 | tf_op jit(solution)/shard_map/ppermute | solution.py:316
  429.6 6.0 %collective-permute-done.95 = bf16[192,1024]{1,0:T(8,128)(2,1)} collective-permute-done((bf16[192,1024]{1,0:T(8,128)(2,1)}, bf16[192,1024]{1,0:T(8,128)(2,1)}, u32[]{:S(2)}, u32[]{:S(2)}) %collective-permute-start.95) | collective-permute-done | bytes 393248 | tf_op jit(solution)/shard_map/ppermute | solution.py:316
  445.9 9.7 %shard_map.388 = bf16[768,768]{1,0:T(8,128)(2,1)} custom-call(bf16[768,768]{1,0:T(8,128)(2,1)} %add_convert_fusion.1.qkv_ref, s32[768,1]{1,0:T(8,128)} %broadcast_in_dim.145.col_ref, s32[1,768]{1,0:T(1,128)} %broadcast_in_dim.129.row_ref, f32[4,768]{1,0:T(4,128)} %get-tuple-element.303.max_ref, f32[4,768]{1,0:T(4,128)} %get-tuple-element.304.sum_ref, ...), custom_call_target="tpu_custom_call" | custom-call | flops 6039797760 | bytes 3145728 | tf_op jit(solution)/shard_map/pallas_call | solution.py:127
  459.3 2.6 convolution_convert_fusion.4
  467.1 2.7 collective-permute-done.101
  476.2 9.6 %collective-permute-done.110 = f32[23,256]{1,0:T(8,128)S(1)} collective-permute-done((f32[23,256]{1,0:T(8,128)S(1)}, f32[23,256]{1,0:T(8,128)S(1)}, u32[]{:S(2)}, u32[]{:S(2)}) %collective-permute-start.110) | collective-permute-done | bytes 23584 | tf_op jit(solution)/shard_map/ppermute | solution.py:316
  492.0 10.3 %collective-permute-done.113 = f32[23,128]{1,0:T(8,128)S(1)} collective-permute-done((f32[23,128]{1,0:T(8,128)S(1)}, f32[23,128]{1,0:T(8,128)S(1)}, u32[]{:S(2)}, u32[]{:S(2)}) %collective-permute-start.113) | collective-permute-done | bytes 11808 | tf_op jit(solution)/shard_map/ppermute | solution.py:316
  509.7 8.1 %collective-permute-done.114 = bf16[144,1024]{1,0:T(8,128)(2,1)S(1)} collective-permute-done((bf16[144,1024]{1,0:T(8,128)(2,1)S(1)}, bf16[144,1024]{1,0:T(8,128)(2,1)S(1)}, u32[]{:S(2)}, u32[]{:S(2)}) %collective-permute-start.114) | collective-permute-done | bytes 294944 | tf_op jit(solution)/shard_map/ppermute | solution.py:316
  526.5 8.7 %collective-permute-done.119 = bf16[128,1024]{1,0:T(8,128)(2,1)S(1)} collective-permute-done((bf16[128,1024]{1,0:T(8,128)(2,1)S(1)}, bf16[128,1024]{1,0:T(8,128)(2,1)S(1)}, u32[]{:S(2)}, u32[]{:S(2)}) %collective-permute-start.119) | collective-permute-done | bytes 262176 | tf_op jit(solution)/shard_map/ppermute | solution.py:316
  (827 shorter events, 249.5 us)
Async XLA Ops:
  10.1 16.9 %collective-permute-start.4 = (bf16[32,4864]{1,0:T(8,128)(2,1)}, bf16[32,4864]{1,0:T(8,128)(2,1)S(1)}, u32[]{:S(2)}, u32[]{:S(2)}) collective-permute-start(bf16[32,4864]{1,0:T(8,128)(2,1)} %get-tuple-element.218), channel_id=1, source_target_pairs={{0,3},{1,2},{2,1},{3,0},{4,7},{5,6},{6,5},{7,4},{8,11},{9,10},{10,... | collective-permute-start | bytes 933896 | tf_op jit(solution)/shard_map/ppermute | solution.py:316
  11.4 15.6 %collective-permute-start.3 = (bf16[32,4864]{1,0:T(8,128)(2,1)}, bf16[32,4864]{1,0:T(8,128)(2,1)S(1)}, u32[]{:S(2)}, u32[]{:S(2)}) collective-permute-start(bf16[32,4864]{1,0:T(8,128)(2,1)} %get-tuple-element.216), channel_id=1, source_target_pairs={{0,2},{1,3},{2,0},{3,1},{4,6},{5,7},{6,4},{7,5},{8,10},{9,11},{10,... | collective-permute-start | bytes 933896 | tf_op jit(solution)/shard_map/ppermute | solution.py:316
  16.4 14.3 %collective-permute-start.12 = (bf16[32,4864]{1,0:T(8,128)(2,1)}, bf16[32,4864]{1,0:T(8,128)(2,1)S(1)}, u32[]{:S(2)}, u32[]{:S(2)}) collective-permute-start(bf16[32,4864]{1,0:T(8,128)(2,1)} %get-tuple-element.228), channel_id=1, source_target_pairs={{0,1},{1,0},{2,3},{3,2},{4,5},{5,4},{6,7},{7,6},{8,9},{9,8},{10,11... | collective-permute-start | bytes 933896 | tf_op jit(solution)/shard_map/ppermute | solution.py:316
  41.4 19.8 %collective-permute-start.11 = (bf16[288,768]{1,0:T(8,128)(2,1)S(1)}, bf16[288,768]{1,0:T(8,128)(2,1)S(1)}, u32[]{:S(2)}, u32[]{:S(2)}) collective-permute-start(bf16[288,768]{1,0:T(8,128)(2,1)S(1)} %collective-permute-done.10.refs_1_), channel_id=1, source_target_pairs={{0,4},{1,5},{2,6},{3,7},{4,0},{5,1},{6,2},{7,3},{8,12},{9,13},{10,... | collective-permute-start | bytes 1327112 | tf_op jit(solution)/shard_map/ppermute | solution.py:316
  61.3 20.6 %collective-permute-start.18 = (bf16[256,1024]{1,0:T(8,128)(2,1)S(1)}, bf16[256,1024]{1,0:T(8,128)(2,1)S(1)}, u32[]{:S(2)}, u32[]{:S(2)}) collective-permute-start(bf16[256,1024]{1,0:T(8,128)(2,1)S(1)} %constant_dynamic-update-slice_fusion.refs_0_), channel_id=1, source_target_pairs={{0,4},{1,5},{2,6},{3,7},{4,0},{5,1},{6,2},{7,3},{8,12},{9,13},{10,... | collective-permute-start | bytes 1572872 | tf_op jit(solution)/shard_map/ppermute | solution.py:316
  62.9 19.0 %collective-permute-start.17 = (bf16[256,1024]{1,0:T(8,128)(2,1)S(1)}, bf16[256,1024]{1,0:T(8,128)(2,1)S(1)}, u32[]{:S(2)}, u32[]{:S(2)}) collective-permute-start(bf16[256,1024]{1,0:T(8,128)(2,1)S(1)} %constant_dynamic-update-slice_fusion.refs_0_), channel_id=1, source_target_pairs={{0,8},{1,9},{2,10},{3,11},{4,12},{5,13},{6,14},{7,15},{8,0},{9,1},... | collective-permute-start | bytes 1572872 | tf_op jit(solution)/shard_map/ppermute | solution.py:316
  83.6 20.0 %collective-permute-start.22 = (bf16[256,1024]{1,0:T(8,128)(2,1)S(1)}, bf16[256,1024]{1,0:T(8,128)(2,1)S(1)}, u32[]{:S(2)}, u32[]{:S(2)}) collective-permute-start(bf16[256,1024]{1,0:T(8,128)(2,1)S(1)} %collective-permute-done.17.refs_1_), channel_id=1, source_target_pairs={{0,4},{1,5},{2,6},{3,7},{4,0},{5,1},{6,2},{7,3},{8,12},{9,13},{10,... | collective-permute-start | bytes 1572872 | tf_op jit(solution)/shard_map/ppermute | solution.py:316
  84.6 19.0 %collective-permute-start.19 = (bf16[192,1024]{1,0:T(8,128)(2,1)S(1)}, bf16[192,1024]{1,0:T(8,128)(2,1)S(1)}, u32[]{:S(2)}, u32[]{:S(2)}) collective-permute-start(bf16[192,1024]{1,0:T(8,128)(2,1)S(1)} %slice.2851), channel_id=1, source_target_pairs={{0,1},{1,0},{2,3},{3,2},{4,5},{5,4},{6,7},{7,6},{8,9},{9,8},{10,11... | collective-permute-start | bytes 1179656 | tf_op jit(solution)/shard_map/ppermute | solution.py:316
  85.4 18.2 %collective-permute-start.21 = (bf16[192,1024]{1,0:T(8,128)(2,1)S(1)}, bf16[192,1024]{1,0:T(8,128)(2,1)S(1)}, u32[]{:S(2)}, u32[]{:S(2)}) collective-permute-start(bf16[192,1024]{1,0:T(8,128)(2,1)S(1)} %fusion.95), channel_id=1, source_target_pairs={{0,2},{1,3},{2,0},{3,1},{4,6},{5,7},{6,4},{7,5},{8,10},{9,11},{10,... | collective-permute-start | bytes 1179656 | tf_op jit(solution)/shard_map/ppermute | solution.py:316
  86.7 16.9 %collective-permute-start.24 = (bf16[128,1024]{1,0:T(8,128)(2,1)S(1)}, bf16[128,1024]{1,0:T(8,128)(2,1)S(1)}, u32[]{:S(2)}, u32[]{:S(2)}) collective-permute-start(bf16[128,1024]{1,0:T(8,128)(2,1)S(1)} %copy-done.70), channel_id=1, source_target_pairs={{0,4},{1,5},{2,6},{3,7},{4,0},{5,1},{6,2},{7,3},{8,12},{9,13},{10,... | collective-permute-start | bytes 786440 | tf_op jit(solution)/shard_map/ppermute | solution.py:316
  87.8 15.7 %collective-permute-start.23 = (bf16[128,1024]{1,0:T(8,128)(2,1)S(1)}, bf16[128,1024]{1,0:T(8,128)(2,1)S(1)}, u32[]{:S(2)}, u32[]{:S(2)}) collective-permute-start(bf16[128,1024]{1,0:T(8,128)(2,1)S(1)} %get-tuple-element.248), channel_id=1, source_target_pairs={{0,16},{1,17},{2,18},{3,19},{4,20},{5,21},{6,22},{7,23},{8,24},{9,... | collective-permute-start | bytes 786440 | tf_op jit(solution)/shard_map/ppermute | solution.py:316
  108.7 14.4 %collective-permute-start.25 = (bf16[192,1024]{1,0:T(8,128)(2,1)S(1)}, bf16[192,1024]{1,0:T(8,128)(2,1)S(1)}, u32[]{:S(2)}, u32[]{:S(2)}) collective-permute-start(bf16[192,1024]{1,0:T(8,128)(2,1)S(1)} %fusion.121), channel_id=1, source_target_pairs={{0,1},{1,0},{2,3},{3,2},{4,5},{5,4},{6,7},{7,6},{8,9},{9,8},{10,11... | collective-permute-start | bytes 1179656 | tf_op jit(solution)/shard_map/ppermute | solution.py:316
  142.1 16.3 %collective-permute-start.37 = (bf16[256,768]{1,0:T(8,128)(2,1)S(1)}, bf16[256,768]{1,0:T(8,128)(2,1)S(1)}, u32[]{:S(2)}, u32[]{:S(2)}) collective-permute-start(bf16[256,768]{1,0:T(8,128)(2,1)S(1)} %constant_dynamic-update-slice_fusion.2.refs_0_), channel_id=1, source_target_pairs={{0,4},{1,5},{2,6},{3,7},{4,0},{5,1},{6,2},{7,3},{8,12},{9,13},{10,... | collective-permute-start | bytes 1179656 | tf_op jit(solution)/shard_map/ppermute | solution.py:316
  143.7 16.8 %collective-permute-start.36 = (bf16[256,768]{1,0:T(8,128)(2,1)S(1)}, bf16[256,768]{1,0:T(8,128)(2,1)S(1)}, u32[]{:S(2)}, u32[]{:S(2)}) collective-permute-start(bf16[256,768]{1,0:T(8,128)(2,1)S(1)} %constant_dynamic-update-slice_fusion.2.refs_0_), channel_id=1, source_target_pairs={{0,8},{1,9},{2,10},{3,11},{4,12},{5,13},{6,14},{7,15},{8,0},{9,1},... | collective-permute-start | bytes 1179656 | tf_op jit(solution)/shard_map/ppermute | solution.py:316
  145.0 15.5 %collective-permute-start.33 = (bf16[192,1024]{1,0:T(8,128)(2,1)S(1)}, bf16[192,1024]{1,0:T(8,128)(2,1)S(1)}, u32[]{:S(2)}, u32[]{:S(2)}) collective-permute-start(bf16[192,1024]{1,0:T(8,128)(2,1)S(1)} %slice.2849), channel_id=1, source_target_pairs={{0,1},{1,0},{2,3},{3,2},{4,5},{5,4},{6,7},{7,6},{8,9},{9,8},{10,11... | collective-permute-start | bytes 1179656 | tf_op jit(solution)/shard_map/ppermute | solution.py:316
  145.2 15.3 %collective-permute-start.35 = (bf16[192,1024]{1,0:T(8,128)(2,1)S(1)}, bf16[192,1024]{1,0:T(8,128)(2,1)S(1)}, u32[]{:S(2)}, u32[]{:S(2)}) collective-permute-start(bf16[192,1024]{1,0:T(8,128)(2,1)S(1)} %fusion.93), channel_id=1, source_target_pairs={{0,2},{1,3},{2,0},{3,1},{4,6},{5,7},{6,4},{7,5},{8,10},{9,11},{10,... | collective-permute-start | bytes 1179656 | tf_op jit(solution)/shard_map/ppermute | solution.py:316
  161.5 15.3 %collective-permute-start.40 = (bf16[192,1024]{1,0:T(8,128)(2,1)S(1)}, bf16[192,1024]{1,0:T(8,128)(2,1)S(1)}, u32[]{:S(2)}, u32[]{:S(2)}) collective-permute-start(bf16[192,1024]{1,0:T(8,128)(2,1)S(1)} %fusion.122), channel_id=1, source_target_pairs={{0,2},{1,3},{2,0},{3,1},{4,6},{5,7},{6,4},{7,5},{8,10},{9,11},{10,... | collective-permute-start | bytes 1179656 | tf_op jit(solution)/shard_map/ppermute | solution.py:316
  162.7 14.1 %collective-permute-start.41 = (bf16[256,768]{1,0:T(8,128)(2,1)S(1)}, bf16[256,768]{1,0:T(8,128)(2,1)S(1)}, u32[]{:S(2)}, u32[]{:S(2)}) collective-permute-start(bf16[256,768]{1,0:T(8,128)(2,1)S(1)} %collective-permute-done.36.refs_1_), channel_id=1, source_target_pairs={{0,4},{1,5},{2,6},{3,7},{4,0},{5,1},{6,2},{7,3},{8,12},{9,13},{10,... | collective-permute-start | bytes 1179656 | tf_op jit(solution)/shard_map/ppermute | solution.py:316
  164.9 16.3 %collective-permute-start.39 = (bf16[192,1024]{1,0:T(8,128)(2,1)S(1)}, bf16[192,1024]{1,0:T(8,128)(2,1)S(1)}, u32[]{:S(2)}, u32[]{:S(2)}) collective-permute-start(bf16[192,1024]{1,0:T(8,128)(2,1)S(1)} %fusion.122), channel_id=1, source_target_pairs={{0,1},{1,0},{2,3},{3,2},{4,5},{5,4},{6,7},{7,6},{8,9},{9,8},{10,11... | collective-permute-start | bytes 1179656 | tf_op jit(solution)/shard_map/ppermute | solution.py:316
  177.0 14.9 %collective-permute-start.45 = (bf16[256,1024]{1,0:T(8,128)(2,1)S(1)}, bf16[256,1024]{1,0:T(8,128)(2,1)S(1)}, u32[]{:S(2)}, u32[]{:S(2)}) collective-permute-start(bf16[256,1024]{1,0:T(8,128)(2,1)S(1)} %constant_dynamic-update-slice_fusion.4.refs_0_), channel_id=1, source_target_pairs={{0,4},{1,5},{2,6},{3,7},{4,0},{5,1},{6,2},{7,3},{8,12},{9,13},{10,... | collective-permute-start | bytes 1572872 | tf_op jit(solution)/shard_map/ppermute | solution.py:316
  178.6 14.0 %collective-permute-start.44 = (bf16[256,1024]{1,0:T(8,128)(2,1)S(1)}, bf16[256,1024]{1,0:T(8,128)(2,1)S(1)}, u32[]{:S(2)}, u32[]{:S(2)}) collective-permute-start(bf16[256,1024]{1,0:T(8,128)(2,1)S(1)} %constant_dynamic-update-slice_fusion.4.refs_0_), channel_id=1, source_target_pairs={{0,8},{1,9},{2,10},{3,11},{4,12},{5,13},{6,14},{7,15},{8,0},{9,1},... | collective-permute-start | bytes 1572872 | tf_op jit(solution)/shard_map/ppermute | solution.py:316
  194.3 18.6 %collective-permute-start.49 = (bf16[256,1024]{1,0:T(8,128)(2,1)S(1)}, bf16[256,1024]{1,0:T(8,128)(2,1)S(1)}, u32[]{:S(2)}, u32[]{:S(2)}) collective-permute-start(bf16[256,1024]{1,0:T(8,128)(2,1)S(1)} %collective-permute-done.44.refs_1_), channel_id=1, source_target_pairs={{0,4},{1,5},{2,6},{3,7},{4,0},{5,1},{6,2},{7,3},{8,12},{9,13},{10,... | collective-permute-start | bytes 1572872 | tf_op jit(solution)/shard_map/ppermute | solution.py:316
  196.1 16.8 %collective-permute-start.48 = (bf16[192,1024]{1,0:T(8,128)(2,1)S(1)}, bf16[192,1024]{1,0:T(8,128)(2,1)S(1)}, u32[]{:S(2)}, u32[]{:S(2)}) collective-permute-start(bf16[192,1024]{1,0:T(8,128)(2,1)S(1)} %fusion.91), channel_id=1, source_target_pairs={{0,2},{1,3},{2,0},{3,1},{4,6},{5,7},{6,4},{7,5},{8,10},{9,11},{10,... | collective-permute-start | bytes 1179656 | tf_op jit(solution)/shard_map/ppermute | solution.py:316
  197.4 15.5 %collective-permute-start.46 = (bf16[192,1024]{1,0:T(8,128)(2,1)S(1)}, bf16[192,1024]{1,0:T(8,128)(2,1)S(1)}, u32[]{:S(2)}, u32[]{:S(2)}) collective-permute-start(bf16[192,1024]{1,0:T(8,128)(2,1)S(1)} %slice.2847), channel_id=1, source_target_pairs={{0,1},{1,0},{2,3},{3,2},{4,5},{5,4},{6,7},{7,6},{8,9},{9,8},{10,11... | collective-permute-start | bytes 1179656 | tf_op jit(solution)/shard_map/ppermute | solution.py:316
  197.5 15.4 %collective-permute-start.50 = (bf16[128,1024]{1,0:T(8,128)(2,1)S(1)}, bf16[128,1024]{1,0:T(8,128)(2,1)S(1)}, u32[]{:S(2)}, u32[]{:S(2)}) collective-permute-start(bf16[128,1024]{1,0:T(8,128)(2,1)S(1)} %get-tuple-element.289), channel_id=1, source_target_pairs={{0,16},{1,17},{2,18},{3,19},{4,20},{5,21},{6,22},{7,23},{8,24},{9,... | collective-permute-start | bytes 786440 | tf_op jit(solution)/shard_map/ppermute | solution.py:316
  227.4 14.3 %collective-permute-start.56 = (bf16[256,1024]{1,0:T(8,128)(2,1)S(1)}, bf16[256,1024]{1,0:T(8,128)(2,1)S(1)}, u32[]{:S(2)}, u32[]{:S(2)}) collective-permute-start(bf16[256,1024]{1,0:T(8,128)(2,1)S(1)} %collective-permute-done.53.refs_1_), channel_id=1, source_target_pairs={{0,4},{1,5},{2,6},{3,7},{4,0},{5,1},{6,2},{7,3},{8,12},{9,13},{10,... | collective-permute-start | bytes 1572872 | tf_op jit(solution)/shard_map/ppermute | solution.py:316
  284.2 25.4 %collective-permute-start.61 = (bf16[192,1024]{1,0:T(8,128)(2,1)S(1)}, bf16[192,1024]{1,0:T(8,128)(2,1)S(1)}, u32[]{:S(2)}, u32[]{:S(2)}) collective-permute-start(bf16[192,1024]{1,0:T(8,128)(2,1)S(1)} %slice.2843), channel_id=1, source_target_pairs={{0,1},{1,0},{2,3},{3,2},{4,5},{5,4},{6,7},{7,6},{8,9},{9,8},{10,11... | collective-permute-start | bytes 1179656 | tf_op jit(solution)/shard_map/ppermute | solution.py:316
  293.8 14.1 %collective-permute-start.66 = (bf16[2,128,1024]{2,1,0:T(8,128)(2,1)S(1)}, bf16[2,128,1024]{2,1,0:T(8,128)(2,1)S(1)}, u32[]{:S(2)}, u32[]{:S(2)}) collective-permute-start(bf16[2,128,1024]{2,1,0:T(8,128)(2,1)S(1)} %select_bitcast_fusion.19), channel_id=1, source_target_pairs={{0,4},{1,5},{2,6},{3,7},{4,0},{5,1},{6,2},{7,3},{8,12},{9,13},{10,... | collective-permute-start | bytes 1572872 | tf_op jit(solution)/shard_map/ppermute | solution.py:316
  328.3 15.6 %collective-permute-start.84 = (bf16[256,256]{1,0:T(8,128)(2,1)S(1)}, bf16[256,256]{1,0:T(8,128)(2,1)S(1)}, u32[]{:S(2)}, u32[]{:S(2)}) collective-permute-start(bf16[256,256]{1,0:T(8,128)(2,1)S(1)} %get-tuple-element.434), channel_id=1, source_target_pairs={{0,2},{1,3},{2,0},{3,1},{4,6},{5,7},{6,4},{7,5},{8,10},{9,11},{10,... | collective-permute-start | bytes 393224 | tf_op jit(solution)/shard_map/ppermute | solution.py:316
  329.6 14.3 %collective-permute-start.85 = (bf16[256,256]{1,0:T(8,128)(2,1)S(1)}, bf16[256,256]{1,0:T(8,128)(2,1)S(1)}, u32[]{:S(2)}, u32[]{:S(2)}) collective-permute-start(bf16[256,256]{1,0:T(8,128)(2,1)S(1)} %get-tuple-element.514), channel_id=1, source_target_pairs={{0,1},{1,0},{2,3},{3,2},{4,5},{5,4},{6,7},{7,6},{8,9},{9,8},{10,11... | collective-permute-start | bytes 393224 | tf_op jit(solution)/shard_map/ppermute | solution.py:316
  329.6 14.3 %collective-permute-start.83 = (bf16[256,256]{1,0:T(8,128)(2,1)S(1)}, bf16[256,256]{1,0:T(8,128)(2,1)S(1)}, u32[]{:S(2)}, u32[]{:S(2)}) collective-permute-start(bf16[256,256]{1,0:T(8,128)(2,1)S(1)} %get-tuple-element.515), channel_id=1, source_target_pairs={{0,3},{1,2},{2,1},{3,0},{4,7},{5,6},{6,5},{7,4},{8,11},{9,10},{10,... | collective-permute-start | bytes 393224 | tf_op jit(solution)/shard_map/ppermute | solution.py:316
  330.5 14.9 %collective-permute-start.72 = (bf16[128,1024]{1,0:T(8,128)(2,1)}, bf16[128,1024]{1,0:T(8,128)(2,1)S(1)}, u32[]{:S(2)}, u32[]{:S(2)}) collective-permute-start(bf16[128,1024]{1,0:T(8,128)(2,1)} %select_bitcast_fusion.37), channel_id=1, source_target_pairs={{0,16},{1,17},{2,18},{3,19},{4,20},{5,21},{6,22},{7,23},{8,24},{9,... | collective-permute-start | bytes 786440 | tf_op jit(solution)/shard_map/ppermute | solution.py:316
  367.6 16.9 %collective-permute-start.81 = (bf16[192,1024]{1,0:T(8,128)(2,1)S(1)}, bf16[192,1024]{1,0:T(8,128)(2,1)S(1)}, u32[]{:S(2)}, u32[]{:S(2)}) collective-permute-start(bf16[192,1024]{1,0:T(8,128)(2,1)S(1)} %get-tuple-element.427), channel_id=1, source_target_pairs={{0,2},{1,3},{2,0},{3,1},{4,6},{5,7},{6,4},{7,5},{8,10},{9,11},{10,... | collective-permute-start | bytes 1179656 | tf_op jit(solution)/shard_map/ppermute | solution.py:316
  369.2 15.3 %collective-permute-start.82 = (bf16[128,1024]{1,0:T(8,128)(2,1)S(1)}, bf16[128,1024]{1,0:T(8,128)(2,1)S(1)}, u32[]{:S(2)}, u32[]{:S(2)}) collective-permute-start(bf16[128,1024]{1,0:T(8,128)(2,1)S(1)} %select_bitcast_fusion.36), channel_id=1, source_target_pairs={{0,16},{1,17},{2,18},{3,19},{4,20},{5,21},{6,22},{7,23},{8,24},{9,... | collective-permute-start | bytes 786440 | tf_op jit(solution)/shard_map/ppermute | solution.py:316
  370.6 14.1 %collective-permute-start.86 = (bf16[2,128,1024]{2,1,0:T(8,128)(2,1)S(1)}, bf16[2,128,1024]{2,1,0:T(8,128)(2,1)S(1)}, u32[]{:S(2)}, u32[]{:S(2)}) collective-permute-start(bf16[2,128,1024]{2,1,0:T(8,128)(2,1)S(1)} %pad_maximum_fusion.13), channel_id=1, source_target_pairs={{0,4},{1,5},{2,6},{3,7},{4,0},{5,1},{6,2},{7,3},{8,12},{9,13},{10,... | collective-permute-start | bytes 1572872 | tf_op jit(solution)/shard_map/ppermute | solution.py:316
  373.7 46.1 %collective-permute-start.80 = (bf16[192,1024]{1,0:T(8,128)(2,1)S(1)}, bf16[192,1024]{1,0:T(8,128)(2,1)S(1)}, u32[]{:S(2)}, u32[]{:S(2)}) collective-permute-start(bf16[192,1024]{1,0:T(8,128)(2,1)S(1)} %slice.2839), channel_id=1, source_target_pairs={{0,1},{1,0},{2,3},{3,2},{4,5},{5,4},{6,7},{7,6},{8,9},{9,8},{10,11... | collective-permute-start | bytes 1179656 | tf_op jit(solution)/shard_map/ppermute | solution.py:316
  384.8 14.4 %collective-permute-start.89 = (bf16[2,128,1024]{2,1,0:T(8,128)(2,1)S(1)}, bf16[2,128,1024]{2,1,0:T(8,128)(2,1)S(1)}, u32[]{:S(2)}, u32[]{:S(2)}) collective-permute-start(bf16[2,128,1024]{2,1,0:T(8,128)(2,1)S(1)} %pad_maximum_fusion.14), channel_id=1, source_target_pairs={{0,4},{1,5},{2,6},{3,7},{4,0},{5,1},{6,2},{7,3},{8,12},{9,13},{10,... | collective-permute-start | bytes 1572872 | tf_op jit(solution)/shard_map/ppermute | solution.py:316
  385.3 14.1 %collective-permute-start.88 = (bf16[2,128,1024]{2,1,0:T(8,128)(2,1)S(1)}, bf16[2,128,1024]{2,1,0:T(8,128)(2,1)S(1)}, u32[]{:S(2)}, u32[]{:S(2)}) collective-permute-start(bf16[2,128,1024]{2,1,0:T(8,128)(2,1)S(1)} %add_convert_fusion.5), channel_id=1, source_target_pairs={{0,8},{1,9},{2,10},{3,11},{4,12},{5,13},{6,14},{7,15},{8,0},{9,1},... | collective-permute-start | bytes 1572872 | tf_op jit(solution)/shard_map/ppermute | solution.py:316
  402.7 14.4 %collective-permute-start.92 = (bf16[128,1024]{1,0:T(8,128)(2,1)S(1)}, bf16[128,1024]{1,0:T(8,128)(2,1)S(1)}, u32[]{:S(2)}, u32[]{:S(2)}) collective-permute-start(bf16[128,1024]{1,0:T(8,128)(2,1)S(1)} %select_bitcast_fusion.33), channel_id=1, source_target_pairs={{0,16},{1,17},{2,18},{3,19},{4,20},{5,21},{6,22},{7,23},{8,24},{9,... | collective-permute-start | bytes 786440 | tf_op jit(solution)/shard_map/ppermute | solution.py:316
  404.4 14.3 %collective-permute-start.93 = (bf16[2,128,1024]{2,1,0:T(8,128)(2,1)S(1)}, bf16[2,128,1024]{2,1,0:T(8,128)(2,1)S(1)}, u32[]{:S(2)}, u32[]{:S(2)}) collective-permute-start(bf16[2,128,1024]{2,1,0:T(8,128)(2,1)S(1)} %select_bitcast_fusion.15), channel_id=1, source_target_pairs={{0,4},{1,5},{2,6},{3,7},{4,0},{5,1},{6,2},{7,3},{8,12},{9,13},{10,... | collective-permute-start | bytes 1572872 | tf_op jit(solution)/shard_map/ppermute | solution.py:316
  420.9 14.7 %collective-permute-start.97 = (bf16[2,128,1024]{2,1,0:T(8,128)(2,1)}, bf16[2,128,1024]{2,1,0:T(8,128)(2,1)}, u32[]{:S(2)}, u32[]{:S(2)}) collective-permute-start(bf16[2,128,1024]{2,1,0:T(8,128)(2,1)} %select_bitcast_fusion.14), channel_id=1, source_target_pairs={{0,4},{1,5},{2,6},{3,7},{4,0},{5,1},{6,2},{7,3},{8,12},{9,13},{10,... | collective-permute-start | bytes 1572872 | tf_op jit(solution)/shard_map/ppermute | solution.py:316
  441.5 17.5 %collective-permute-start.99 = (bf16[128,1024]{1,0:T(8,128)(2,1)S(1)}, bf16[128,1024]{1,0:T(8,128)(2,1)S(1)}, u32[]{:S(2)}, u32[]{:S(2)}) collective-permute-start(bf16[128,1024]{1,0:T(8,128)(2,1)S(1)} %select_bitcast_fusion.32), channel_id=1, source_target_pairs={{0,16},{1,17},{2,18},{3,19},{4,20},{5,21},{6,22},{7,23},{8,24},{9,... | collective-permute-start | bytes 786440 | tf_op jit(solution)/shard_map/ppermute | solution.py:316
  445.4 13.8 %collective-permute-start.100 = (bf16[2,128,1024]{2,1,0:T(8,128)(2,1)S(1)}, bf16[2,128,1024]{2,1,0:T(8,128)(2,1)S(1)}, u32[]{:S(2)}, u32[]{:S(2)}) collective-permute-start(bf16[2,128,1024]{2,1,0:T(8,128)(2,1)S(1)} %copy-done.36), channel_id=1, source_target_pairs={{0,4},{1,5},{2,6},{3,7},{4,0},{5,1},{6,2},{7,3},{8,12},{9,13},{10,... | collective-permute-start | bytes 1572872 | tf_op jit(solution)/shard_map/ppermute | solution.py:316
  471.6 14.2 %collective-permute-start.109 = (bf16[2,128,1024]{2,1,0:T(8,128)(2,1)S(1)}, bf16[2,128,1024]{2,1,0:T(8,128)(2,1)S(1)}, u32[]{:S(2)}, u32[]{:S(2)}) collective-permute-start(bf16[2,128,1024]{2,1,0:T(8,128)(2,1)S(1)} %copy-done.33), channel_id=1, source_target_pairs={{0,8},{1,9},{2,10},{3,11},{4,12},{5,13},{6,14},{7,15},{8,0},{9,1},... | collective-permute-start | bytes 1572872 | tf_op jit(solution)/shard_map/ppermute | solution.py:316
  471.6 15.1 %collective-permute-start.108 = (bf16[2,144,1024]{2,1,0:T(8,128)(2,1)S(1)}, bf16[2,144,1024]{2,1,0:T(8,128)(2,1)S(1)}, u32[]{:S(2)}, u32[]{:S(2)}) collective-permute-start(bf16[2,144,1024]{2,1,0:T(8,128)(2,1)S(1)} %pad_maximum_fusion.6), channel_id=1, source_target_pairs={{0,4},{1,5},{2,6},{3,7},{4,0},{5,1},{6,2},{7,3},{8,12},{9,13},{10,... | collective-permute-start | bytes 1769480 | tf_op jit(solution)/shard_map/ppermute | solution.py:316
  487.9 14.4 %collective-permute-start.112 = (bf16[2,144,1024]{2,1,0:T(8,128)(2,1)S(1)}, bf16[2,144,1024]{2,1,0:T(8,128)(2,1)S(1)}, u32[]{:S(2)}, u32[]{:S(2)}) collective-permute-start(bf16[2,144,1024]{2,1,0:T(8,128)(2,1)S(1)} %pad_maximum_fusion.7), channel_id=1, source_target_pairs={{0,4},{1,5},{2,6},{3,7},{4,0},{5,1},{6,2},{7,3},{8,12},{9,13},{10,... | collective-permute-start | bytes 1769480 | tf_op jit(solution)/shard_map/ppermute | solution.py:316
  488.3 14.0 %collective-permute-start.111 = (bf16[2,144,1024]{2,1,0:T(8,128)(2,1)S(1)}, bf16[2,144,1024]{2,1,0:T(8,128)(2,1)S(1)}, u32[]{:S(2)}, u32[]{:S(2)}) collective-permute-start(bf16[2,144,1024]{2,1,0:T(8,128)(2,1)S(1)} %add_convert_fusion.3), channel_id=1, source_target_pairs={{0,8},{1,9},{2,10},{3,11},{4,12},{5,13},{6,14},{7,15},{8,0},{9,1},... | collective-permute-start | bytes 1769480 | tf_op jit(solution)/shard_map/ppermute | solution.py:316
  502.3 15.5 %collective-permute-start.115 = (bf16[2,128,1024]{2,1,0:T(8,128)(2,1)S(1)}, bf16[2,128,1024]{2,1,0:T(8,128)(2,1)S(1)}, u32[]{:S(2)}, u32[]{:S(2)}) collective-permute-start(bf16[2,128,1024]{2,1,0:T(8,128)(2,1)S(1)} %copy-done.35), channel_id=1, source_target_pairs={{0,4},{1,5},{2,6},{3,7},{4,0},{5,1},{6,2},{7,3},{8,12},{9,13},{10,... | collective-permute-start | bytes 1572872 | tf_op jit(solution)/shard_map/ppermute | solution.py:316
  (210 other events, 1523.1 us)

commit v4 on v3

--- a/solution.py
+++ b/solution.py
@@ -189,10 +189,10 @@
             ]
 
 
-def place(pieces, order, sizes, unpack=None):
+def place(pieces, order, sizes, unpack=None, missing=0):
     columns = pieces[0].shape[1]
     order = tuple(tuple(o) if isinstance(o, (list, tuple)) else (o,) for o in order)
-    count = sum(len(o) for o in order)
+    count = sum(len(o) for o in order) + missing
     whole = pl.BlockSpec(memory_space=pltpu.VMEM)
     shapes = [jax.ShapeDtypeStruct((count * rows, columns), BF) for rows in sizes]
     body = functools.partial(place_kernel, order, tuple(sizes))
@@ -212,6 +212,36 @@
         compiler_params=pltpu.CompilerParams(vmem_limit_bytes=VMEM_LIMIT),
         cost_estimate=pl.CostEstimate(flops=0, bytes_accessed=0, transcendentals=0),
     )(*pieces)
+
+
+def place_more_kernel(order, rows, buffer, piece, out, sem):
+    me = lax.axis_index("dp")
+    copies = []
+    for i, step in enumerate(order):
+        at = pl.multiple_of((me ^ step) * rows, rows)
+        copies.append(
+            pltpu.make_async_copy(
+                piece.at[pl.ds(i * rows, rows)], out.at[pl.ds(at, rows)], sem.at[i]
+            )
+        )
+    for copy in copies:
+        copy.start()
+    for copy in copies:
+        copy.wait()
+
+
+def place_more(buffer, piece, order):
+    anywhere = pl.BlockSpec(memory_space=pl.ANY)
+    return pl.pallas_call(
+        functools.partial(place_more_kernel, tuple(order), piece.shape[0] // len(order)),
+        out_shape=jax.ShapeDtypeStruct(buffer.shape, buffer.dtype),
+        in_specs=[anywhere, pl.BlockSpec(memory_space=pltpu.VMEM)],
+        out_specs=anywhere,
+        scratch_shapes=[pltpu.SemaphoreType.DMA((len(order),))],
+        input_output_aliases={0: 0},
+        compiler_params=pltpu.CompilerParams(vmem_limit_bytes=VMEM_LIMIT),
+        cost_estimate=pl.CostEstimate(flops=0, bytes_accessed=0, transcendentals=0),
+    )(buffer, piece)
 
 
 def split_kernel(n_seq, plan, part, smalls, *refs):
@@ -367,7 +397,7 @@
     def both(halves):
         return jnp.concatenate(halves, axis=0)
 
-    def reduce_seq(left, right, moves=(), gate=None):
+    def reduce_seq(left, right, moves=(), gate=None, marks=None):
         near, far = left
         moving = launch(moves, far if gate is None else gate)
         size = near.shape[0] // 2
@@ -379,6 +409,8 @@
         total = [None] + [
             chip(far[i * 2 * size : (i + 1) * 2 * size], False) for i in range(len(x_steps) - 1)
         ]
+        if marks is not None:
+            marks.append(total[-1])
         for i, bit in enumerate(seq_bits[1:]):
             middle = len(total) // 2
             got = [swap(t.astype(BF), bit) for t in total[middle:]]
@@ -469,6 +501,14 @@
 
                 def last(self):
                     return [(self, "y_near", self.near, n_seq)]
+
+                def open(self, rows):
+                    pieces = [self.line, self.near, self.y_line]
+                    opened = place(pieces, [[0, 4], [2, 6], [1, 5]], (rows,), missing=2)[0]
+                    return [(self, "opened", opened, 0)]
+
+                def closed(self):
+                    return place_more(self.opened, self.y_near, (3, 7))
 
                 def ready(self, sizes):
                     return [(self, "full", self.whole(sizes)[0], 0)]
@@ -580,9 +620,9 @@
                     return shrink_0.middle() + expand_0.ready((block_rows,))
                 if (layer, point) == (0, "active"):
                     expand_all.append(expand_0.full)
-                    return shrink_0.last() + qkv_1.far() + outs[1].step(2)
+                    return shrink_0.last() + qkv_1.far() + outs[1].step(2) + shrink_0.open(hidden_part)
                 if (layer, point) == (0, "shrink"):
-                    shrink_all.append(shrink_0.whole((hidden_part,))[0])
+                    shrink_all.append(shrink_0.closed())
                     return qkv_1.middle() + outs[1].step(4)
                 if (layer, point) == (1, "group"):
                     return qkv_1.last() + expand_1.far()
@@ -596,9 +636,9 @@
                     return shrink_1.middle() + expand_1.ready((block_rows,))
                 if (layer, point) == (1, "active"):
                     expand_all.append(expand_1.full)
-                    return shrink_1.last()
+                    return shrink_1.last() + shrink_1.open(hidden_part)
                 if (layer, point) == (1, "shrink"):
-                    shrink_all.append(shrink_1.whole((hidden_part,))[0])
+                    shrink_all.append(shrink_1.closed())
                 return []
         else:
             qkv_all, expand_all, shrink_all = [], [], []
@@ -847,7 +887,8 @@
                 )
 
             def layer_rows():
-                vectors[0], inner_vectors[0] = token_rows(), hidden_rows(inner_sums)
+                vectors[0] = jnp.concatenate([token_rows()] + head_rows, axis=0)
+                inner_vectors[0] = hidden_rows(inner_sums)
                 return jnp.concatenate(vectors + [lex_row] + inner_vectors, axis=0)
 
             above = big[layer + 1] if special and layer + 1 < layers else None
@@ -862,14 +903,17 @@
             second_group = both(halves)
             inner_group = both(low_inner)
             shrink_grad = dot(active, second_group, 0, 0).astype(BF)
-            expand_grad = dot(normed_group, inner_group, 0, 0).astype(BF)
-            moves = []
+            moves, marks = [], []
             if special:
                 big[layer] = mine = Grads()
-                mine.shrink, mine.expand = Sums([shrink_grad]), Sums([expand_grad])
+                mine.shrink = Sums([shrink_grad])
                 moves = (above.qkv.last() if above else []) + mine.shrink.first()
-            summed = reduce_seq(low_inner, (expand_all[layer], (1, 1)), moves)
-            inner_sums = sum(column_sums(half) for half in low_inner)
+            summed = reduce_seq(low_inner, (expand_all[layer], (1, 1)), moves, None, marks)
+            inner_group = after(inner_group, *marks)
+            expand_grad = dot(normed_group, inner_group, 0, 0).astype(BF)
+            if special:
+                mine.expand = Sums([expand_grad])
+            inner_sums = column_sums(inner_group)
             grad_normed = grad_second + summed
             grad_first, ngain, nbias = norm_back(grad_normed, gain_one, rhat_one, inverse_one)
             low_first = grad_first.astype(BF)
@@ -877,88 +921,46 @@
                 moves = mine.shrink.middle()
             first_group = both(gather_seq(low_first, moves, summed))
             if special:
+                gate = mine.shrink.near
                 moves = mine.shrink.last() + mine.expand.first()
-                moving = launch(moves, first_group)
+                moving = launch(moves, gate)
             low_attn = dot(first_group, out_all[layer], 1, 1).astype(BF)
             out_grad = dot(attended, first_group, 0, 0).astype(BF)
             if special:
                 quarter = dim // n_seq
                 pieces = [out_grad[:, s * quarter : (s + 1) * quarter] for s in range(n_seq)]
-                if layer == 0:
-                    done = [
-                        g.rows().astype(BF) for m in big[1:] for g in (m.expand, m.qkv)
-                    ]
-                    for s in range(n_seq):
-                        rows = jnp.concatenate([g[s * part : (s + 1) * part] for g in done], axis=1)
-                        cut = [
-                            rows[:, i : i + quarter] for i in range(0, rows.shape[1], quarter)
-                        ]
-                        pieces[s] = jnp.concatenate([pieces[s]] + cut, axis=0)
-                pieces = exchange_steps(pieces)
-                if layer == 0:
-                    upper_rows = by_origin([p[width:] for p in pieces])
-                    pieces = [p[:width] for p in pieces]
-                pieces = [p.reshape(pairs_here, 1, 2 * HEAD, quarter) for p in by_origin(pieces)]
-                out_columns = jnp.concatenate(pieces, axis=1).reshape(dim, quarter)
+                out_back = Back(pieces)
+                moving += launch(out_back.moves(), first_group)
             grad_qkv = attend_back(qkv, starts, row_max, row_sum, low_attn)
             if special:
                 grad_qkv = settle(grad_qkv, moving)
-            qkv_grad = dot(group, grad_qkv, 0, 0).astype(BF)
+
+            def late_grads(grad_qkv):
+                qkv_grad = dot(group, grad_qkv, 0, 0).astype(BF)
+                if special:
+                    pieces = out_back.got()
+                    pieces = [p.reshape(pairs_here, 1, 2 * HEAD, quarter) for p in by_origin(pieces)]
+                    out_columns = jnp.concatenate(pieces, axis=1).reshape(dim, quarter)
+                    mine.qkv = Sums([qkv_grad, out_columns])
+                return qkv_grad
+
+            gate, moves, marks = grad_qkv, [], []
+            if special and layer == 0:
+                late_grads(grad_qkv)
+                tail_moving = launch(mine.qkv.first() + mine.expand.middle_z(), grad_qkv)
+            elif special:
+                moves = mine.expand.middle()
+            left = (grad_qkv[:chip_rows], grad_qkv[chip_rows:])
+            summed = reduce_seq(left, (qkv_all[layer], (1, 1)), moves, gate, marks)
+            grad_qkv = after(grad_qkv, *marks)
             qkv_sums = column_sums(grad_qkv)
-            if special:
-                joined = [qkv_grad, out_columns]
-                extra = 0
-                if layer == 0:
-                    extra = 16
-                    rows = jnp.concatenate(
-                        [
-                            qkv_sums[:width].reshape(pairs_here, 2 * HEAD),
-                            qkv_sums[2 * width :].reshape(pairs_here, 2 * HEAD),
-                        ],
-                        axis=1,
-                    )
-                    hot = (jnp.arange(n_seq) == seq)[None, :, None]
-                    rows = jnp.where(hot, rows[:, None, :], 0.0).reshape(n_dp, 1, 4 * HEAD)
-                    rows = jnp.pad(rows, ((0, 0), (0, 15), (0, 3 * width - 4 * HEAD))).astype(BF)
-                    joined = [
-                        jnp.pad(g.reshape(n_dp, block_rows, -1), ((0, 0), (0, 16), (0, 0)))
-                        for g in joined
-                    ]
-                    joined[0] = jnp.concatenate([joined[0][:, :block_rows], rows], axis=1)
-                mine.qkv = Sums(joined, block_rows + extra)
-                if layer:
-                    moves = mine.expand.middle()
-                else:
-                    table = Table(layer_rows(), scores)
-                    qkv_grad = settle(qkv_grad, launch(table.step(), grad_qkv))
-                    moves = mine.qkv.first() + mine.expand.middle_z() + table.step()
-            else:
-                moves = []
-            left = after(grad_qkv, qkv_grad)
-            left = (left[:chip_rows], left[chip_rows:])
-            summed = reduce_seq(left, (qkv_all[layer], (1, 1)), moves, qkv_grad)
+            if layer or not special:
+                qkv_grad = late_grads(grad_qkv)
+            head_rows = [columns_row(qkv_sums[:width]), columns_row(qkv_sums[2 * width :])]
             if special and layer == 0:
-
-                def back_of(grads, extra=0):
-                    grads = [g.astype(BF) for g in grads]
-                    blocks = []
-                    for s in range(n_seq):
-                        rows = [g[s * part : (s + 1) * part] for g in grads]
-                        if extra:
-                            rows = [jnp.concatenate([r, g[block_rows:]], axis=0) for r, g in zip(rows, grads)]
-                        blocks.append(jnp.concatenate(rows, axis=1) if len(rows) > 1 else rows[0])
-                    return Back(blocks)
-
-                gate = summed
-                moves = mine.qkv.middle() + table.step()
-                gate = settle(gate, launch(moves, gate))
-                moves = mine.qkv.last() + mine.expand.middle_y() + table.group_step()
-                gate = settle(gate, launch(moves, gate))
-                last_back = back_of([mine.qkv.rows()], 16)
-                moves = mine.expand.last() + last_back.moves()
-                gate = settle(gate, launch(moves, gate))
-                expand_back = back_of([mine.expand.rows()])
-                settle(gate, launch(expand_back.moves(), gate))
+                table = Table(layer_rows(), scores)
+                for home, name, array in launch(table.step(), marks[0]):
+                    setattr(home, name, array)
             if not special:
                 big[layer] = (
                     scatter_dp(shrink_grad),
@@ -967,84 +969,105 @@
                     scatter_dp(qkv_grad),
                 )
             grad_now = grad_first + summed
-            head_rows = [columns_row(qkv_sums[:width]), columns_row(qkv_sums[2 * width :])]
             if layer or not special:
-                vectors[layer] = token_rows()
-                if layer:
-                    vectors[layer] = jnp.concatenate([vectors[layer]] + head_rows, axis=0)
+                vectors[layer] = jnp.concatenate([token_rows()] + head_rows, axis=0)
                 inner_vectors[layer] = hidden_rows(inner_sums)
 
         tokens_grad = grad_now.astype(BF)
 
         counts = [v.shape[0] for v in vectors] + [1] + [n_seq] * layers
+
+        def small_outs(table, inner_tables=None):
+            cut = [0]
+            for count in counts:
+                cut.append(cut[-1] + count)
+            tables = [table[cut[i] : cut[i + 1]] for i in range(len(counts))]
+            inner_tables = inner_tables or tables[layers + 1 :]
+            inner_out = jnp.stack(
+                [lax.dynamic_index_in_dim(t, seq, 0, keepdims=False) for t in inner_tables]
+            )
+            scores = table[-1:, : queries.shape[1]]
+            stats = tables[layers][0, :2] / (rows_here * n_dev)
+            vector_outs = [
+                jnp.stack([own_part(tables[i][row]) for i in range(layers)])
+                for row in (6, 7, 0, 1, 2, 3, 4, 5)
+            ]
+            return [scores, stats, inner_out] + vector_outs
+
+        def stacked(arrays):
+            return jnp.stack([a.astype(F32) for a in arrays])
+
+        def head_outs(gots):
+            outs = [
+                stacked(
+                    [
+                        unsplit([g[:, i * width : (i + 1) * width] for g in got], 2 * HEAD)
+                        for got in gots
+                    ]
+                )
+                for i in range(3)
+            ]
+            return outs + [
+                stacked([jnp.concatenate([g[:, 3 * width :] for g in got], axis=1) for got in gots])
+            ]
+
         if special:
-            table = table.whole()
-            scores = table[-1:, : scores.shape[1]]
+
+            def back_of(grads):
+                grads = [g.astype(BF) for g in grads]
+                return Back(
+                    [
+                        jnp.concatenate([g[s * part : (s + 1) * part] for g in grads], axis=1)
+                        for s in range(n_seq)
+                    ]
+                )
+
+            low = big[0]
+            gate = settle(marks[0], tail_moving)
+            moves = low.qkv.middle()
+            for home, name, array in launch(table.step(), gate):
+                setattr(home, name, array)
+            gate, tokens_grad = settle([gate, tokens_grad], launch(moves + table.step(), gate))
+            moves = low.qkv.last() + low.expand.middle_y() + table.group_step()
+            gate = settle(gate, launch(moves, gate))
+            back = back_of([low.qkv.rows()] + [g.rows() for m in big[1:] for g in (m.expand, m.qkv)])
+            moving = launch(low.expand.last(), gate)
+            gate = settle(gate, launch(back.moves(), gate))
+            got = by_origin(back.got())
+            size = 3 * width + dim // n_seq
+            gots, upper_expand = [[g[:, :size] for g in got]], []
+            for layer in range(1, layers):
+                at = size + (layer - 1) * (own_hidden + size)
+                upper_expand.append(
+                    unsplit([g[:, at : at + own_hidden] for g in got], hidden_part).astype(F32)
+                )
+                gots.append([g[:, at + own_hidden : at + own_hidden + size] for g in got])
+            smalls = small_outs(table.whole())
+            heads = head_outs(gots)
+            shrink_out = stacked([m.shrink.rows() for m in big])
+            ready = settle(smalls + heads + upper_expand + [shrink_out, gate], moving)
+            smalls, heads = ready[:11], ready[11:15]
+            upper_expand, shrink_out, gate = ready[15:-2], ready[-2], ready[-1]
+            back = back_of([low.expand.rows()])
+            settle(gate, launch(back.moves(), gate))
+            expand_out = stacked([unsplit(by_origin(back.got()), hidden_part)] + upper_expand)
         else:
             table = reduce_rows(jnp.concatenate(vectors + [lex_row], axis=0), scores)
-            scores = table[-1:, : scores.shape[1]]
             inner = reduce_rows(jnp.concatenate(inner_vectors, axis=0))
-            last = reduce_rows(jnp.concatenate(head_rows, axis=0))
-        cut = [0]
-        for count in counts:
-            cut.append(cut[-1] + count)
-        tables = [table[cut[i] : cut[i + 1]] for i in range(len(counts))]
-        if special:
-            inner_tables = tables[layers + 1 :]
-        else:
-            inner_tables = [inner[i * n_seq : (i + 1) * n_seq] for i in range(layers)]
-        lexical_stats = tables[layers][0, :2] / (rows_here * n_dev)
-        inner_out = jnp.stack(
-            [lax.dynamic_index_in_dim(t, seq, 0, keepdims=False) for t in inner_tables]
-        )
-
-        layer_outs = []
-        for layer in range(layers):
-            if special:
-                shrink_rows = big[layer].shrink.rows()
-                if layer:
-                    count = (own_hidden + 3 * width + quarter) // quarter
-                    got = []
-                    for g in upper_rows:
-                        g = g[(layer - 1) * count * part : layer * count * part]
-                        cut = [g[i * part : (i + 1) * part] for i in range(count)]
-                        got.append(jnp.concatenate(cut, axis=1))
-                    expand_out = [g[:, :own_hidden] for g in got]
-                    got = [g[:, own_hidden:] for g in got]
-                else:
-                    got = last_back.got()
-                    source = seq ^ lax.rem(dp, n_seq)
-                    row = got[0][part : part + 1, : 4 * HEAD]
-                    for step in range(1, n_seq):
-                        row = jnp.where(source == step, got[step][part : part + 1, : 4 * HEAD], row)
-                    last = row.reshape(2, 2 * HEAD).astype(F32)
-                    got = by_origin([g[:part] for g in got])
-                    expand_out = by_origin(expand_back.got())
-                out_out = jnp.concatenate([g[:, 3 * width :] for g in got], axis=1)
-            else:
-                shrink_rows, expand_rows, out_out, qkv_rows = big[layer]
-                got, expand_out = by_origin(rows_back(qkv_rows)), by_origin(rows_back(expand_rows))
-            layer_outs.append(
-                [
-                    unsplit([g[:, i * width : (i + 1) * width] for g in got], 2 * HEAD)
-                    for i in range(3)
-                ]
-                + [out_out, unsplit(expand_out, hidden_part), shrink_rows]
-            )
-        def vector_out(index):
-            if index < 2:
-                return jnp.stack(
-                    [own_part(tables[i][6 + index] if i else last[index]) for i in range(layers)]
-                )
-            return jnp.stack([own_part(tables[i][index - 2]) for i in range(layers)])
-
-        big_out = [jnp.stack([lo[i].astype(F32) for lo in layer_outs]) for i in range(6)]
+            smalls = small_outs(table, [inner[i * n_seq : (i + 1) * n_seq] for i in range(layers)])
+            gots = [by_origin(rows_back(b[3])) for b in big]
+            gots = [[jnp.concatenate([g, g[:, :0]], axis=1) for g in got] for got in gots]
+            heads = head_outs(gots)[:3] + [stacked([b[2] for b in big])]
+            expand_out = stacked([unsplit(by_origin(rows_back(b[1])), hidden_part) for b in big])
+            shrink_out = stacked([b[0] for b in big])
+        scores, lexical_stats, inner_out = smalls[:3]
+        vector_outs = smalls[3:]
         return (
             encoded, scores, lexical_stats, tokens_grad,
-            big_out[0], vector_out(0), big_out[1], big_out[2], vector_out(1),
-            big_out[3], vector_out(2), vector_out(3), vector_out(4),
-            big_out[4], inner_out, big_out[5], vector_out(5),
-            vector_out(6), vector_out(7),
+            heads[0], vector_outs[0], heads[1], heads[2], vector_outs[1],
+            heads[3], vector_outs[2], vector_outs[3], vector_outs[4],
+            expand_out, inner_out, shrink_out, vector_outs[5],
+            vector_outs[6], vector_outs[7],
         )
 
     rows = P(AXES, None)

time: 553 us -> 540 us (0.976)
  waiting for transfers between devices: 228 us -> 198 us
  other arithmetic: 52.3 us -> 59.9 us
    ppermute x126, waiting for transfers between devices: 228 us -> 198 us  [swap(): return lax.ppermute(array, AXES, [(p, p ^ bit) for p in range(n_dev)])]
    another operation x16 -> x17, other arithmetic: 9.83 us -> 14.1 us  [the longest x8 8.9 us: stacked(): return jnp.stack([a.astype(F32) for a in arrays])]
    unnamed x344 -> x318, local copies, waits for them, and re-layouts: 11.1 us -> 12.7 us
  transfers between devices with their start and end apart: 126 -> 126, of which waited for: 60 -> 55; matrix products, arithmetic and copies ran while one was open for 18% -> 21% of each run, Pallas kernels for 9% -> 11%
where the time goes in v4:
time: 540 us; the launch traced here: 530 us
  waiting for transfers between devices  198 us (37%)
  starting transfers between devices  107 us (20%)
  matrix products  72.2 us (13%)
  Pallas kernels  62.6 us (12%)
  other arithmetic  59.9 us (11%)
  local copies, waits for them, and re-layouts  24.7 us (5%)
    ppermute x126, waiting for transfers between devices, swap(): return lax.ppermute(array, AXES, [(p, p ^ bit) for p in range(n_dev)])  198 us
    ppermute x126, starting transfers between devices, swap(): return lax.ppermute(array, AXES, [(p, p ^ bit) for p in range(n_dev)])  107 us
    dot_general x37, matrix products, dot(): lax.dot_general(left, right, (((left_dim,), (right_dim,)), ((), ())), pre...  70.8 us
    pallas_call x2, Pallas kernels, attend_back(): pl.pallas_call(functools.partial(attend_back_kernel, math.gcd(tokens, 768...  20.2 us
    pallas_call x6, Pallas kernels, place(): pl.pallas_call(body, out_shape=tuple(shapes), in_specs=[whole] * len(piec...  17.1 us
    pallas_call x2, Pallas kernels, attend(): pl.pallas_call(functools.partial(attend_kernel, math.gcd(tokens, 768)), o...  13.1 us
    unnamed x318, local copies, waits for them, and re-layouts  12.7 us
  transfers between devices with their start and end apart: 126, of which 55 were waited for; matrix products, arithmetic and copies ran while one was open for 21% of the time, Pallas kernels for 11%

profile of v4, /device:TPU:0, one launch (start us, length us, event | category | flops | bytes accessed | tf_op | source)
XLA Modules:
  0.0 529.6 jit_solution(13054677953350982979)
XLA Ops:
  13.6 2.8 collective-permute-start.8
  16.4 10.7 %collective-permute-done.8 = bf16[144,768]{1,0:T(8,128)(2,1)S(1)} collective-permute-done((bf16[144,768]{1,0:T(8,128)(2,1)}, bf16[144,768]{1,0:T(8,128)(2,1)S(1)}, u32[]{:S(2)}, u32[]{:S(2)}) %collective-permute-start.8) | collective-permute-done | bytes 221216 | tf_op jit(solution)/shard_map/ppermute | solution.py:346
  44.8 3.1 collective-permute-start.13
  49.1 3.1 collective-permute-done.9.refs_2_
  53.9 4.2 collective-permute-done.13
  58.1 3.2 collective-permute-done.11.refs_3_
  64.6 2.8 shard_map.379
  68.2 3.1 collective-permute-start.16
  71.4 3.9 add_convert_fusion.1.qkv_ref
  75.3 6.5 %shard_map.380 = (bf16[768,256]{1,0:T(8,128)(2,1)}, f32[4,768]{1,0:T(4,128)}, f32[4,768]{1,0:T(4,128)}) custom-call(bf16[768,768]{1,0:T(8,128)(2,1)} %add_convert_fusion.1.qkv_ref, s32[768,1]{1,0:T(8,128)} %broadcast_in_dim.133.col_ref, s32[1,768]{1,0:T(1,128)} %broadcast_in_dim.121.row_ref), custom_call_target="tpu_custom_call" | custom-call | flops 6039797760 | bytes 3145728 | tf_op jit(solution)/shard_map/pallas_call | solution.py:108
  90.5 13.0 %collective-permute-done.24 = bf16[128,1024]{1,0:T(8,128)(2,1)S(1)} collective-permute-done((bf16[128,1024]{1,0:T(8,128)(2,1)S(1)}, bf16[128,1024]{1,0:T(8,128)(2,1)S(1)}, u32[]{:S(2)}, u32[]{:S(2)}) %collective-permute-start.24) | collective-permute-done | bytes 262176 | tf_op jit(solution)/shard_map/ppermute | solution.py:346
  109.7 3.0 shard_map.381
  112.7 5.0 collective-permute-done.26
  123.1 2.8 shard_map.382.buffer
  125.9 3.9 multiply_convert_fusion.3
  129.8 3.5 multiply_convert_fusion.2
  138.1 2.7 fusion.183
  147.1 10.2 %collective-permute-done.38 = bf16[128,1024]{1,0:T(8,128)(2,1)S(1)} collective-permute-done((bf16[128,1024]{1,0:T(8,128)(2,1)S(1)}, bf16[128,1024]{1,0:T(8,128)(2,1)S(1)}, u32[]{:S(2)}, u32[]{:S(2)}) %collective-permute-start.38) | collective-permute-done | bytes 262176 | tf_op jit(solution)/shard_map/ppermute | solution.py:346
  164.0 11.7 %collective-permute-done.42 = bf16[128,1024]{1,0:T(8,128)(2,1)S(1)} collective-permute-done((bf16[128,1024]{1,0:T(8,128)(2,1)S(1)}, bf16[128,1024]{1,0:T(8,128)(2,1)S(1)}, u32[]{:S(2)}, u32[]{:S(2)}) %collective-permute-start.42) | collective-permute-done | bytes 262176 | tf_op jit(solution)/shard_map/ppermute | solution.py:346
  180.2 4.1 add_convert_fusion.qkv_ref
  184.3 6.6 %shard_map.385 = (bf16[768,256]{1,0:T(8,128)(2,1)}, f32[4,768]{1,0:T(4,128)}, f32[4,768]{1,0:T(4,128)}) custom-call(bf16[768,768]{1,0:T(8,128)(2,1)} %add_convert_fusion.qkv_ref, s32[768,1]{1,0:T(8,128)} %broadcast_in_dim.133.col_ref, s32[1,768]{1,0:T(1,128)} %broadcast_in_dim.121.row_ref), custom_call_target="tpu_custom_call" | custom-call | flops 6039797760 | bytes 3145728 | tf_op jit(solution)/shard_map/pallas_call | solution.py:108
  198.9 12.7 %collective-permute-done.50 = bf16[128,1024]{1,0:T(8,128)(2,1)S(1)} collective-permute-done((bf16[128,1024]{1,0:T(8,128)(2,1)S(1)}, bf16[128,1024]{1,0:T(8,128)(2,1)S(1)}, u32[]{:S(2)}, u32[]{:S(2)}) %collective-permute-start.50) | collective-permute-done | bytes 262176 | tf_op jit(solution)/shard_map/ppermute | solution.py:346
  214.7 3.0 shard_map.386
  217.7 6.2 %collective-permute-done.52 = bf16[192,1024]{1,0:T(8,128)(2,1)S(1)} collective-permute-done((bf16[192,1024]{1,0:T(8,128)(2,1)S(1)}, bf16[192,1024]{1,0:T(8,128)(2,1)S(1)}, u32[]{:S(2)}, u32[]{:S(2)}) %collective-permute-start.52) | collective-permute-done | bytes 393248 | tf_op jit(solution)/shard_map/ppermute | solution.py:346
  227.7 2.9 shard_map.387.buffer
  230.6 3.6 multiply_convert_fusion.1
  234.2 3.3 multiply_convert_fusion
  237.5 3.0 collective-permute-done.56.piece
  243.2 2.7 fusion.185
  250.5 10.1 %collective-permute-done.59 = bf16[192,1024]{1,0:T(8,128)(2,1)} collective-permute-done((bf16[192,1024]{1,0:T(8,128)(2,1)}, bf16[192,1024]{1,0:T(8,128)(2,1)}, u32[]{:S(2)}, u32[]{:S(2)}) %collective-permute-start.59) | collective-permute-done | bytes 393248 | tf_op jit(solution)/shard_map/ppermute | solution.py:346
  272.6 3.8 collective-permute-done.62
  276.4 3.8 fusion.5
  281.9 3.1 convolution_convert_fusion.3
  295.7 3.0 convolution_convert_fusion.2
  299.8 5.1 collective-permute-done.66
  312.2 7.5 %collective-permute-done.68 = bf16[192,1024]{1,0:T(8,128)(2,1)S(1)} collective-permute-done((bf16[192,1024]{1,0:T(8,128)(2,1)S(1)}, bf16[192,1024]{1,0:T(8,128)(2,1)S(1)}, u32[]{:S(2)}, u32[]{:S(2)}) %collective-permute-start.68) | collective-permute-done | bytes 393248 | tf_op jit(solution)/shard_map/ppermute | solution.py:346
  329.2 10.2 %shard_map.389 = bf16[768,768]{1,0:T(8,128)(2,1)} custom-call(bf16[768,768]{1,0:T(8,128)(2,1)} %add_convert_fusion.qkv_ref, s32[768,1]{1,0:T(8,128)} %broadcast_in_dim.133.col_ref, s32[1,768]{1,0:T(1,128)} %broadcast_in_dim.121.row_ref, f32[4,768]{1,0:T(4,128)} %get-tuple-element.341.max_ref, f32[4,768]{1,0:T(4,128)} %get-tuple-element.342.sum_ref, ...), custom_call_target="tpu_custom_call" | custom-call | flops 6039797760 | bytes 3145728 | tf_op jit(solution)/shard_map/pallas_call | solution.py:127
  352.7 4.5 collective-permute-done.81
  367.9 10.8 %collective-permute-done.85 = bf16[128,1024]{1,0:T(8,128)(2,1)S(1)} collective-permute-done((bf16[128,1024]{1,0:T(8,128)(2,1)S(1)}, bf16[128,1024]{1,0:T(8,128)(2,1)S(1)}, u32[]{:S(2)}, u32[]{:S(2)}) %collective-permute-start.85) | collective-permute-done | bytes 262176 | tf_op jit(solution)/shard_map/ppermute | solution.py:346
  386.8 6.5 %collective-permute-done.89 = bf16[2,128,1024]{2,1,0:T(8,128)(2,1)S(1)} collective-permute-done((bf16[2,128,1024]{2,1,0:T(8,128)(2,1)S(1)}, bf16[2,128,1024]{2,1,0:T(8,128)(2,1)S(1)}, u32[]{:S(2)}, u32[]{:S(2)}) %collective-permute-start.89) | collective-permute-done | bytes 524320 | tf_op jit(solution)/shard_map/ppermute | solution.py:346
  399.5 3.0 convolution_convert_fusion
  404.0 6.9 %collective-permute-done.92 = bf16[128,1024]{1,0:T(8,128)(2,1)S(1)} collective-permute-done((bf16[128,1024]{1,0:T(8,128)(2,1)S(1)}, bf16[128,1024]{1,0:T(8,128)(2,1)S(1)}, u32[]{:S(2)}, u32[]{:S(2)}) %collective-permute-start.92) | collective-permute-done | bytes 262176 | tf_op jit(solution)/shard_map/ppermute | solution.py:346
  418.1 8.0 %collective-permute-done.95 = bf16[192,1024]{1,0:T(8,128)(2,1)S(1)} collective-permute-done((bf16[192,1024]{1,0:T(8,128)(2,1)S(1)}, bf16[192,1024]{1,0:T(8,128)(2,1)S(1)}, u32[]{:S(2)}, u32[]{:S(2)}) %collective-permute-start.95) | collective-permute-done | bytes 393248 | tf_op jit(solution)/shard_map/ppermute | solution.py:346
  435.2 10.0 %shard_map.390 = bf16[768,768]{1,0:T(8,128)(2,1)} custom-call(bf16[768,768]{1,0:T(8,128)(2,1)} %add_convert_fusion.1.qkv_ref, s32[768,1]{1,0:T(8,128)} %broadcast_in_dim.133.col_ref, s32[1,768]{1,0:T(1,128)} %broadcast_in_dim.121.row_ref, f32[4,768]{1,0:T(4,128)} %get-tuple-element.337.max_ref, f32[4,768]{1,0:T(4,128)} %get-tuple-element.338.sum_ref, ...), custom_call_target="tpu_custom_call" | custom-call | flops 6039797760 | bytes 3145728 | tf_op jit(solution)/shard_map/pallas_call | solution.py:127
  469.0 2.7 collective-permute-done.111
  481.2 7.6 %collective-permute-done.113 = f32[25,128]{1,0:T(8,128)S(1)} collective-permute-done((f32[25,128]{1,0:T(8,128)S(1)}, f32[25,128]{1,0:T(8,128)S(1)}, u32[]{:S(2)}, u32[]{:S(2)}) %collective-permute-start.113) | collective-permute-done | bytes 12832 | tf_op jit(solution)/shard_map/ppermute | solution.py:346
  495.9 6.3 %collective-permute-done.114 = bf16[128,1024]{1,0:T(8,128)(2,1)S(1)} collective-permute-done((bf16[128,1024]{1,0:T(8,128)(2,1)S(1)}, bf16[128,1024]{1,0:T(8,128)(2,1)S(1)}, u32[]{:S(2)}, u32[]{:S(2)}) %collective-permute-start.114) | collective-permute-done | bytes 262176 | tf_op jit(solution)/shard_map/ppermute | solution.py:346
  513.6 2.9 collective-permute-done.121
  (796 shorter events, 261.6 us)
Async XLA Ops:
  10.1 16.9 %collective-permute-start.4 = (bf16[32,4864]{1,0:T(8,128)(2,1)}, bf16[32,4864]{1,0:T(8,128)(2,1)S(1)}, u32[]{:S(2)}, u32[]{:S(2)}) collective-permute-start(bf16[32,4864]{1,0:T(8,128)(2,1)} %get-tuple-element.250), channel_id=1, source_target_pairs={{0,3},{1,2},{2,1},{3,0},{4,7},{5,6},{6,5},{7,4},{8,11},{9,10},{10,... | collective-permute-start | bytes 933896 | tf_op jit(solution)/shard_map/ppermute | solution.py:346
  11.4 15.6 %collective-permute-start.3 = (bf16[32,4864]{1,0:T(8,128)(2,1)}, bf16[32,4864]{1,0:T(8,128)(2,1)S(1)}, u32[]{:S(2)}, u32[]{:S(2)}) collective-permute-start(bf16[32,4864]{1,0:T(8,128)(2,1)} %get-tuple-element.248), channel_id=1, source_target_pairs={{0,2},{1,3},{2,0},{3,1},{4,6},{5,7},{6,4},{7,5},{8,10},{9,11},{10,... | collective-permute-start | bytes 933896 | tf_op jit(solution)/shard_map/ppermute | solution.py:346
  16.4 14.3 %collective-permute-start.12 = (bf16[32,4864]{1,0:T(8,128)(2,1)}, bf16[32,4864]{1,0:T(8,128)(2,1)S(1)}, u32[]{:S(2)}, u32[]{:S(2)}) collective-permute-start(bf16[32,4864]{1,0:T(8,128)(2,1)} %get-tuple-element.260), channel_id=1, source_target_pairs={{0,1},{1,0},{2,3},{3,2},{4,5},{5,4},{6,7},{7,6},{8,9},{9,8},{10,11... | collective-permute-start | bytes 933896 | tf_op jit(solution)/shard_map/ppermute | solution.py:346
  41.4 19.9 %collective-permute-start.11 = (bf16[288,768]{1,0:T(8,128)(2,1)S(1)}, bf16[288,768]{1,0:T(8,128)(2,1)S(1)}, u32[]{:S(2)}, u32[]{:S(2)}) collective-permute-start(bf16[288,768]{1,0:T(8,128)(2,1)S(1)} %collective-permute-done.10.refs_1_), channel_id=1, source_target_pairs={{0,4},{1,5},{2,6},{3,7},{4,0},{5,1},{6,2},{7,3},{8,12},{9,13},{10,... | collective-permute-start | bytes 1327112 | tf_op jit(solution)/shard_map/ppermute | solution.py:346
  61.3 20.5 %collective-permute-start.18 = (bf16[256,1024]{1,0:T(8,128)(2,1)S(1)}, bf16[256,1024]{1,0:T(8,128)(2,1)S(1)}, u32[]{:S(2)}, u32[]{:S(2)}) collective-permute-start(bf16[256,1024]{1,0:T(8,128)(2,1)S(1)} %constant_dynamic-update-slice_fusion.refs_0_), channel_id=1, source_target_pairs={{0,4},{1,5},{2,6},{3,7},{4,0},{5,1},{6,2},{7,3},{8,12},{9,13},{10,... | collective-permute-start | bytes 1572872 | tf_op jit(solution)/shard_map/ppermute | solution.py:346
  62.9 18.9 %collective-permute-start.17 = (bf16[256,1024]{1,0:T(8,128)(2,1)S(1)}, bf16[256,1024]{1,0:T(8,128)(2,1)S(1)}, u32[]{:S(2)}, u32[]{:S(2)}) collective-permute-start(bf16[256,1024]{1,0:T(8,128)(2,1)S(1)} %constant_dynamic-update-slice_fusion.refs_0_), channel_id=1, source_target_pairs={{0,8},{1,9},{2,10},{3,11},{4,12},{5,13},{6,14},{7,15},{8,0},{9,1},... | collective-permute-start | bytes 1572872 | tf_op jit(solution)/shard_map/ppermute | solution.py:346
  83.6 20.0 %collective-permute-start.22 = (bf16[256,1024]{1,0:T(8,128)(2,1)S(1)}, bf16[256,1024]{1,0:T(8,128)(2,1)S(1)}, u32[]{:S(2)}, u32[]{:S(2)}) collective-permute-start(bf16[256,1024]{1,0:T(8,128)(2,1)S(1)} %collective-permute-done.17.refs_1_), channel_id=1, source_target_pairs={{0,4},{1,5},{2,6},{3,7},{4,0},{5,1},{6,2},{7,3},{8,12},{9,13},{10,... | collective-permute-start | bytes 1572872 | tf_op jit(solution)/shard_map/ppermute | solution.py:346
  84.6 19.0 %collective-permute-start.19 = (bf16[192,1024]{1,0:T(8,128)(2,1)S(1)}, bf16[192,1024]{1,0:T(8,128)(2,1)S(1)}, u32[]{:S(2)}, u32[]{:S(2)}) collective-permute-start(bf16[192,1024]{1,0:T(8,128)(2,1)S(1)} %slice.2353), channel_id=1, source_target_pairs={{0,1},{1,0},{2,3},{3,2},{4,5},{5,4},{6,7},{7,6},{8,9},{9,8},{10,11... | collective-permute-start | bytes 1179656 | tf_op jit(solution)/shard_map/ppermute | solution.py:346
  85.4 18.2 %collective-permute-start.21 = (bf16[192,1024]{1,0:T(8,128)(2,1)S(1)}, bf16[192,1024]{1,0:T(8,128)(2,1)S(1)}, u32[]{:S(2)}, u32[]{:S(2)}) collective-permute-start(bf16[192,1024]{1,0:T(8,128)(2,1)S(1)} %fusion.86), channel_id=1, source_target_pairs={{0,2},{1,3},{2,0},{3,1},{4,6},{5,7},{6,4},{7,5},{8,10},{9,11},{10,... | collective-permute-start | bytes 1179656 | tf_op jit(solution)/shard_map/ppermute | solution.py:346
  86.7 16.8 %collective-permute-start.24 = (bf16[128,1024]{1,0:T(8,128)(2,1)S(1)}, bf16[128,1024]{1,0:T(8,128)(2,1)S(1)}, u32[]{:S(2)}, u32[]{:S(2)}) collective-permute-start(bf16[128,1024]{1,0:T(8,128)(2,1)S(1)} %copy-done.75), channel_id=1, source_target_pairs={{0,4},{1,5},{2,6},{3,7},{4,0},{5,1},{6,2},{7,3},{8,12},{9,13},{10,... | collective-permute-start | bytes 786440 | tf_op jit(solution)/shard_map/ppermute | solution.py:346
  87.8 15.7 %collective-permute-start.23 = (bf16[128,1024]{1,0:T(8,128)(2,1)S(1)}, bf16[128,1024]{1,0:T(8,128)(2,1)S(1)}, u32[]{:S(2)}, u32[]{:S(2)}) collective-permute-start(bf16[128,1024]{1,0:T(8,128)(2,1)S(1)} %get-tuple-element.280), channel_id=1, source_target_pairs={{0,16},{1,17},{2,18},{3,19},{4,20},{5,21},{6,22},{7,23},{8,24},{9,... | collective-permute-start | bytes 786440 | tf_op jit(solution)/shard_map/ppermute | solution.py:346
  108.7 17.1 %collective-permute-start.25 = (bf16[192,1024]{1,0:T(8,128)(2,1)S(1)}, bf16[192,1024]{1,0:T(8,128)(2,1)}, u32[]{:S(2)}, u32[]{:S(2)}) collective-permute-start(bf16[192,1024]{1,0:T(8,128)(2,1)S(1)} %fusion.112), channel_id=1, source_target_pairs={{0,1},{1,0},{2,3},{3,2},{4,5},{5,4},{6,7},{7,6},{8,9},{9,8},{10,11... | collective-permute-start | bytes 1179656 | tf_op jit(solution)/shard_map/ppermute | solution.py:346
  118.5 14.8 %collective-permute-start.31 = (bf16[128,768]{1,0:T(8,128)(2,1)S(1)}, bf16[128,768]{1,0:T(8,128)(2,1)S(1)}, u32[]{:S(2)}, u32[]{:S(2)}) collective-permute-start(bf16[128,768]{1,0:T(8,128)(2,1)S(1)} %copy-done.76), channel_id=1, source_target_pairs={{0,16},{1,17},{2,18},{3,19},{4,20},{5,21},{6,22},{7,23},{8,24},{9,... | collective-permute-start | bytes 589832 | tf_op jit(solution)/shard_map/ppermute | solution.py:346
  121.6 13.8 %collective-permute-start.30 = (bf16[256,1024]{1,0:T(8,128)(2,1)S(1)}, bf16[256,1024]{1,0:T(8,128)(2,1)S(1)}, u32[]{:S(2)}, u32[]{:S(2)}) collective-permute-start(bf16[256,1024]{1,0:T(8,128)(2,1)S(1)} %collective-permute-done.27.refs_1_), channel_id=1, source_target_pairs={{0,4},{1,5},{2,6},{3,7},{4,0},{5,1},{6,2},{7,3},{8,12},{9,13},{10,... | collective-permute-start | bytes 1572872 | tf_op jit(solution)/shard_map/ppermute | solution.py:346
  141.0 16.3 %collective-permute-start.37 = (bf16[256,768]{1,0:T(8,128)(2,1)S(1)}, bf16[256,768]{1,0:T(8,128)(2,1)S(1)}, u32[]{:S(2)}, u32[]{:S(2)}) collective-permute-start(bf16[256,768]{1,0:T(8,128)(2,1)S(1)} %constant_dynamic-update-slice_fusion.2.refs_0_), channel_id=1, source_target_pairs={{0,4},{1,5},{2,6},{3,7},{4,0},{5,1},{6,2},{7,3},{8,12},{9,13},{10,... | collective-permute-start | bytes 1179656 | tf_op jit(solution)/shard_map/ppermute | solution.py:346
  142.6 16.8 %collective-permute-start.36 = (bf16[256,768]{1,0:T(8,128)(2,1)S(1)}, bf16[256,768]{1,0:T(8,128)(2,1)S(1)}, u32[]{:S(2)}, u32[]{:S(2)}) collective-permute-start(bf16[256,768]{1,0:T(8,128)(2,1)S(1)} %constant_dynamic-update-slice_fusion.2.refs_0_), channel_id=1, source_target_pairs={{0,8},{1,9},{2,10},{3,11},{4,12},{5,13},{6,14},{7,15},{8,0},{9,1},... | collective-permute-start | bytes 1179656 | tf_op jit(solution)/shard_map/ppermute | solution.py:346
  144.0 15.5 %collective-permute-start.33 = (bf16[192,1024]{1,0:T(8,128)(2,1)S(1)}, bf16[192,1024]{1,0:T(8,128)(2,1)S(1)}, u32[]{:S(2)}, u32[]{:S(2)}) collective-permute-start(bf16[192,1024]{1,0:T(8,128)(2,1)S(1)} %slice.2351), channel_id=1, source_target_pairs={{0,1},{1,0},{2,3},{3,2},{4,5},{5,4},{6,7},{7,6},{8,9},{9,8},{10,11... | collective-permute-start | bytes 1179656 | tf_op jit(solution)/shard_map/ppermute | solution.py:346
  144.2 15.3 %collective-permute-start.35 = (bf16[192,1024]{1,0:T(8,128)(2,1)S(1)}, bf16[192,1024]{1,0:T(8,128)(2,1)S(1)}, u32[]{:S(2)}, u32[]{:S(2)}) collective-permute-start(bf16[192,1024]{1,0:T(8,128)(2,1)S(1)} %fusion.84), channel_id=1, source_target_pairs={{0,2},{1,3},{2,0},{3,1},{4,6},{5,7},{6,4},{7,5},{8,10},{9,11},{10,... | collective-permute-start | bytes 1179656 | tf_op jit(solution)/shard_map/ppermute | solution.py:346
  160.4 15.3 %collective-permute-start.40 = (bf16[192,1024]{1,0:T(8,128)(2,1)S(1)}, bf16[192,1024]{1,0:T(8,128)(2,1)S(1)}, u32[]{:S(2)}, u32[]{:S(2)}) collective-permute-start(bf16[192,1024]{1,0:T(8,128)(2,1)S(1)} %fusion.113), channel_id=1, source_target_pairs={{0,2},{1,3},{2,0},{3,1},{4,6},{5,7},{6,4},{7,5},{8,10},{9,11},{10,... | collective-permute-start | bytes 1179656 | tf_op jit(solution)/shard_map/ppermute | solution.py:346
  161.6 14.1 %collective-permute-start.41 = (bf16[256,768]{1,0:T(8,128)(2,1)S(1)}, bf16[256,768]{1,0:T(8,128)(2,1)S(1)}, u32[]{:S(2)}, u32[]{:S(2)}) collective-permute-start(bf16[256,768]{1,0:T(8,128)(2,1)S(1)} %collective-permute-done.36.refs_1_), channel_id=1, source_target_pairs={{0,4},{1,5},{2,6},{3,7},{4,0},{5,1},{6,2},{7,3},{8,12},{9,13},{10,... | collective-permute-start | bytes 1179656 | tf_op jit(solution)/shard_map/ppermute | solution.py:346
  163.9 16.2 %collective-permute-start.39 = (bf16[192,1024]{1,0:T(8,128)(2,1)S(1)}, bf16[192,1024]{1,0:T(8,128)(2,1)S(1)}, u32[]{:S(2)}, u32[]{:S(2)}) collective-permute-start(bf16[192,1024]{1,0:T(8,128)(2,1)S(1)} %fusion.113), channel_id=1, source_target_pairs={{0,1},{1,0},{2,3},{3,2},{4,5},{5,4},{6,7},{7,6},{8,9},{9,8},{10,11... | collective-permute-start | bytes 1179656 | tf_op jit(solution)/shard_map/ppermute | solution.py:346
  175.9 14.9 %collective-permute-start.45 = (bf16[256,1024]{1,0:T(8,128)(2,1)S(1)}, bf16[256,1024]{1,0:T(8,128)(2,1)S(1)}, u32[]{:S(2)}, u32[]{:S(2)}) collective-permute-start(bf16[256,1024]{1,0:T(8,128)(2,1)S(1)} %constant_dynamic-update-slice_fusion.4.refs_0_), channel_id=1, source_target_pairs={{0,4},{1,5},{2,6},{3,7},{4,0},{5,1},{6,2},{7,3},{8,12},{9,13},{10,... | collective-permute-start | bytes 1572872 | tf_op jit(solution)/shard_map/ppermute | solution.py:346
  177.5 14.0 %collective-permute-start.44 = (bf16[256,1024]{1,0:T(8,128)(2,1)S(1)}, bf16[256,1024]{1,0:T(8,128)(2,1)S(1)}, u32[]{:S(2)}, u32[]{:S(2)}) collective-permute-start(bf16[256,1024]{1,0:T(8,128)(2,1)S(1)} %constant_dynamic-update-slice_fusion.4.refs_0_), channel_id=1, source_target_pairs={{0,8},{1,9},{2,10},{3,11},{4,12},{5,13},{6,14},{7,15},{8,0},{9,1},... | collective-permute-start | bytes 1572872 | tf_op jit(solution)/shard_map/ppermute | solution.py:346
  193.2 18.5 %collective-permute-start.49 = (bf16[256,1024]{1,0:T(8,128)(2,1)S(1)}, bf16[256,1024]{1,0:T(8,128)(2,1)S(1)}, u32[]{:S(2)}, u32[]{:S(2)}) collective-permute-start(bf16[256,1024]{1,0:T(8,128)(2,1)S(1)} %collective-permute-done.44.refs_1_), channel_id=1, source_target_pairs={{0,4},{1,5},{2,6},{3,7},{4,0},{5,1},{6,2},{7,3},{8,12},{9,13},{10,... | collective-permute-start | bytes 1572872 | tf_op jit(solution)/shard_map/ppermute | solution.py:346
  195.0 16.7 %collective-permute-start.48 = (bf16[192,1024]{1,0:T(8,128)(2,1)S(1)}, bf16[192,1024]{1,0:T(8,128)(2,1)S(1)}, u32[]{:S(2)}, u32[]{:S(2)}) collective-permute-start(bf16[192,1024]{1,0:T(8,128)(2,1)S(1)} %fusion.82), channel_id=1, source_target_pairs={{0,2},{1,3},{2,0},{3,1},{4,6},{5,7},{6,4},{7,5},{8,10},{9,11},{10,... | collective-permute-start | bytes 1179656 | tf_op jit(solution)/shard_map/ppermute | solution.py:346
  196.4 15.4 %collective-permute-start.46 = (bf16[192,1024]{1,0:T(8,128)(2,1)S(1)}, bf16[192,1024]{1,0:T(8,128)(2,1)S(1)}, u32[]{:S(2)}, u32[]{:S(2)}) collective-permute-start(bf16[192,1024]{1,0:T(8,128)(2,1)S(1)} %slice.2349), channel_id=1, source_target_pairs={{0,1},{1,0},{2,3},{3,2},{4,5},{5,4},{6,7},{7,6},{8,9},{9,8},{10,11... | collective-permute-start | bytes 1179656 | tf_op jit(solution)/shard_map/ppermute | solution.py:346
  196.4 15.2 %collective-permute-start.50 = (bf16[128,1024]{1,0:T(8,128)(2,1)S(1)}, bf16[128,1024]{1,0:T(8,128)(2,1)S(1)}, u32[]{:S(2)}, u32[]{:S(2)}) collective-permute-start(bf16[128,1024]{1,0:T(8,128)(2,1)S(1)} %get-tuple-element.322), channel_id=1, source_target_pairs={{0,16},{1,17},{2,18},{3,19},{4,20},{5,21},{6,22},{7,23},{8,24},{9,... | collective-permute-start | bytes 786440 | tf_op jit(solution)/shard_map/ppermute | solution.py:346
  214.7 15.9 %collective-permute-start.51 = (bf16[192,1024]{1,0:T(8,128)(2,1)S(1)}, bf16[192,1024]{1,0:T(8,128)(2,1)}, u32[]{:S(2)}, u32[]{:S(2)}) collective-permute-start(bf16[192,1024]{1,0:T(8,128)(2,1)S(1)} %fusion.114), channel_id=1, source_target_pairs={{0,1},{1,0},{2,3},{3,2},{4,5},{5,4},{6,7},{7,6},{8,9},{9,8},{10,11... | collective-permute-start | bytes 1179656 | tf_op jit(solution)/shard_map/ppermute | solution.py:346
  226.2 14.3 %collective-permute-start.56 = (bf16[256,1024]{1,0:T(8,128)(2,1)S(1)}, bf16[256,1024]{1,0:T(8,128)(2,1)S(1)}, u32[]{:S(2)}, u32[]{:S(2)}) collective-permute-start(bf16[256,1024]{1,0:T(8,128)(2,1)S(1)} %collective-permute-done.53.refs_1_), channel_id=1, source_target_pairs={{0,4},{1,5},{2,6},{3,7},{4,0},{5,1},{6,2},{7,3},{8,12},{9,13},{10,... | collective-permute-start | bytes 1572872 | tf_op jit(solution)/shard_map/ppermute | solution.py:346
  281.3 24.6 %collective-permute-start.61 = (bf16[192,1024]{1,0:T(8,128)(2,1)S(1)}, bf16[192,1024]{1,0:T(8,128)(2,1)S(1)}, u32[]{:S(2)}, u32[]{:S(2)}) collective-permute-start(bf16[192,1024]{1,0:T(8,128)(2,1)S(1)} %slice.2345), channel_id=1, source_target_pairs={{0,1},{1,0},{2,3},{3,2},{4,5},{5,4},{6,7},{7,6},{8,9},{9,8},{10,11... | collective-permute-start | bytes 1179656 | tf_op jit(solution)/shard_map/ppermute | solution.py:346
  290.9 14.1 %collective-permute-start.66 = (bf16[2,128,1024]{2,1,0:T(8,128)(2,1)S(1)}, bf16[2,128,1024]{2,1,0:T(8,128)(2,1)S(1)}, u32[]{:S(2)}, u32[]{:S(2)}) collective-permute-start(bf16[2,128,1024]{2,1,0:T(8,128)(2,1)S(1)} %select_bitcast_fusion.19), channel_id=1, source_target_pairs={{0,4},{1,5},{2,6},{3,7},{4,0},{5,1},{6,2},{7,3},{8,12},{9,13},{10,... | collective-permute-start | bytes 1572872 | tf_op jit(solution)/shard_map/ppermute | solution.py:346
  321.9 17.5 %collective-permute-start.72 = (bf16[128,1024]{1,0:T(8,128)(2,1)}, bf16[128,1024]{1,0:T(8,128)(2,1)}, u32[]{:S(2)}, u32[]{:S(2)}) collective-permute-start(bf16[128,1024]{1,0:T(8,128)(2,1)} %select_bitcast_fusion.37), channel_id=1, source_target_pairs={{0,16},{1,17},{2,18},{3,19},{4,20},{5,21},{6,22},{7,23},{8,24},{9,... | collective-permute-start | bytes 786440 | tf_op jit(solution)/shard_map/ppermute | solution.py:346
  323.6 15.8 %collective-permute-start.73 = (bf16[2,128,1024]{2,1,0:T(8,128)(2,1)}, bf16[2,128,1024]{2,1,0:T(8,128)(2,1)S(1)}, u32[]{:S(2)}, u32[]{:S(2)}) collective-permute-start(bf16[2,128,1024]{2,1,0:T(8,128)(2,1)} %select_bitcast_fusion.17), channel_id=1, source_target_pairs={{0,4},{1,5},{2,6},{3,7},{4,0},{5,1},{6,2},{7,3},{8,12},{9,13},{10,... | collective-permute-start | bytes 1572872 | tf_op jit(solution)/shard_map/ppermute | solution.py:346
  346.0 13.8 %collective-permute-start.77 = (bf16[192,1024]{1,0:T(8,128)(2,1)S(1)}, bf16[192,1024]{1,0:T(8,128)(2,1)S(1)}, u32[]{:S(2)}, u32[]{:S(2)}) collective-permute-start(bf16[192,1024]{1,0:T(8,128)(2,1)S(1)} %slice.2343), channel_id=1, source_target_pairs={{0,1},{1,0},{2,3},{3,2},{4,5},{5,4},{6,7},{7,6},{8,9},{9,8},{10,11... | collective-permute-start | bytes 1179656 | tf_op jit(solution)/shard_map/ppermute | solution.py:346
  361.8 16.9 %collective-permute-start.84 = (bf16[192,1024]{1,0:T(8,128)(2,1)S(1)}, bf16[192,1024]{1,0:T(8,128)(2,1)S(1)}, u32[]{:S(2)}, u32[]{:S(2)}) collective-permute-start(bf16[192,1024]{1,0:T(8,128)(2,1)S(1)} %get-tuple-element.492), channel_id=1, source_target_pairs={{0,2},{1,3},{2,0},{3,1},{4,6},{5,7},{6,4},{7,5},{8,10},{9,11},{10,... | collective-permute-start | bytes 1179656 | tf_op jit(solution)/shard_map/ppermute | solution.py:346
  363.4 15.3 %collective-permute-start.85 = (bf16[128,1024]{1,0:T(8,128)(2,1)S(1)}, bf16[128,1024]{1,0:T(8,128)(2,1)S(1)}, u32[]{:S(2)}, u32[]{:S(2)}) collective-permute-start(bf16[128,1024]{1,0:T(8,128)(2,1)S(1)} %select_bitcast_fusion.36), channel_id=1, source_target_pairs={{0,16},{1,17},{2,18},{3,19},{4,20},{5,21},{6,22},{7,23},{8,24},{9,... | collective-permute-start | bytes 786440 | tf_op jit(solution)/shard_map/ppermute | solution.py:346
  364.0 14.7 %collective-permute-start.86 = (bf16[2,128,1024]{2,1,0:T(8,128)(2,1)S(1)}, bf16[2,128,1024]{2,1,0:T(8,128)(2,1)S(1)}, u32[]{:S(2)}, u32[]{:S(2)}) collective-permute-start(bf16[2,128,1024]{2,1,0:T(8,128)(2,1)S(1)} %pad_maximum_fusion.13), channel_id=1, source_target_pairs={{0,4},{1,5},{2,6},{3,7},{4,0},{5,1},{6,2},{7,3},{8,12},{9,13},{10,... | collective-permute-start | bytes 1572872 | tf_op jit(solution)/shard_map/ppermute | solution.py:346
  367.8 43.9 %collective-permute-start.83 = (bf16[192,1024]{1,0:T(8,128)(2,1)S(1)}, bf16[192,1024]{1,0:T(8,128)(2,1)S(1)}, u32[]{:S(2)}, u32[]{:S(2)}) collective-permute-start(bf16[192,1024]{1,0:T(8,128)(2,1)S(1)} %slice.2341), channel_id=1, source_target_pairs={{0,1},{1,0},{2,3},{3,2},{4,5},{5,4},{6,7},{7,6},{8,9},{9,8},{10,11... | collective-permute-start | bytes 1179656 | tf_op jit(solution)/shard_map/ppermute | solution.py:346
  379.0 14.3 %collective-permute-start.89 = (bf16[2,128,1024]{2,1,0:T(8,128)(2,1)S(1)}, bf16[2,128,1024]{2,1,0:T(8,128)(2,1)S(1)}, u32[]{:S(2)}, u32[]{:S(2)}) collective-permute-start(bf16[2,128,1024]{2,1,0:T(8,128)(2,1)S(1)} %pad_maximum_fusion.14), channel_id=1, source_target_pairs={{0,4},{1,5},{2,6},{3,7},{4,0},{5,1},{6,2},{7,3},{8,12},{9,13},{10,... | collective-permute-start | bytes 1572872 | tf_op jit(solution)/shard_map/ppermute | solution.py:346
  380.1 14.0 %collective-permute-start.88 = (bf16[2,128,1024]{2,1,0:T(8,128)(2,1)S(1)}, bf16[2,128,1024]{2,1,0:T(8,128)(2,1)S(1)}, u32[]{:S(2)}, u32[]{:S(2)}) collective-permute-start(bf16[2,128,1024]{2,1,0:T(8,128)(2,1)S(1)} %add_convert_fusion.5), channel_id=1, source_target_pairs={{0,8},{1,9},{2,10},{3,11},{4,12},{5,13},{6,14},{7,15},{8,0},{9,1},... | collective-permute-start | bytes 1572872 | tf_op jit(solution)/shard_map/ppermute | solution.py:346
  395.6 15.3 %collective-permute-start.92 = (bf16[128,1024]{1,0:T(8,128)(2,1)S(1)}, bf16[128,1024]{1,0:T(8,128)(2,1)S(1)}, u32[]{:S(2)}, u32[]{:S(2)}) collective-permute-start(bf16[128,1024]{1,0:T(8,128)(2,1)S(1)} %select_bitcast_fusion.33), channel_id=1, source_target_pairs={{0,16},{1,17},{2,18},{3,19},{4,20},{5,21},{6,22},{7,23},{8,24},{9,... | collective-permute-start | bytes 786440 | tf_op jit(solution)/shard_map/ppermute | solution.py:346
  397.4 14.0 %collective-permute-start.93 = (bf16[2,128,1024]{2,1,0:T(8,128)(2,1)S(1)}, bf16[2,128,1024]{2,1,0:T(8,128)(2,1)S(1)}, u32[]{:S(2)}, u32[]{:S(2)}) collective-permute-start(bf16[2,128,1024]{2,1,0:T(8,128)(2,1)S(1)} %select_bitcast_fusion.15), channel_id=1, source_target_pairs={{0,4},{1,5},{2,6},{3,7},{4,0},{5,1},{6,2},{7,3},{8,12},{9,13},{10,... | collective-permute-start | bytes 1572872 | tf_op jit(solution)/shard_map/ppermute | solution.py:346
  427.9 17.3 %collective-permute-start.99 = (bf16[128,1024]{1,0:T(8,128)(2,1)}, bf16[128,1024]{1,0:T(8,128)(2,1)}, u32[]{:S(2)}, u32[]{:S(2)}) collective-permute-start(bf16[128,1024]{1,0:T(8,128)(2,1)} %select_bitcast_fusion.32), channel_id=1, source_target_pairs={{0,16},{1,17},{2,18},{3,19},{4,20},{5,21},{6,22},{7,23},{8,24},{9,... | collective-permute-start | bytes 786440 | tf_op jit(solution)/shard_map/ppermute | solution.py:346
  429.1 16.1 %collective-permute-start.100 = (bf16[2,128,1024]{2,1,0:T(8,128)(2,1)}, bf16[2,128,1024]{2,1,0:T(8,128)(2,1)S(1)}, u32[]{:S(2)}, u32[]{:S(2)}) collective-permute-start(bf16[2,128,1024]{2,1,0:T(8,128)(2,1)} %select_bitcast_fusion.13), channel_id=1, source_target_pairs={{0,4},{1,5},{2,6},{3,7},{4,0},{5,1},{6,2},{7,3},{8,12},{9,13},{10,... | collective-permute-start | bytes 1572872 | tf_op jit(solution)/shard_map/ppermute | solution.py:346
  457.2 14.7 %collective-permute-start.105 = (bf16[2,128,1024]{2,1,0:T(8,128)(2,1)}, bf16[2,128,1024]{2,1,0:T(8,128)(2,1)}, u32[]{:S(2)}, u32[]{:S(2)}) collective-permute-start(bf16[2,128,1024]{2,1,0:T(8,128)(2,1)} %pad_maximum_fusion.16), channel_id=1, source_target_pairs={{0,4},{1,5},{2,6},{3,7},{4,0},{5,1},{6,2},{7,3},{8,12},{9,13},{10,... | collective-permute-start | bytes 1572872 | tf_op jit(solution)/shard_map/ppermute | solution.py:346
  458.1 15.3 %collective-permute-start.106 = (bf16[2,128,1024]{2,1,0:T(8,128)(2,1)}, bf16[2,128,1024]{2,1,0:T(8,128)(2,1)}, u32[]{:S(2)}, u32[]{:S(2)}) collective-permute-start(bf16[2,128,1024]{2,1,0:T(8,128)(2,1)} %fusion.61), channel_id=1, source_target_pairs={{0,8},{1,9},{2,10},{3,11},{4,12},{5,13},{6,14},{7,15},{8,0},{9,1},... | collective-permute-start | bytes 1572872 | tf_op jit(solution)/shard_map/ppermute | solution.py:346
  459.9 18.9 %collective-permute-start.107 = (bf16[192,1024]{1,0:T(8,128)(2,1)}, bf16[192,1024]{1,0:T(8,128)(2,1)}, u32[]{:S(2)}, u32[]{:S(2)}) collective-permute-start(bf16[192,1024]{1,0:T(8,128)(2,1)} %slice.2338), channel_id=1, source_target_pairs={{0,1},{1,0},{2,3},{3,2},{4,5},{5,4},{6,7},{7,6},{8,9},{9,8},{10,11... | collective-permute-start | bytes 1179656 | tf_op jit(solution)/shard_map/ppermute | solution.py:346
  507.3 14.1 %collective-permute-start.122 = (bf16[128,1024]{1,0:T(8,128)(2,1)S(1)}, bf16[128,1024]{1,0:T(8,128)(2,1)S(1)}, u32[]{:S(2)}, u32[]{:S(2)}) collective-permute-start(bf16[128,1024]{1,0:T(8,128)(2,1)S(1)} %select_bitcast_fusion.28), channel_id=1, source_target_pairs={{0,16},{1,17},{2,18},{3,19},{4,20},{5,21},{6,22},{7,23},{8,24},{9,... | collective-permute-start | bytes 786440 | tf_op jit(solution)/shard_map/ppermute | solution.py:346
  (201 other events, 1323.6 us)

commit v5 on v4

--- a/solution.py
+++ b/solution.py
@@ -615,7 +615,7 @@
                     return outs[0].step(4) + expand_0.middle()
                 if (layer, point) == (0, "out"):
                     out_all.append(outs[0].take())
-                    return expand_0.last() + shrink_0.far() + outs[1].step(1)
+                    return shrink_0.far() + expand_0.last() + outs[1].step(1)
                 if (layer, point) == (0, "normed"):
                     return shrink_0.middle() + expand_0.ready((block_rows,))
                 if (layer, point) == (0, "active"):
@@ -625,13 +625,13 @@
                     shrink_all.append(shrink_0.closed())
                     return qkv_1.middle() + outs[1].step(4)
                 if (layer, point) == (1, "group"):
-                    return qkv_1.last() + expand_1.far()
+                    return expand_1.far() + qkv_1.last()
                 if (layer, point) == (1, "attend"):
                     qkv_all.append(qkv_1.whole((block_rows,))[0])
                     return expand_1.middle()
                 if (layer, point) == (1, "out"):
                     out_all.append(outs[1].take())
-                    return expand_1.last() + shrink_1.far()
+                    return shrink_1.far() + expand_1.last()
                 if (layer, point) == (1, "normed"):
                     return shrink_1.middle() + expand_1.ready((block_rows,))
                 if (layer, point) == (1, "active"):
@@ -947,7 +947,9 @@
             gate, moves, marks = grad_qkv, [], []
             if special and layer == 0:
                 late_grads(grad_qkv)
-                tail_moving = launch(mine.qkv.first() + mine.expand.middle_z(), grad_qkv)
+                tail_moves = mine.qkv.first() + mine.expand.middle_z()
+                tail_moving = launch(tail_moves, grad_qkv)
+                grad_qkv = after(grad_qkv, tail_moves[0][2])
             elif special:
                 moves = mine.expand.middle()
             left = (grad_qkv[:chip_rows], grad_qkv[chip_rows:])

time: 540 us -> 538 us (level)
    unnamed x318 -> x306, local copies, waits for them, and re-layouts: 12.7 us -> 11.3 us
  transfers between devices with their start and end apart: 126 -> 126, of which waited for: 55 -> 56; matrix products, arithmetic and copies ran while one was open for 21% -> 21% of each run, Pallas kernels for 11% -> 11%
where the time goes in v5:
time: 538 us; the launch traced here: 528 us
  waiting for transfers between devices  198 us (37%)
  starting transfers between devices  107 us (20%)
  matrix products  72.4 us (13%)
  Pallas kernels  62.7 us (12%)
  other arithmetic  59 us (11%)
  local copies, waits for them, and re-layouts  23.3 us (4%)
    ppermute x126, waiting for transfers between devices, swap(): return lax.ppermute(array, AXES, [(p, p ^ bit) for p in range(n_dev)])  198 us
    ppermute x126, starting transfers between devices, swap(): return lax.ppermute(array, AXES, [(p, p ^ bit) for p in range(n_dev)])  107 us
    dot_general x37, matrix products, dot(): lax.dot_general(left, right, (((left_dim,), (right_dim,)), ((), ())), pre...  70.9 us
    pallas_call x2, Pallas kernels, attend_back(): pl.pallas_call(functools.partial(attend_back_kernel, math.gcd(tokens, 768...  20.2 us
    pallas_call x6, Pallas kernels, place(): pl.pallas_call(body, out_shape=tuple(shapes), in_specs=[whole] * len(piec...  17.2 us
    pallas_call x2, Pallas kernels, attend(): pl.pallas_call(functools.partial(attend_kernel, math.gcd(tokens, 768)), o...  13.1 us
    unnamed x306, local copies, waits for them, and re-layouts  11.3 us
  transfers between devices with their start and end apart: 126, of which 56 were waited for; matrix products, arithmetic and copies ran while one was open for 21% of the time, Pallas kernels for 11%

profile of v5, /device:TPU:0, one launch (start us, length us, event | category | flops | bytes accessed | tf_op | source)
XLA Modules:
  0.0 527.6 jit_solution(3376554700808584647)
XLA Ops:
  13.6 2.8 collective-permute-start.8
  16.4 10.7 %collective-permute-done.8 = bf16[144,768]{1,0:T(8,128)(2,1)S(1)} collective-permute-done((bf16[144,768]{1,0:T(8,128)(2,1)}, bf16[144,768]{1,0:T(8,128)(2,1)S(1)}, u32[]{:S(2)}, u32[]{:S(2)}) %collective-permute-start.8) | collective-permute-done | bytes 221216 | tf_op jit(solution)/shard_map/ppermute | solution.py:346
  44.8 3.1 collective-permute-start.13
  49.1 3.1 collective-permute-done.9.refs_2_
  53.9 4.2 collective-permute-done.13
  58.1 3.2 collective-permute-done.11.refs_3_
  64.6 2.9 shard_map.379
  68.3 3.1 collective-permute-start.16
  71.4 3.9 add_convert_fusion.1.qkv_ref
  75.3 6.6 %shard_map.380 = (bf16[768,256]{1,0:T(8,128)(2,1)}, f32[4,768]{1,0:T(4,128)}, f32[4,768]{1,0:T(4,128)}) custom-call(bf16[768,768]{1,0:T(8,128)(2,1)} %add_convert_fusion.1.qkv_ref, s32[768,1]{1,0:T(8,128)} %broadcast_in_dim.133.col_ref, s32[1,768]{1,0:T(1,128)} %broadcast_in_dim.121.row_ref), custom_call_target="tpu_custom_call" | custom-call | flops 6039797760 | bytes 3145728 | tf_op jit(solution)/shard_map/pallas_call | solution.py:108
  90.5 13.0 %collective-permute-done.24 = bf16[128,1024]{1,0:T(8,128)(2,1)S(1)} collective-permute-done((bf16[128,1024]{1,0:T(8,128)(2,1)S(1)}, bf16[128,1024]{1,0:T(8,128)(2,1)S(1)}, u32[]{:S(2)}, u32[]{:S(2)}) %collective-permute-start.24) | collective-permute-done | bytes 262176 | tf_op jit(solution)/shard_map/ppermute | solution.py:346
  109.6 3.0 shard_map.381
  112.7 4.9 collective-permute-done.26
  123.1 2.8 shard_map.382.buffer
  125.9 3.9 multiply_convert_fusion.3
  129.8 3.5 multiply_convert_fusion.2
  147.1 10.2 %collective-permute-done.38 = bf16[128,1024]{1,0:T(8,128)(2,1)S(1)} collective-permute-done((bf16[128,1024]{1,0:T(8,128)(2,1)S(1)}, bf16[128,1024]{1,0:T(8,128)(2,1)S(1)}, u32[]{:S(2)}, u32[]{:S(2)}) %collective-permute-start.38) | collective-permute-done | bytes 262176 | tf_op jit(solution)/shard_map/ppermute | solution.py:346
  164.0 11.7 %collective-permute-done.41 = bf16[128,1024]{1,0:T(8,128)(2,1)S(1)} collective-permute-done((bf16[128,1024]{1,0:T(8,128)(2,1)S(1)}, bf16[128,1024]{1,0:T(8,128)(2,1)S(1)}, u32[]{:S(2)}, u32[]{:S(2)}) %collective-permute-start.41) | collective-permute-done | bytes 262176 | tf_op jit(solution)/shard_map/ppermute | solution.py:346
  180.1 4.1 add_convert_fusion.qkv_ref
  184.2 6.6 %shard_map.385 = (bf16[768,256]{1,0:T(8,128)(2,1)}, f32[4,768]{1,0:T(4,128)}, f32[4,768]{1,0:T(4,128)}) custom-call(bf16[768,768]{1,0:T(8,128)(2,1)} %add_convert_fusion.qkv_ref, s32[768,1]{1,0:T(8,128)} %broadcast_in_dim.133.col_ref, s32[1,768]{1,0:T(1,128)} %broadcast_in_dim.121.row_ref), custom_call_target="tpu_custom_call" | custom-call | flops 6039797760 | bytes 3145728 | tf_op jit(solution)/shard_map/pallas_call | solution.py:108
  198.9 12.7 %collective-permute-done.49 = bf16[128,1024]{1,0:T(8,128)(2,1)S(1)} collective-permute-done((bf16[128,1024]{1,0:T(8,128)(2,1)S(1)}, bf16[128,1024]{1,0:T(8,128)(2,1)S(1)}, u32[]{:S(2)}, u32[]{:S(2)}) %collective-permute-start.49) | collective-permute-done | bytes 262176 | tf_op jit(solution)/shard_map/ppermute | solution.py:346
  214.7 3.0 shard_map.386
  217.7 6.2 %collective-permute-done.52 = bf16[192,1024]{1,0:T(8,128)(2,1)S(1)} collective-permute-done((bf16[192,1024]{1,0:T(8,128)(2,1)S(1)}, bf16[192,1024]{1,0:T(8,128)(2,1)S(1)}, u32[]{:S(2)}, u32[]{:S(2)}) %collective-permute-start.52) | collective-permute-done | bytes 393248 | tf_op jit(solution)/shard_map/ppermute | solution.py:346
  227.7 2.9 shard_map.387.buffer
  230.6 3.6 multiply_convert_fusion.1
  234.2 3.3 multiply_convert_fusion
  237.4 3.1 collective-permute-done.56.piece
  243.2 2.7 fusion.185
  250.5 10.1 %collective-permute-done.59 = bf16[192,1024]{1,0:T(8,128)(2,1)} collective-permute-done((bf16[192,1024]{1,0:T(8,128)(2,1)}, bf16[192,1024]{1,0:T(8,128)(2,1)}, u32[]{:S(2)}, u32[]{:S(2)}) %collective-permute-start.59) | collective-permute-done | bytes 393248 | tf_op jit(solution)/shard_map/ppermute | solution.py:346
  272.6 3.8 collective-permute-done.62
  276.4 3.8 fusion.5
  281.8 3.1 convolution_convert_fusion.3
  295.6 3.0 convolution_convert_fusion.2
  299.8 5.1 collective-permute-done.66
  312.8 6.9 %collective-permute-done.68 = bf16[192,1024]{1,0:T(8,128)(2,1)S(1)} collective-permute-done((bf16[192,1024]{1,0:T(8,128)(2,1)S(1)}, bf16[192,1024]{1,0:T(8,128)(2,1)S(1)}, u32[]{:S(2)}, u32[]{:S(2)}) %collective-permute-start.68) | collective-permute-done | bytes 393248 | tf_op jit(solution)/shard_map/ppermute | solution.py:346
  329.1 10.2 %shard_map.389 = bf16[768,768]{1,0:T(8,128)(2,1)} custom-call(bf16[768,768]{1,0:T(8,128)(2,1)} %add_convert_fusion.qkv_ref, s32[768,1]{1,0:T(8,128)} %broadcast_in_dim.133.col_ref, s32[1,768]{1,0:T(1,128)} %broadcast_in_dim.121.row_ref, f32[4,768]{1,0:T(4,128)} %get-tuple-element.342.max_ref, f32[4,768]{1,0:T(4,128)} %get-tuple-element.343.sum_ref, ...), custom_call_target="tpu_custom_call" | custom-call | flops 6039797760 | bytes 3145728 | tf_op jit(solution)/shard_map/pallas_call | solution.py:127
  352.6 4.5 collective-permute-done.81
  367.8 10.8 %collective-permute-done.85 = bf16[128,1024]{1,0:T(8,128)(2,1)S(1)} collective-permute-done((bf16[128,1024]{1,0:T(8,128)(2,1)S(1)}, bf16[128,1024]{1,0:T(8,128)(2,1)S(1)}, u32[]{:S(2)}, u32[]{:S(2)}) %collective-permute-start.85) | collective-permute-done | bytes 262176 | tf_op jit(solution)/shard_map/ppermute | solution.py:346
  386.8 6.4 %collective-permute-done.89 = bf16[2,128,1024]{2,1,0:T(8,128)(2,1)S(1)} collective-permute-done((bf16[2,128,1024]{2,1,0:T(8,128)(2,1)S(1)}, bf16[2,128,1024]{2,1,0:T(8,128)(2,1)S(1)}, u32[]{:S(2)}, u32[]{:S(2)}) %collective-permute-start.89) | collective-permute-done | bytes 524320 | tf_op jit(solution)/shard_map/ppermute | solution.py:346
  399.4 3.0 convolution_convert_fusion
  403.9 6.9 %collective-permute-done.92 = bf16[128,1024]{1,0:T(8,128)(2,1)S(1)} collective-permute-done((bf16[128,1024]{1,0:T(8,128)(2,1)S(1)}, bf16[128,1024]{1,0:T(8,128)(2,1)S(1)}, u32[]{:S(2)}, u32[]{:S(2)}) %collective-permute-start.92) | collective-permute-done | bytes 262176 | tf_op jit(solution)/shard_map/ppermute | solution.py:346
  417.2 8.8 %collective-permute-done.95 = bf16[192,1024]{1,0:T(8,128)(2,1)S(1)} collective-permute-done((bf16[192,1024]{1,0:T(8,128)(2,1)S(1)}, bf16[192,1024]{1,0:T(8,128)(2,1)S(1)}, u32[]{:S(2)}, u32[]{:S(2)}) %collective-permute-start.95) | collective-permute-done | bytes 393248 | tf_op jit(solution)/shard_map/ppermute | solution.py:346
  434.5 10.0 %shard_map.390 = bf16[768,768]{1,0:T(8,128)(2,1)} custom-call(bf16[768,768]{1,0:T(8,128)(2,1)} %add_convert_fusion.1.qkv_ref, s32[768,1]{1,0:T(8,128)} %broadcast_in_dim.133.col_ref, s32[1,768]{1,0:T(1,128)} %broadcast_in_dim.121.row_ref, f32[4,768]{1,0:T(4,128)} %get-tuple-element.338.max_ref, f32[4,768]{1,0:T(4,128)} %get-tuple-element.339.sum_ref, ...), custom_call_target="tpu_custom_call" | custom-call | flops 6039797760 | bytes 3145728 | tf_op jit(solution)/shard_map/pallas_call | solution.py:127
  444.5 2.9 convolution_convert_fusion.4
  467.1 2.8 collective-permute-done.111
  479.3 7.6 %collective-permute-done.113 = f32[25,128]{1,0:T(8,128)S(1)} collective-permute-done((f32[25,128]{1,0:T(8,128)S(1)}, f32[25,128]{1,0:T(8,128)S(1)}, u32[]{:S(2)}, u32[]{:S(2)}) %collective-permute-start.113) | collective-permute-done | bytes 12832 | tf_op jit(solution)/shard_map/ppermute | solution.py:346
  493.9 6.2 %collective-permute-done.114 = bf16[128,1024]{1,0:T(8,128)(2,1)S(1)} collective-permute-done((bf16[128,1024]{1,0:T(8,128)(2,1)S(1)}, bf16[128,1024]{1,0:T(8,128)(2,1)S(1)}, u32[]{:S(2)}, u32[]{:S(2)}) %collective-permute-start.114) | collective-permute-done | bytes 262176 | tf_op jit(solution)/shard_map/ppermute | solution.py:346
  511.6 2.9 collective-permute-done.121
  (784 shorter events, 259.2 us)
Async XLA Ops:
  10.1 16.9 %collective-permute-start.4 = (bf16[32,4864]{1,0:T(8,128)(2,1)}, bf16[32,4864]{1,0:T(8,128)(2,1)S(1)}, u32[]{:S(2)}, u32[]{:S(2)}) collective-permute-start(bf16[32,4864]{1,0:T(8,128)(2,1)} %get-tuple-element.251), channel_id=1, source_target_pairs={{0,3},{1,2},{2,1},{3,0},{4,7},{5,6},{6,5},{7,4},{8,11},{9,10},{10,... | collective-permute-start | bytes 933896 | tf_op jit(solution)/shard_map/ppermute | solution.py:346
  11.4 15.6 %collective-permute-start.3 = (bf16[32,4864]{1,0:T(8,128)(2,1)}, bf16[32,4864]{1,0:T(8,128)(2,1)S(1)}, u32[]{:S(2)}, u32[]{:S(2)}) collective-permute-start(bf16[32,4864]{1,0:T(8,128)(2,1)} %get-tuple-element.249), channel_id=1, source_target_pairs={{0,2},{1,3},{2,0},{3,1},{4,6},{5,7},{6,4},{7,5},{8,10},{9,11},{10,... | collective-permute-start | bytes 933896 | tf_op jit(solution)/shard_map/ppermute | solution.py:346
  16.4 14.3 %collective-permute-start.12 = (bf16[32,4864]{1,0:T(8,128)(2,1)}, bf16[32,4864]{1,0:T(8,128)(2,1)S(1)}, u32[]{:S(2)}, u32[]{:S(2)}) collective-permute-start(bf16[32,4864]{1,0:T(8,128)(2,1)} %get-tuple-element.261), channel_id=1, source_target_pairs={{0,1},{1,0},{2,3},{3,2},{4,5},{5,4},{6,7},{7,6},{8,9},{9,8},{10,11... | collective-permute-start | bytes 933896 | tf_op jit(solution)/shard_map/ppermute | solution.py:346
  41.4 19.9 %collective-permute-start.11 = (bf16[288,768]{1,0:T(8,128)(2,1)S(1)}, bf16[288,768]{1,0:T(8,128)(2,1)S(1)}, u32[]{:S(2)}, u32[]{:S(2)}) collective-permute-start(bf16[288,768]{1,0:T(8,128)(2,1)S(1)} %collective-permute-done.10.refs_1_), channel_id=1, source_target_pairs={{0,4},{1,5},{2,6},{3,7},{4,0},{5,1},{6,2},{7,3},{8,12},{9,13},{10,... | collective-permute-start | bytes 1327112 | tf_op jit(solution)/shard_map/ppermute | solution.py:346
  61.3 20.6 %collective-permute-start.18 = (bf16[256,1024]{1,0:T(8,128)(2,1)S(1)}, bf16[256,1024]{1,0:T(8,128)(2,1)S(1)}, u32[]{:S(2)}, u32[]{:S(2)}) collective-permute-start(bf16[256,1024]{1,0:T(8,128)(2,1)S(1)} %constant_dynamic-update-slice_fusion.refs_0_), channel_id=1, source_target_pairs={{0,4},{1,5},{2,6},{3,7},{4,0},{5,1},{6,2},{7,3},{8,12},{9,13},{10,... | collective-permute-start | bytes 1572872 | tf_op jit(solution)/shard_map/ppermute | solution.py:346
  62.9 19.0 %collective-permute-start.17 = (bf16[256,1024]{1,0:T(8,128)(2,1)S(1)}, bf16[256,1024]{1,0:T(8,128)(2,1)S(1)}, u32[]{:S(2)}, u32[]{:S(2)}) collective-permute-start(bf16[256,1024]{1,0:T(8,128)(2,1)S(1)} %constant_dynamic-update-slice_fusion.refs_0_), channel_id=1, source_target_pairs={{0,8},{1,9},{2,10},{3,11},{4,12},{5,13},{6,14},{7,15},{8,0},{9,1},... | collective-permute-start | bytes 1572872 | tf_op jit(solution)/shard_map/ppermute | solution.py:346
  83.6 20.0 %collective-permute-start.23 = (bf16[256,1024]{1,0:T(8,128)(2,1)S(1)}, bf16[256,1024]{1,0:T(8,128)(2,1)S(1)}, u32[]{:S(2)}, u32[]{:S(2)}) collective-permute-start(bf16[256,1024]{1,0:T(8,128)(2,1)S(1)} %collective-permute-done.17.refs_1_), channel_id=1, source_target_pairs={{0,4},{1,5},{2,6},{3,7},{4,0},{5,1},{6,2},{7,3},{8,12},{9,13},{10,... | collective-permute-start | bytes 1572872 | tf_op jit(solution)/shard_map/ppermute | solution.py:346
  84.6 19.0 %collective-permute-start.19 = (bf16[192,1024]{1,0:T(8,128)(2,1)S(1)}, bf16[192,1024]{1,0:T(8,128)(2,1)S(1)}, u32[]{:S(2)}, u32[]{:S(2)}) collective-permute-start(bf16[192,1024]{1,0:T(8,128)(2,1)S(1)} %slice.2353), channel_id=1, source_target_pairs={{0,1},{1,0},{2,3},{3,2},{4,5},{5,4},{6,7},{7,6},{8,9},{9,8},{10,11... | collective-permute-start | bytes 1179656 | tf_op jit(solution)/shard_map/ppermute | solution.py:346
  85.4 18.2 %collective-permute-start.21 = (bf16[192,1024]{1,0:T(8,128)(2,1)S(1)}, bf16[192,1024]{1,0:T(8,128)(2,1)S(1)}, u32[]{:S(2)}, u32[]{:S(2)}) collective-permute-start(bf16[192,1024]{1,0:T(8,128)(2,1)S(1)} %fusion.86), channel_id=1, source_target_pairs={{0,2},{1,3},{2,0},{3,1},{4,6},{5,7},{6,4},{7,5},{8,10},{9,11},{10,... | collective-permute-start | bytes 1179656 | tf_op jit(solution)/shard_map/ppermute | solution.py:346
  86.7 16.9 %collective-permute-start.24 = (bf16[128,1024]{1,0:T(8,128)(2,1)S(1)}, bf16[128,1024]{1,0:T(8,128)(2,1)S(1)}, u32[]{:S(2)}, u32[]{:S(2)}) collective-permute-start(bf16[128,1024]{1,0:T(8,128)(2,1)S(1)} %copy-done.74), channel_id=1, source_target_pairs={{0,4},{1,5},{2,6},{3,7},{4,0},{5,1},{6,2},{7,3},{8,12},{9,13},{10,... | collective-permute-start | bytes 786440 | tf_op jit(solution)/shard_map/ppermute | solution.py:346
  87.8 15.7 %collective-permute-start.22 = (bf16[128,1024]{1,0:T(8,128)(2,1)S(1)}, bf16[128,1024]{1,0:T(8,128)(2,1)S(1)}, u32[]{:S(2)}, u32[]{:S(2)}) collective-permute-start(bf16[128,1024]{1,0:T(8,128)(2,1)S(1)} %get-tuple-element.279), channel_id=1, source_target_pairs={{0,16},{1,17},{2,18},{3,19},{4,20},{5,21},{6,22},{7,23},{8,24},{9,... | collective-permute-start | bytes 786440 | tf_op jit(solution)/shard_map/ppermute | solution.py:346
  108.7 17.2 %collective-permute-start.25 = (bf16[192,1024]{1,0:T(8,128)(2,1)S(1)}, bf16[192,1024]{1,0:T(8,128)(2,1)}, u32[]{:S(2)}, u32[]{:S(2)}) collective-permute-start(bf16[192,1024]{1,0:T(8,128)(2,1)S(1)} %fusion.112), channel_id=1, source_target_pairs={{0,1},{1,0},{2,3},{3,2},{4,5},{5,4},{6,7},{7,6},{8,9},{9,8},{10,11... | collective-permute-start | bytes 1179656 | tf_op jit(solution)/shard_map/ppermute | solution.py:346
  118.5 14.9 %collective-permute-start.31 = (bf16[128,768]{1,0:T(8,128)(2,1)S(1)}, bf16[128,768]{1,0:T(8,128)(2,1)S(1)}, u32[]{:S(2)}, u32[]{:S(2)}) collective-permute-start(bf16[128,768]{1,0:T(8,128)(2,1)S(1)} %copy-done.75), channel_id=1, source_target_pairs={{0,16},{1,17},{2,18},{3,19},{4,20},{5,21},{6,22},{7,23},{8,24},{9,... | collective-permute-start | bytes 589832 | tf_op jit(solution)/shard_map/ppermute | solution.py:346
  121.5 13.8 %collective-permute-start.30 = (bf16[256,1024]{1,0:T(8,128)(2,1)S(1)}, bf16[256,1024]{1,0:T(8,128)(2,1)S(1)}, u32[]{:S(2)}, u32[]{:S(2)}) collective-permute-start(bf16[256,1024]{1,0:T(8,128)(2,1)S(1)} %collective-permute-done.27.refs_1_), channel_id=1, source_target_pairs={{0,4},{1,5},{2,6},{3,7},{4,0},{5,1},{6,2},{7,3},{8,12},{9,13},{10,... | collective-permute-start | bytes 1572872 | tf_op jit(solution)/shard_map/ppermute | solution.py:346
  141.0 16.3 %collective-permute-start.37 = (bf16[256,768]{1,0:T(8,128)(2,1)S(1)}, bf16[256,768]{1,0:T(8,128)(2,1)S(1)}, u32[]{:S(2)}, u32[]{:S(2)}) collective-permute-start(bf16[256,768]{1,0:T(8,128)(2,1)S(1)} %constant_dynamic-update-slice_fusion.2.refs_0_), channel_id=1, source_target_pairs={{0,4},{1,5},{2,6},{3,7},{4,0},{5,1},{6,2},{7,3},{8,12},{9,13},{10,... | collective-permute-start | bytes 1179656 | tf_op jit(solution)/shard_map/ppermute | solution.py:346
  142.5 16.8 %collective-permute-start.36 = (bf16[256,768]{1,0:T(8,128)(2,1)S(1)}, bf16[256,768]{1,0:T(8,128)(2,1)S(1)}, u32[]{:S(2)}, u32[]{:S(2)}) collective-permute-start(bf16[256,768]{1,0:T(8,128)(2,1)S(1)} %constant_dynamic-update-slice_fusion.2.refs_0_), channel_id=1, source_target_pairs={{0,8},{1,9},{2,10},{3,11},{4,12},{5,13},{6,14},{7,15},{8,0},{9,1},... | collective-permute-start | bytes 1179656 | tf_op jit(solution)/shard_map/ppermute | solution.py:346
  144.0 15.5 %collective-permute-start.33 = (bf16[192,1024]{1,0:T(8,128)(2,1)S(1)}, bf16[192,1024]{1,0:T(8,128)(2,1)S(1)}, u32[]{:S(2)}, u32[]{:S(2)}) collective-permute-start(bf16[192,1024]{1,0:T(8,128)(2,1)S(1)} %slice.2351), channel_id=1, source_target_pairs={{0,1},{1,0},{2,3},{3,2},{4,5},{5,4},{6,7},{7,6},{8,9},{9,8},{10,11... | collective-permute-start | bytes 1179656 | tf_op jit(solution)/shard_map/ppermute | solution.py:346
  144.1 15.3 %collective-permute-start.35 = (bf16[192,1024]{1,0:T(8,128)(2,1)S(1)}, bf16[192,1024]{1,0:T(8,128)(2,1)S(1)}, u32[]{:S(2)}, u32[]{:S(2)}) collective-permute-start(bf16[192,1024]{1,0:T(8,128)(2,1)S(1)} %fusion.84), channel_id=1, source_target_pairs={{0,2},{1,3},{2,0},{3,1},{4,6},{5,7},{6,4},{7,5},{8,10},{9,11},{10,... | collective-permute-start | bytes 1179656 | tf_op jit(solution)/shard_map/ppermute | solution.py:346
  160.3 15.4 %collective-permute-start.40 = (bf16[192,1024]{1,0:T(8,128)(2,1)S(1)}, bf16[192,1024]{1,0:T(8,128)(2,1)S(1)}, u32[]{:S(2)}, u32[]{:S(2)}) collective-permute-start(bf16[192,1024]{1,0:T(8,128)(2,1)S(1)} %fusion.113), channel_id=1, source_target_pairs={{0,2},{1,3},{2,0},{3,1},{4,6},{5,7},{6,4},{7,5},{8,10},{9,11},{10,... | collective-permute-start | bytes 1179656 | tf_op jit(solution)/shard_map/ppermute | solution.py:346
  161.6 14.1 %collective-permute-start.42 = (bf16[256,768]{1,0:T(8,128)(2,1)S(1)}, bf16[256,768]{1,0:T(8,128)(2,1)S(1)}, u32[]{:S(2)}, u32[]{:S(2)}) collective-permute-start(bf16[256,768]{1,0:T(8,128)(2,1)S(1)} %collective-permute-done.36.refs_1_), channel_id=1, source_target_pairs={{0,4},{1,5},{2,6},{3,7},{4,0},{5,1},{6,2},{7,3},{8,12},{9,13},{10,... | collective-permute-start | bytes 1179656 | tf_op jit(solution)/shard_map/ppermute | solution.py:346
  163.9 16.2 %collective-permute-start.39 = (bf16[192,1024]{1,0:T(8,128)(2,1)S(1)}, bf16[192,1024]{1,0:T(8,128)(2,1)S(1)}, u32[]{:S(2)}, u32[]{:S(2)}) collective-permute-start(bf16[192,1024]{1,0:T(8,128)(2,1)S(1)} %fusion.113), channel_id=1, source_target_pairs={{0,1},{1,0},{2,3},{3,2},{4,5},{5,4},{6,7},{7,6},{8,9},{9,8},{10,11... | collective-permute-start | bytes 1179656 | tf_op jit(solution)/shard_map/ppermute | solution.py:346
  175.9 14.9 %collective-permute-start.45 = (bf16[256,1024]{1,0:T(8,128)(2,1)S(1)}, bf16[256,1024]{1,0:T(8,128)(2,1)S(1)}, u32[]{:S(2)}, u32[]{:S(2)}) collective-permute-start(bf16[256,1024]{1,0:T(8,128)(2,1)S(1)} %constant_dynamic-update-slice_fusion.4.refs_0_), channel_id=1, source_target_pairs={{0,4},{1,5},{2,6},{3,7},{4,0},{5,1},{6,2},{7,3},{8,12},{9,13},{10,... | collective-permute-start | bytes 1572872 | tf_op jit(solution)/shard_map/ppermute | solution.py:346
  177.5 14.0 %collective-permute-start.44 = (bf16[256,1024]{1,0:T(8,128)(2,1)S(1)}, bf16[256,1024]{1,0:T(8,128)(2,1)S(1)}, u32[]{:S(2)}, u32[]{:S(2)}) collective-permute-start(bf16[256,1024]{1,0:T(8,128)(2,1)S(1)} %constant_dynamic-update-slice_fusion.4.refs_0_), channel_id=1, source_target_pairs={{0,8},{1,9},{2,10},{3,11},{4,12},{5,13},{6,14},{7,15},{8,0},{9,1},... | collective-permute-start | bytes 1572872 | tf_op jit(solution)/shard_map/ppermute | solution.py:346
  193.1 18.5 %collective-permute-start.50 = (bf16[256,1024]{1,0:T(8,128)(2,1)S(1)}, bf16[256,1024]{1,0:T(8,128)(2,1)S(1)}, u32[]{:S(2)}, u32[]{:S(2)}) collective-permute-start(bf16[256,1024]{1,0:T(8,128)(2,1)S(1)} %collective-permute-done.44.refs_1_), channel_id=1, source_target_pairs={{0,4},{1,5},{2,6},{3,7},{4,0},{5,1},{6,2},{7,3},{8,12},{9,13},{10,... | collective-permute-start | bytes 1572872 | tf_op jit(solution)/shard_map/ppermute | solution.py:346
  195.0 16.7 %collective-permute-start.48 = (bf16[192,1024]{1,0:T(8,128)(2,1)S(1)}, bf16[192,1024]{1,0:T(8,128)(2,1)S(1)}, u32[]{:S(2)}, u32[]{:S(2)}) collective-permute-start(bf16[192,1024]{1,0:T(8,128)(2,1)S(1)} %fusion.82), channel_id=1, source_target_pairs={{0,2},{1,3},{2,0},{3,1},{4,6},{5,7},{6,4},{7,5},{8,10},{9,11},{10,... | collective-permute-start | bytes 1179656 | tf_op jit(solution)/shard_map/ppermute | solution.py:346
  196.3 15.4 %collective-permute-start.46 = (bf16[192,1024]{1,0:T(8,128)(2,1)S(1)}, bf16[192,1024]{1,0:T(8,128)(2,1)S(1)}, u32[]{:S(2)}, u32[]{:S(2)}) collective-permute-start(bf16[192,1024]{1,0:T(8,128)(2,1)S(1)} %slice.2349), channel_id=1, source_target_pairs={{0,1},{1,0},{2,3},{3,2},{4,5},{5,4},{6,7},{7,6},{8,9},{9,8},{10,11... | collective-permute-start | bytes 1179656 | tf_op jit(solution)/shard_map/ppermute | solution.py:346
  196.4 15.2 %collective-permute-start.49 = (bf16[128,1024]{1,0:T(8,128)(2,1)S(1)}, bf16[128,1024]{1,0:T(8,128)(2,1)S(1)}, u32[]{:S(2)}, u32[]{:S(2)}) collective-permute-start(bf16[128,1024]{1,0:T(8,128)(2,1)S(1)} %get-tuple-element.321), channel_id=1, source_target_pairs={{0,16},{1,17},{2,18},{3,19},{4,20},{5,21},{6,22},{7,23},{8,24},{9,... | collective-permute-start | bytes 786440 | tf_op jit(solution)/shard_map/ppermute | solution.py:346
  214.7 15.9 %collective-permute-start.51 = (bf16[192,1024]{1,0:T(8,128)(2,1)S(1)}, bf16[192,1024]{1,0:T(8,128)(2,1)}, u32[]{:S(2)}, u32[]{:S(2)}) collective-permute-start(bf16[192,1024]{1,0:T(8,128)(2,1)S(1)} %fusion.114), channel_id=1, source_target_pairs={{0,1},{1,0},{2,3},{3,2},{4,5},{5,4},{6,7},{7,6},{8,9},{9,8},{10,11... | collective-permute-start | bytes 1179656 | tf_op jit(solution)/shard_map/ppermute | solution.py:346
  226.2 14.3 %collective-permute-start.56 = (bf16[256,1024]{1,0:T(8,128)(2,1)S(1)}, bf16[256,1024]{1,0:T(8,128)(2,1)S(1)}, u32[]{:S(2)}, u32[]{:S(2)}) collective-permute-start(bf16[256,1024]{1,0:T(8,128)(2,1)S(1)} %collective-permute-done.53.refs_1_), channel_id=1, source_target_pairs={{0,4},{1,5},{2,6},{3,7},{4,0},{5,1},{6,2},{7,3},{8,12},{9,13},{10,... | collective-permute-start | bytes 1572872 | tf_op jit(solution)/shard_map/ppermute | solution.py:346
  281.3 24.6 %collective-permute-start.61 = (bf16[192,1024]{1,0:T(8,128)(2,1)S(1)}, bf16[192,1024]{1,0:T(8,128)(2,1)S(1)}, u32[]{:S(2)}, u32[]{:S(2)}) collective-permute-start(bf16[192,1024]{1,0:T(8,128)(2,1)S(1)} %slice.2345), channel_id=1, source_target_pairs={{0,1},{1,0},{2,3},{3,2},{4,5},{5,4},{6,7},{7,6},{8,9},{9,8},{10,11... | collective-permute-start | bytes 1179656 | tf_op jit(solution)/shard_map/ppermute | solution.py:346
  290.9 14.1 %collective-permute-start.66 = (bf16[2,128,1024]{2,1,0:T(8,128)(2,1)S(1)}, bf16[2,128,1024]{2,1,0:T(8,128)(2,1)S(1)}, u32[]{:S(2)}, u32[]{:S(2)}) collective-permute-start(bf16[2,128,1024]{2,1,0:T(8,128)(2,1)S(1)} %select_bitcast_fusion.19), channel_id=1, source_target_pairs={{0,4},{1,5},{2,6},{3,7},{4,0},{5,1},{6,2},{7,3},{8,12},{9,13},{10,... | collective-permute-start | bytes 1572872 | tf_op jit(solution)/shard_map/ppermute | solution.py:346
  321.8 17.4 %collective-permute-start.72 = (bf16[128,1024]{1,0:T(8,128)(2,1)}, bf16[128,1024]{1,0:T(8,128)(2,1)}, u32[]{:S(2)}, u32[]{:S(2)}) collective-permute-start(bf16[128,1024]{1,0:T(8,128)(2,1)} %select_bitcast_fusion.37), channel_id=1, source_target_pairs={{0,16},{1,17},{2,18},{3,19},{4,20},{5,21},{6,22},{7,23},{8,24},{9,... | collective-permute-start | bytes 786440 | tf_op jit(solution)/shard_map/ppermute | solution.py:346
  323.6 15.7 %collective-permute-start.73 = (bf16[2,128,1024]{2,1,0:T(8,128)(2,1)}, bf16[2,128,1024]{2,1,0:T(8,128)(2,1)S(1)}, u32[]{:S(2)}, u32[]{:S(2)}) collective-permute-start(bf16[2,128,1024]{2,1,0:T(8,128)(2,1)} %select_bitcast_fusion.17), channel_id=1, source_target_pairs={{0,4},{1,5},{2,6},{3,7},{4,0},{5,1},{6,2},{7,3},{8,12},{9,13},{10,... | collective-permute-start | bytes 1572872 | tf_op jit(solution)/shard_map/ppermute | solution.py:346
  345.9 13.8 %collective-permute-start.77 = (bf16[192,1024]{1,0:T(8,128)(2,1)S(1)}, bf16[192,1024]{1,0:T(8,128)(2,1)S(1)}, u32[]{:S(2)}, u32[]{:S(2)}) collective-permute-start(bf16[192,1024]{1,0:T(8,128)(2,1)S(1)} %slice.2343), channel_id=1, source_target_pairs={{0,1},{1,0},{2,3},{3,2},{4,5},{5,4},{6,7},{7,6},{8,9},{9,8},{10,11... | collective-permute-start | bytes 1179656 | tf_op jit(solution)/shard_map/ppermute | solution.py:346
  361.7 16.9 %collective-permute-start.84 = (bf16[192,1024]{1,0:T(8,128)(2,1)S(1)}, bf16[192,1024]{1,0:T(8,128)(2,1)S(1)}, u32[]{:S(2)}, u32[]{:S(2)}) collective-permute-start(bf16[192,1024]{1,0:T(8,128)(2,1)S(1)} %get-tuple-element.494), channel_id=1, source_target_pairs={{0,2},{1,3},{2,0},{3,1},{4,6},{5,7},{6,4},{7,5},{8,10},{9,11},{10,... | collective-permute-start | bytes 1179656 | tf_op jit(solution)/shard_map/ppermute | solution.py:346
  363.3 15.3 %collective-permute-start.85 = (bf16[128,1024]{1,0:T(8,128)(2,1)S(1)}, bf16[128,1024]{1,0:T(8,128)(2,1)S(1)}, u32[]{:S(2)}, u32[]{:S(2)}) collective-permute-start(bf16[128,1024]{1,0:T(8,128)(2,1)S(1)} %select_bitcast_fusion.36), channel_id=1, source_target_pairs={{0,16},{1,17},{2,18},{3,19},{4,20},{5,21},{6,22},{7,23},{8,24},{9,... | collective-permute-start | bytes 786440 | tf_op jit(solution)/shard_map/ppermute | solution.py:346
  364.0 14.6 %collective-permute-start.86 = (bf16[2,128,1024]{2,1,0:T(8,128)(2,1)S(1)}, bf16[2,128,1024]{2,1,0:T(8,128)(2,1)S(1)}, u32[]{:S(2)}, u32[]{:S(2)}) collective-permute-start(bf16[2,128,1024]{2,1,0:T(8,128)(2,1)S(1)} %pad_maximum_fusion.13), channel_id=1, source_target_pairs={{0,4},{1,5},{2,6},{3,7},{4,0},{5,1},{6,2},{7,3},{8,12},{9,13},{10,... | collective-permute-start | bytes 1572872 | tf_op jit(solution)/shard_map/ppermute | solution.py:346
  367.7 43.8 %collective-permute-start.83 = (bf16[192,1024]{1,0:T(8,128)(2,1)S(1)}, bf16[192,1024]{1,0:T(8,128)(2,1)S(1)}, u32[]{:S(2)}, u32[]{:S(2)}) collective-permute-start(bf16[192,1024]{1,0:T(8,128)(2,1)S(1)} %slice.2341), channel_id=1, source_target_pairs={{0,1},{1,0},{2,3},{3,2},{4,5},{5,4},{6,7},{7,6},{8,9},{9,8},{10,11... | collective-permute-start | bytes 1179656 | tf_op jit(solution)/shard_map/ppermute | solution.py:346
  378.8 14.3 %collective-permute-start.89 = (bf16[2,128,1024]{2,1,0:T(8,128)(2,1)S(1)}, bf16[2,128,1024]{2,1,0:T(8,128)(2,1)S(1)}, u32[]{:S(2)}, u32[]{:S(2)}) collective-permute-start(bf16[2,128,1024]{2,1,0:T(8,128)(2,1)S(1)} %pad_maximum_fusion.14), channel_id=1, source_target_pairs={{0,4},{1,5},{2,6},{3,7},{4,0},{5,1},{6,2},{7,3},{8,12},{9,13},{10,... | collective-permute-start | bytes 1572872 | tf_op jit(solution)/shard_map/ppermute | solution.py:346
  380.0 14.0 %collective-permute-start.88 = (bf16[2,128,1024]{2,1,0:T(8,128)(2,1)S(1)}, bf16[2,128,1024]{2,1,0:T(8,128)(2,1)S(1)}, u32[]{:S(2)}, u32[]{:S(2)}) collective-permute-start(bf16[2,128,1024]{2,1,0:T(8,128)(2,1)S(1)} %add_convert_fusion.5), channel_id=1, source_target_pairs={{0,8},{1,9},{2,10},{3,11},{4,12},{5,13},{6,14},{7,15},{8,0},{9,1},... | collective-permute-start | bytes 1572872 | tf_op jit(solution)/shard_map/ppermute | solution.py:346
  395.5 15.3 %collective-permute-start.92 = (bf16[128,1024]{1,0:T(8,128)(2,1)S(1)}, bf16[128,1024]{1,0:T(8,128)(2,1)S(1)}, u32[]{:S(2)}, u32[]{:S(2)}) collective-permute-start(bf16[128,1024]{1,0:T(8,128)(2,1)S(1)} %select_bitcast_fusion.33), channel_id=1, source_target_pairs={{0,16},{1,17},{2,18},{3,19},{4,20},{5,21},{6,22},{7,23},{8,24},{9,... | collective-permute-start | bytes 786440 | tf_op jit(solution)/shard_map/ppermute | solution.py:346
  397.3 14.0 %collective-permute-start.93 = (bf16[2,128,1024]{2,1,0:T(8,128)(2,1)S(1)}, bf16[2,128,1024]{2,1,0:T(8,128)(2,1)S(1)}, u32[]{:S(2)}, u32[]{:S(2)}) collective-permute-start(bf16[2,128,1024]{2,1,0:T(8,128)(2,1)S(1)} %select_bitcast_fusion.15), channel_id=1, source_target_pairs={{0,4},{1,5},{2,6},{3,7},{4,0},{5,1},{6,2},{7,3},{8,12},{9,13},{10,... | collective-permute-start | bytes 1572872 | tf_op jit(solution)/shard_map/ppermute | solution.py:346
  427.8 16.7 %collective-permute-start.99 = (bf16[128,1024]{1,0:T(8,128)(2,1)}, bf16[128,1024]{1,0:T(8,128)(2,1)}, u32[]{:S(2)}, u32[]{:S(2)}) collective-permute-start(bf16[128,1024]{1,0:T(8,128)(2,1)} %select_bitcast_fusion.32), channel_id=1, source_target_pairs={{0,16},{1,17},{2,18},{3,19},{4,20},{5,21},{6,22},{7,23},{8,24},{9,... | collective-permute-start | bytes 786440 | tf_op jit(solution)/shard_map/ppermute | solution.py:346
  429.0 15.5 %collective-permute-start.100 = (bf16[2,128,1024]{2,1,0:T(8,128)(2,1)S(1)}, bf16[2,128,1024]{2,1,0:T(8,128)(2,1)S(1)}, u32[]{:S(2)}, u32[]{:S(2)}) collective-permute-start(bf16[2,128,1024]{2,1,0:T(8,128)(2,1)S(1)} %select_bitcast_fusion.13), channel_id=1, source_target_pairs={{0,4},{1,5},{2,6},{3,7},{4,0},{5,1},{6,2},{7,3},{8,12},{9,13},{10,... | collective-permute-start | bytes 1572872 | tf_op jit(solution)/shard_map/ppermute | solution.py:346
  455.2 14.7 %collective-permute-start.105 = (bf16[2,128,1024]{2,1,0:T(8,128)(2,1)}, bf16[2,128,1024]{2,1,0:T(8,128)(2,1)}, u32[]{:S(2)}, u32[]{:S(2)}) collective-permute-start(bf16[2,128,1024]{2,1,0:T(8,128)(2,1)} %pad_maximum_fusion.16), channel_id=1, source_target_pairs={{0,4},{1,5},{2,6},{3,7},{4,0},{5,1},{6,2},{7,3},{8,12},{9,13},{10,... | collective-permute-start | bytes 1572872 | tf_op jit(solution)/shard_map/ppermute | solution.py:346
  456.2 15.3 %collective-permute-start.106 = (bf16[2,128,1024]{2,1,0:T(8,128)(2,1)}, bf16[2,128,1024]{2,1,0:T(8,128)(2,1)}, u32[]{:S(2)}, u32[]{:S(2)}) collective-permute-start(bf16[2,128,1024]{2,1,0:T(8,128)(2,1)} %fusion.61), channel_id=1, source_target_pairs={{0,8},{1,9},{2,10},{3,11},{4,12},{5,13},{6,14},{7,15},{8,0},{9,1},... | collective-permute-start | bytes 1572872 | tf_op jit(solution)/shard_map/ppermute | solution.py:346
  458.0 18.8 %collective-permute-start.107 = (bf16[192,1024]{1,0:T(8,128)(2,1)}, bf16[192,1024]{1,0:T(8,128)(2,1)}, u32[]{:S(2)}, u32[]{:S(2)}) collective-permute-start(bf16[192,1024]{1,0:T(8,128)(2,1)} %slice.2338), channel_id=1, source_target_pairs={{0,1},{1,0},{2,3},{3,2},{4,5},{5,4},{6,7},{7,6},{8,9},{9,8},{10,11... | collective-permute-start | bytes 1179656 | tf_op jit(solution)/shard_map/ppermute | solution.py:346
  505.4 14.1 %collective-permute-start.122 = (bf16[128,1024]{1,0:T(8,128)(2,1)S(1)}, bf16[128,1024]{1,0:T(8,128)(2,1)S(1)}, u32[]{:S(2)}, u32[]{:S(2)}) collective-permute-start(bf16[128,1024]{1,0:T(8,128)(2,1)S(1)} %select_bitcast_fusion.28), channel_id=1, source_target_pairs={{0,16},{1,17},{2,18},{3,19},{4,20},{5,21},{6,22},{7,23},{8,24},{9,... | collective-permute-start | bytes 786440 | tf_op jit(solution)/shard_map/ppermute | solution.py:346
  (195 other events, 1308.9 us)
